TPU v7x, 128 devices: a whole 4x4x4 slice. The times are simulated.
128 devices in a mesh: blk: 32 (over x, z_hi, y), rep: 4 (over z_lo, core).
Axes of the slice: x: 4, y: 4, z: 4 (z_hi: 2, z_lo: 2; z = z_hi * 2 + z_lo), core: 2. Of those that a mesh axis runs over, the one named last changes fastest.
Arguments:
- generated: float32 [8192, 1024], P(('blk', 'rep')), may hold values from -6 to 6
- real_bank: float32 [65536, 1024], P(('blk', 'rep')), may hold values from -6 to 6
- subset_rows: int32 [32768], P(('blk', 'rep')), may hold values from 0 to 511
Outputs:
- gradient: float32 [8192, 1024], P(('blk', 'rep'))
All inputs are finite; a program needn't handle non-finite values.
Results may differ from a plain program's by a relative error of at most 0.0003.
Values sent between devices are 32-bit elements; how exact they have to be, the bound alone decides.
No kernel may reach another device: no remote copies, remote signals or barrier semaphores. Data moves between devices by JAX's collectives and lax.ppermute only.
A program may use at most 128 MiB of HBM per device.

v0:
```python
import jax
import jax.numpy as jnp
from jax import lax
from jax.sharding import PartitionSpec as P

BANDS = (0.5, 1.0, 2.0)


def kernel_weight(dist, width):
    total = jnp.zeros_like(dist)
    for factor in BANDS:
        total = total + jnp.exp(-dist / (2.0 * factor * width)) / factor
    return total


def weight_sums(rows, others):
    row_norms = jnp.sum(rows * rows, axis=1)
    other_norms = jnp.sum(others * others, axis=1)
    inner = jnp.dot(
        rows, others.T, precision=lax.Precision.HIGHEST, preferred_element_type=jnp.float32
    )
    dist = jnp.maximum(row_norms[:, None] + other_norms[None, :] - 2.0 * inner, 0.0)
    weights = kernel_weight(dist, float(rows.shape[1]))
    weighted = jnp.dot(
        weights, others, precision=lax.Precision.HIGHEST, preferred_element_type=jnp.float32
    )
    return (jnp.sum(weights, axis=1), weighted)


def on_device(generated, real_bank, subset_rows):
    total_gen = generated.shape[0] * lax.axis_size("blk") * lax.axis_size("rep")
    total_real = subset_rows.shape[0] * lax.axis_size("blk") * lax.axis_size("rep")
    real_local = jnp.take(real_bank, subset_rows, axis=0)
    gen_block = lax.all_gather(generated, "rep", axis=0, tiled=True)

    def add_pairs(piece):
        sums, weighted = weight_sums(gen_block, piece)
        return (sums, weighted)

    self_total, self_weighted = add_pairs(lax.all_gather(generated, "blk", axis=0, tiled=True))
    cross_total, cross_weighted = add_pairs(lax.all_gather(real_local, "blk", axis=0, tiled=True))
    self_part = self_total[:, None] * gen_block - self_weighted
    cross_part = cross_total[:, None] * gen_block - cross_weighted
    gradient = lax.psum_scatter(
        self_part / total_gen - cross_part / total_real, "rep", scatter_dimension=0, tiled=True
    )
    return gradient


def solution(mesh):
    in_specs = (P(("blk", "rep"), None), P(("blk", "rep"), None), P(("blk", "rep")))
    out_specs = P(("blk", "rep"), None)
    return jax.shard_map(
        on_device, mesh=mesh, in_specs=in_specs, out_specs=out_specs, check_vma=False
    )
```

profile of v0, /device:TPU:0, one launch (start us, length us, event | category | flops | bytes accessed | tf_op | source)
XLA Modules:
  0.0 537.0 jit_solution(16454414251477117016)
XLA Ops:
  6.5 0.0 copy-start
  6.5 0.0 copy-start.4
  6.5 0.0 all-gather.4.cloned.1.call-start
  6.5 0.7 all-gather.4.cloned.1.call-update
  7.3 0.0 all-gather.6.cloned.1.call-start
  7.3 0.7 all-gather.6.cloned.1.call-update
  8.0 0.0 all-gather.8.cloned.1.call-start
  8.1 0.7 compare_select_fusion
  8.7 0.0 copy-done
  8.8 1.1 gather_fusion
  9.8 0.0 copy-done.4
  9.9 1.1 broadcast_select_fusion
  11.0 0.0 all-gather.8.cloned.1.call-update
  11.0 0.0 reduce-scatter.2.cloned.1.call-start
  11.0 21.2 %all-gather.4.cloned.1.call-done = f32[256,1024]{1,0:T(8,128)} async-done(((f32[64,1024]{1,0:T(8,128)}), f32[256,1024]{1,0:T(8,128)}) %all-gather.4.cloned.1.call-update) | async-done | bytes 1048592 | tf_op jit(solution)/shard_map/all_gather | solution.py:34
  32.3 0.0 copy-start.2
  32.3 1.5 multiply_reduce_fusion.2
  33.7 107.7 %all-gather.6.cloned.1.call-done = f32[2048,1024]{1,0:T(8,128)} async-done(((f32[64,1024]{1,0:T(8,128)}), f32[2048,1024]{1,0:T(8,128)}) %all-gather.6.cloned.1.call-update) | async-done | bytes 8388624 | tf_op jit(solution)/shard_map/all_gather | solution.py:40
  141.5 0.0 copy-start.1
  141.5 4.1 multiply_reduce_fusion.1
  145.6 0.0 copy-done.2
  145.6 1.6 copy-done.1
  147.2 7.9 %fusion.10 = (f32[256]{0:T(256)S(1)}, f32[256,2048]{1,0:T(8,128)S(1)}) fusion(f32[256,1024]{1,0:T(8,128)S(1)} %copy-done.2, f32[2048,1024]{1,0:T(8,128)S(1)} %copy-done.1, f32[2048]{0:T(1024)S(1)} %multiply_reduce_fusion.1, f32[256]{0:T(256)S(1)} %multiply_reduce_fusion.2), kind=kOutput, calls=%fused_computation.24 | convolution fusion | flops 6449266688 | bytes 11544576 | tf_op jit(solution)/shard_map/dot_general | solution.py:19
  155.2 8.5 %fusion.9 = f32[256,1024]{1,0:T(8,128)} fusion(f32[256,2048]{1,0:T(8,128)S(1)} %get-tuple-element.6, f32[2048,1024]{1,0:T(8,128)S(1)} %copy-done.1, f32[256,1024]{1,0:T(8,128)S(1)} %copy-done.2, f32[256]{0:T(256)S(1)} %get-tuple-element.5), kind=kOutput, calls=%fused_computation.18 | convolution fusion | flops 6443237376 | bytes 12583936 | tf_op jit(solution)/shard_map/dot_general | solution.py:24
  163.7 240.1 %all-gather.8.cloned.1.call-done = f32[8192,1024]{1,0:T(8,128)} async-done(((f32[256,1024]{1,0:T(8,128)}), f32[8192,1024]{1,0:T(8,128)}) %all-gather.8.cloned.1.call-update) | async-done | bytes 33554448 | tf_op jit(solution)/shard_map/all_gather | solution.py:41
  403.8 12.1 %multiply_reduce_fusion = f32[8192]{0:T(1024)S(1)} fusion(f32[8192,1024]{1,0:T(8,128)} %all-gather.8.cloned.1.call-done), kind=kLoop, calls=%fused_computation.1 | loop fusion | flops 16769024 | bytes 33587200 | tf_op jit(solution)/shard_map/reduce_sum | solution.py:18
  415.9 0.0 copy-start.3
  415.9 36.3 %fusion.11 = (f32[256]{0:T(256)S(1)}, f32[256,8192]{0,1:T(8,128)S(1)}) fusion(f32[8192,1024]{1,0:T(8,128)} %all-gather.8.cloned.1.call-done, f32[256,1024]{1,0:T(8,128)S(1)} %copy-done.2, f32[8192]{0:T(1024)S(1)} %multiply_reduce_fusion, f32[256]{0:T(256)S(1)} %multiply_reduce_fusion.2), kind=kOutput, calls=%fused_computation.25 | convolution fusion | flops 25797066752 | bytes 43026432 | tf_op jit(solution)/shard_map/dot_general | solution.py:19
  452.3 0.0 copy-done.3
  452.3 60.2 %fusion.8 = f32[256,1024]{1,0:T(8,128)} fusion(f32[256,1024]{1,0:T(8,128)S(1)} %copy-done.3, f32[256,8192]{0,1:T(8,128)S(1)} %get-tuple-element.8, f32[8192,1024]{1,0:T(8,128)} %all-gather.8.cloned.1.call-done, f32[256,1024]{1,0:T(8,128)S(1)} %copy-done.2, f32[256]{0:T(256)S(1)} %get-tuple-element.7), kind=kOutput, calls=%fused_computation.16 | convolution fusion | flops 25770852352 | bytes 45089792 | tf_op jit(solution)/shard_map/dot_general | solution.py:24
  512.5 0.0 reduce-scatter.2.cloned.1.call-update
  512.6 17.9 %reduce-scatter.2.cloned.1.call-done = f32[64,1024]{1,0:T(8,128)} async-done(((f32[256,1024]{1,0:T(8,128)}), f32[64,1024]{1,0:T(8,128)}) %reduce-scatter.2.cloned.1.call-update) | async-done | bytes 262160 | tf_op jit(solution)/shard_map/reduce_scatter | solution.py:44
  (2 shorter events, 0.0 us)
Async XLA Ops:
  6.5 2.2 copy-start
  6.5 3.3 copy-start.4
  6.5 25.7 %all-gather.4.cloned.1.call-start = ((), (), s32[]{:S(2)}) async-start(), calls=%async_computation.1 | async-start | bytes 1310720 | tf_op jit(solution)/shard_map/all_gather | solution.py:34
  7.3 134.2 %all-gather.6.cloned.1.call-start = ((), (), s32[]{:S(2)}) async-start(), calls=%async_computation.2 | async-start | bytes 8650752 | tf_op jit(solution)/shard_map/all_gather | solution.py:40
  8.0 395.8 %all-gather.8.cloned.1.call-start = ((), (), s32[]{:S(2)}) async-start(), calls=%async_computation.3 | async-start | bytes 34603008 | tf_op jit(solution)/shard_map/all_gather | solution.py:41
  11.0 519.5 %reduce-scatter.2.cloned.1.call-start = ((), (), s32[]{:S(2)}) async-start(), calls=%async_computation.4 | async-start | bytes 1310720 | tf_op jit(solution)/shard_map/reduce_scatter | solution.py:44
  32.3 113.4 %copy-start.2 = (f32[256,1024]{1,0:T(8,128)S(1)}, f32[256,1024]{1,0:T(8,128)}, u32[]{:S(2)}) copy-start(f32[256,1024]{1,0:T(8,128)} %all-gather.4.cloned.1.call-done) | copy-start | bytes 3145732
  141.5 5.8 %copy-start.1 = (f32[2048,1024]{1,0:T(8,128)S(1)}, f32[2048,1024]{1,0:T(8,128)}, u32[]{:S(2)}) copy-start(f32[2048,1024]{1,0:T(8,128)} %all-gather.6.cloned.1.call-done) | copy-start | bytes 25165828
  415.9 36.4 %copy-start.3 = (f32[256,1024]{1,0:T(8,128)S(1)}, f32[256,1024]{1,0:T(8,128)}, u32[]{:S(2)}) copy-start(f32[256,1024]{1,0:T(8,128)} %fusion.9) | copy-start | bytes 3145732
Sparse Core Ops, SparseCore 0:
  9.0 23.1 all-gather.3
  35.4 106.0 all-gather.5
  144.6 259.1 all-gather.7
  512.7 17.7 reduce-scatter.1
where the time goes:
time: 538 us; the launch traced here: 537 us
  waiting for transfers between devices  388 us (72%)
  matrix products  113 us (21%)
  other arithmetic  19.6 us (4%)
  between operations  13.2 us (2%)
    all_gather x1, waiting for transfers between devices, on_device(): lax.all_gather(real_local, 'blk', axis=0, tiled=True)  240 us
    all_gather x1, waiting for transfers between devices, on_device(): lax.all_gather(generated, 'blk', axis=0, tiled=True)  108 us
    dot_general x2, matrix products, weight_sums(): jnp.dot(weights, others, precision=lax.Precision.HIGHEST, preferred_eleme...  68.7 us
    dot_general x2, matrix products, weight_sums(): jnp.dot(rows, others.T, precision=lax.Precision.HIGHEST, preferred_elemen...  44.3 us
    all_gather x1, waiting for transfers between devices, on_device(): gen_block = lax.all_gather(generated, 'rep', axis=0, tiled=True)  21.2 us
    reduce_scatter x1, waiting for transfers between devices, on_device(): lax.psum_scatter(self_part / total_gen - cross_part / total_real, 'rep',...  17.9 us
    reduce_sum x2, other arithmetic, weight_sums(): other_norms = jnp.sum(others * others, axis=1)  16.3 us
  transfers between devices with their start and end apart: 4, of which 4 were waited for; matrix products, arithmetic and copies ran while one was open for 5% of the time, Pallas kernels for 0%

commit v1 on v0

v1 whole, which is shorter than its diff:
```python
import functools
import math

import jax
import jax.numpy as jnp
from jax import lax
from jax.experimental import pallas as pl
from jax.experimental.pallas import tpu as pltpu
from jax.sharding import PartitionSpec as P

AXES = ("blk", "rep")
SIDE = 4


def place(x, y, z, core):
    blk = (x * 2 + z // 2) * SIDE + y
    return blk * 4 + (z % 2) * 2 + core


def partners(axes, step):
    pairs = []
    for x in range(SIDE):
        for y in range(SIDE):
            for z in range(SIDE):
                for core in range(2):
                    to = {"x": x, "y": y, "z": z}
                    at = to[axes[core]]
                    if step == "both" or (step == "near") == (core == 0):
                        at = at ^ 1
                    if step == "both" or (step == "near") == (core == 1):
                        at = SIDE - 1 - at
                    to[axes[core]] = at
                    pairs.append((place(x, y, z, core), place(to["x"], to["y"], to["z"], core)))
    return pairs


STEPS = {(axes, step): partners(axes, step) for axes in ("xy", "yx", "zz") for step in ("near", "far", "both")}
SWAP = [(d, d ^ 1) for d in range(2 * SIDE**3)]


def move(v, axes, step):
    return lax.ppermute(v, AXES, STEPS[axes, step])


def swap(v):
    return lax.ppermute(v, AXES, SWAP)


def dot_t(a, b):
    return lax.dot_general(a, b, (((1,), (1,)), ((), ())), preferred_element_type=jnp.float32)


def lanes(w):
    return sum(w[:, k : k + 128] for k in range(0, w.shape[1], 128))


def pair_kernel(counts, spans, fresh, last, scale, *refs):
    take = iter(refs)
    n_batch = len(counts)
    rows_refs = [[next(take) for _ in range(count)] for count in counts]
    other_refs = [next(take) for _ in spans]
    state_in = [None if new else (next(take), next(take)) for new in fresh]
    state_out = [[next(take) for _ in range(count if last else 2)] for count in counts]
    others_b, others_norms = take
    width = rows_refs[0][0].shape[1]
    kappa = math.log2(math.e) / (4.0 * width)

    def norms_of(others):
        norms = jnp.sum(others * others, axis=1, keepdims=True) * kappa
        return jnp.transpose(jnp.broadcast_to(norms, (norms.shape[0], 128)))[:8]

    gens, reals = [], []
    for ref, span in zip(other_refs, spans):
        if span:
            gens.append(ref[:span])
        reals.append(ref[span:])
    reals = jnp.concatenate(reals, axis=0)
    n_real = reals.shape[0]
    others_norms[:, :n_real] = norms_of(reals)
    others_b[:n_real] = reals.astype(jnp.bfloat16)
    n_gen = sum(spans)
    end = n_real + n_gen
    if n_gen:
        gens = jnp.concatenate(gens, axis=0)
        others_norms[:, n_real:] = norms_of(gens)
        high = gens.astype(jnp.bfloat16)
        others_b[n_real:end] = high
        others_b[end : end + n_gen] = (gens - high.astype(jnp.float32)).astype(jnp.bfloat16)
        others_b[end + n_gen :] = high

    for k in range(n_batch):
        rows = jnp.concatenate([r[...] for r in rows_refs[k]], axis=0)
        row_norms = jnp.sum(rows * rows, axis=1, keepdims=True) * kappa
        rows_b = (rows * (2.0 * kappa)).astype(jnp.bfloat16)

        def weights(at, to, factor):
            power = jnp.minimum(dot_t(rows_b, others_b[at:to]) - row_norms - others_norms[:1, at:to], 0.0)
            e = jnp.exp2(power)
            e2 = e * e
            return (0.5 * factor) * e + e2 * (factor + (2.0 * factor) * e2)

        acc, sums = (0.0, 0.0) if fresh[k] else (state_in[k][0][...], state_in[k][1][...])
        w = weights(0, n_real, -1.0)
        sums = sums + lanes(w)
        w = [w.astype(jnp.bfloat16)]
        if n_gen:
            w_gen = weights(n_real, end, float(scale))
            sums = sums + lanes(w_gen)
            w_hi = w_gen.astype(jnp.bfloat16)
            w += [w_hi, w_hi, (w_gen - w_hi.astype(jnp.float32)).astype(jnp.bfloat16)]
        w = jnp.concatenate(w, axis=1)
        acc = acc + jnp.dot(w, others_b[...], preferred_element_type=jnp.float32)
        if last:
            total = jnp.sum(sums, axis=1, keepdims=True)
            out = (total * rows - acc) * last
            at = 0
            for half in state_out[k]:
                half[...] = out[at : at + half.shape[0]]
                at += half.shape[0]
        else:
            state_out[k][0][...] = acc
            state_out[k][1][...] = sums


def pairs(rows, others, spans, states, last, scale):
    count, width = sum(v.shape[0] for v in rows[0]), rows[0][0].shape[1]
    f32, bf16 = jnp.float32, jnp.bfloat16
    if last:
        shapes = [[jax.ShapeDtypeStruct(v.shape, f32) for v in batch] for batch in rows]
    else:
        shapes = [[jax.ShapeDtypeStruct((count, width), f32), jax.ShapeDtypeStruct((count, 128), f32)] for _ in rows]
    operands = [v for batch in rows for v in batch] + list(others)
    aliases = {}
    for k, state in enumerate(states):
        if state is not None:
            if not last:
                aliases.update({len(operands): 2 * k, len(operands) + 1: 2 * k + 1})
            operands += state
    n_gen = sum(spans)
    n_real = sum(v.shape[0] for v in others) - n_gen
    scratch = [pltpu.VMEM((n_real + 3 * n_gen, width), bf16), pltpu.VMEM((8, n_real + n_gen), f32)]
    n_pairs = count * len(rows) * (n_real + 2 * n_gen)
    vmem = pl.BlockSpec(memory_space=pltpu.VMEM)
    outs = pl.pallas_call(
        functools.partial(pair_kernel, [len(batch) for batch in rows], spans, [s is None for s in states], last, scale),
        out_shape=[v for batch in shapes for v in batch],
        in_specs=[vmem] * len(operands),
        out_specs=[vmem] * sum(len(batch) for batch in shapes),
        scratch_shapes=scratch,
        input_output_aliases=aliases,
        cost_estimate=pl.CostEstimate(
            flops=4 * n_pairs * width, bytes_accessed=4 * width * (n_real + n_gen + 3 * count), transcendentals=n_pairs
        ),
        compiler_params=pltpu.CompilerParams(vmem_limit_bytes=24 * 2**20),
    )(*operands)
    outs = iter(outs)
    return [tuple(next(outs) for _ in batch) for batch in shapes]


def resident(v):
    def copy(v_ref, out_ref):
        out_ref[...] = v_ref[...]

    vmem = pl.BlockSpec(memory_space=pltpu.VMEM)
    return pl.pallas_call(copy, out_shape=jax.ShapeDtypeStruct(v.shape, v.dtype), in_specs=[vmem], out_specs=vmem)(v)


def after(v, *others):
    return lax.optimization_barrier((v, *others))[0]


def resident(v):
    def copy(v_ref, out_ref):
        out_ref[...] = v_ref[...]

    vmem = pl.BlockSpec(memory_space=pltpu.VMEM)
    return pl.pallas_call(copy, out_shape=jax.ShapeDtypeStruct(v.shape, v.dtype), in_specs=[vmem], out_specs=vmem)(v)


def after(v, *others):
    return lax.optimization_barrier((v, *others))[0]


def on_device(generated, real_bank, subset_rows):
    devices = lax.axis_size("blk") * lax.axis_size("rep")
    total_gen = generated.shape[0] * devices
    total_real = subset_rows.shape[0] * devices
    n = generated.shape[0]
    scale = total_real // total_gen
    spans = (n, n)

    generated = resident(generated)
    real = real_bank.at[subset_rows].get(mode="promise_in_bounds", wrap_negative_indices=False)
    own = jnp.concatenate([generated, real], axis=0)
    x_near, x_far = move(own, "zz", "near"), move(own, "zz", "far")

    line = [generated] + [move(generated, "xy", step) for step in ("near", "far", "both")]
    line = jnp.concatenate(line, axis=0)
    half = 2 * n
    own_swapped = swap(after(own, line))
    line_near, line_far = move(line, "yx", "near"), move(line, "yx", "far")

    x_near, x_far, line_near, line_far, own_swapped = lax.optimization_barrier(
        (x_near, x_far, line_near, line_far, own_swapped)
    )
    x_both = move(x_near, "zz", "far")
    x_level = jnp.concatenate([x_near, x_far], axis=0)
    x_level = swap(x_level)
    both = [move(line_near[:half], "yx", "far"), move(line_far[half:], "yx", "near")]
    rows = [[line], [line_near], [line_far], both]
    s = [None] * SIDE
    s[:3] = pairs(rows[:3], (own, own_swapped), spans, s[:3], None, scale)
    x_level, _ = lax.optimization_barrier((x_level, s[:3]))
    count = own.shape[0]
    x_level = (x_near, x_far, x_level[:count], x_level[count:])
    s[:3] = pairs(rows[:3], x_level, spans * 2, s[:3], None, scale)
    x_both, both, _ = lax.optimization_barrier((x_both, both, s[:3]))
    rows[3] = both
    both_two = (x_both, swap(x_both))
    s[3:] = pairs(rows[3:], (own, own_swapped, *x_level), spans * 3, s[3:], None, scale)
    both_two, s = lax.optimization_barrier((both_two, s))
    part = [None] * SIDE
    part[3:] = pairs(rows[3:], both_two, spans, s[3:], 1.0 / total_real, scale)
    s, part[3] = lax.optimization_barrier((s, part[3]))
    part[1:3] = pairs(rows[1:3], both_two, spans, s[1:3], 1.0 / total_real, scale)
    part[:1] = pairs(rows[:1], both_two, spans, s[:1], 1.0 / total_real, scale)

    (total,), (part_near,), (part_far,), both = part
    add_near, add_far = move(both[0], "yx", "far"), move(both[1], "yx", "near")
    near_rest, far_rest = move(part_near[half:], "yx", "near"), move(part_far[:half], "yx", "far")
    add_near, add_far, near_rest, far_rest = lax.optimization_barrier((add_near, add_far, near_rest, far_rest))
    to_near = move(part_near[:half] + add_near, "yx", "near")
    to_far = move(part_far[half:] + add_far, "yx", "far")
    total = jnp.concatenate([total[:half] + to_near + far_rest, total[half:] + near_rest + to_far], axis=0)
    out = total[:n]
    for k, step in enumerate(("near", "far", "both")):
        out = out + move(total[(k + 1) * n : (k + 2) * n], "xy", step)
    return out


def solution(mesh):
    in_specs = (P(AXES, None), P(AXES, None), P(AXES))
    return jax.shard_map(on_device, mesh=mesh, in_specs=in_specs, out_specs=P(AXES, None), check_vma=False)
```

time: 538 us -> 110 us (0.20)
  waiting for transfers between devices: 388 us -> 52.3 us
  matrix products: 113 us -> 0 us
  starting transfers between devices: 0.12 us -> 30.8 us
  Pallas kernels: 0 us -> 20 us
  other arithmetic: 19.6 us -> 3.45 us
  between operations: 13.2 us -> 0.22 us
    all_gather x3 -> x0, waiting for transfers between devices: 369 us -> none  [the longest x1 240 us: on_device(): lax.all_gather(real_local, 'blk', axis=0, tiled=True)]
    dot_general x4 -> x0, matrix products: 113 us -> none  [the longest x2 68.7 us: weight_sums(): jnp.dot(weights, others, precision=lax.Precision.HIGHEST, preferred_eleme...]
    ppermute x0 -> x22, waiting for transfers between devices: none -> 52.3 us  [the longest x19 52.3 us: move(): return lax.ppermute(v, AXES, STEPS[axes, step])]
    ppermute x0 -> x22, starting transfers between devices: none -> 30.8 us  [the longest x19 30.6 us: move(): return lax.ppermute(v, AXES, STEPS[axes, step])]
    pallas_call x0 -> x7, Pallas kernels: none -> 20 us  [the longest x6 18.1 us: pairs(): pl.pallas_call(functools.partial(pair_kernel, [len(batch) for batch in ro...]
    reduce_scatter x1 -> x0, waiting for transfers between devices: 17.9 us -> none  [on_device(): lax.psum_scatter(self_part / total_gen - cross_part / total_real, 'rep',...]
    reduce_sum x3 -> x0, other arithmetic: 17.8 us -> none  [the longest x2 16.3 us: weight_sums(): other_norms = jnp.sum(others * others, axis=1)]
  transfers between devices with their start and end apart: 4 -> 22, of which waited for: 4 -> 14; matrix products, arithmetic and copies ran while one was open for 5% -> 3% of each run, Pallas kernels for 0% -> 13%
where the time goes in v1:
time: 110 us; the launch traced here: 108 us
  waiting for transfers between devices  52.3 us (48%)
  starting transfers between devices  30.8 us (28%)
  Pallas kernels  20 us (18%)
  other arithmetic  3.45 us (3%)
  local copies, waits for them, and re-layouts  1.62 us (1%)
    ppermute x19, waiting for transfers between devices, move(): return lax.ppermute(v, AXES, STEPS[axes, step])  52.3 us
    ppermute x19, starting transfers between devices, move(): return lax.ppermute(v, AXES, STEPS[axes, step])  30.6 us
    pallas_call x6, Pallas kernels, pairs(): pl.pallas_call(functools.partial(pair_kernel, [len(batch) for batch in ro...  18.1 us
  transfers between devices with their start and end apart: 22, of which 14 were waited for; matrix products, arithmetic and copies ran while one was open for 3% of the time, Pallas kernels for 13%

profile of v1, /device:TPU:0, one launch (start us, length us, event | category | flops | bytes accessed | tf_op | source)
XLA Modules:
  0.0 108.3 jit_solution(4222101321560188420)
XLA Ops:
  0.0 0.0 copy-start
  0.0 1.8 %shard_map.37 = f32[64,1024]{1,0:T(8,128)} custom-call(f32[64,1024]{1,0:T(8,128)} %v_ref.1), custom_call_target="tpu_custom_call" | custom-call | tf_op jit(solution)/shard_map/pallas_call | solution.py:177
  1.8 1.6 %collective-permute-start = (f32[64,1024]{1,0:T(8,128)}, f32[64,1024]{1,0:T(8,128)}, u32[]{:S(2)}, u32[]{:S(2)}) collective-permute-start(f32[64,1024]{1,0:T(8,128)} %shard_map.37), channel_id=1, source_target_pairs={{0,32},{1,13},{2,34},{3,15},{16,48},{17,29},{18,50},{19,31},{4,36}... | collective-permute-start | bytes 786440 | tf_op jit(solution)/shard_map/ppermute | solution.py:42
  3.4 2.1 %collective-permute-start.1 = (f32[64,1024]{1,0:T(8,128)}, f32[64,1024]{1,0:T(8,128)}, u32[]{:S(2)}, u32[]{:S(2)}) collective-permute-start(f32[64,1024]{1,0:T(8,128)} %shard_map.37), channel_id=1, source_target_pairs={{0,96},{1,5},{2,98},{3,7},{16,112},{17,21},{18,114},{19,23},{4,100... | collective-permute-start | bytes 786440 | tf_op jit(solution)/shard_map/ppermute | solution.py:42
  5.5 0.6 collective-permute-start.2
  6.1 0.7 pad_clamp_fusion
  6.8 0.0 copy-done
  6.8 1.1 gather_fusion
  7.9 0.0 copy-done.1
  7.9 0.1 pad_maximum_fusion.1.refs_3_.refs_2_
  8.0 2.0 %collective-permute-start.3 = (f32[320,1024]{1,0:T(8,128)S(1)}, f32[320,1024]{1,0:T(8,128)S(1)}, u32[]{:S(2)}, u32[]{:S(2)}) collective-permute-start(f32[320,1024]{1,0:T(8,128)S(1)} %pad_maximum_fusion.1.refs_3_.refs_2_), channel_id=1, source_target_pairs={{0,2},{1,19},{2,0},{3,17},{16,18},{17,3},{18,16},{19,1},{4,6},{5,2... | collective-permute-start | bytes 3932168 | tf_op jit(solution)/shard_map/ppermute | solution.py:42
  10.0 2.5 %collective-permute-start.4 = (f32[320,1024]{1,0:T(8,128)S(1)}, f32[320,1024]{1,0:T(8,128)S(1)}, u32[]{:S(2)}, u32[]{:S(2)}) collective-permute-start(f32[320,1024]{1,0:T(8,128)S(1)} %pad_maximum_fusion.1.refs_3_.refs_2_), channel_id=1, source_target_pairs={{0,18},{1,3},{2,16},{3,1},{16,2},{17,19},{18,0},{19,17},{4,22},{5,... | collective-permute-start | bytes 3932168 | tf_op jit(solution)/shard_map/ppermute | solution.py:42
  12.5 0.0 collective-permute-done
  12.5 1.6 %collective-permute-done.1 = f32[64,1024]{1,0:T(8,128)} collective-permute-done((f32[64,1024]{1,0:T(8,128)}, f32[64,1024]{1,0:T(8,128)}, u32[]{:S(2)}, u32[]{:S(2)}) %collective-permute-start.1) | collective-permute-done | bytes 262176 | tf_op jit(solution)/shard_map/ppermute | solution.py:42
  14.1 0.0 collective-permute-done.2
  14.1 1.2 %pad_maximum_fusion.2.refs_0_ = f32[256,1024]{1,0:T(8,128)S(1)} fusion(f32[64,1024]{1,0:T(8,128)} %collective-permute-done.2, f32[64,1024]{1,0:T(8,128)} %collective-permute-done.1, f32[64,1024]{1,0:T(8,128)} %collective-permute-done, f32[64,1024]{1,0:T(8,128)S(1)} %copy-done.1), kind=kLoop, calls=%fused_computation.3 | loop fusion | flops 786432 | bytes 2097152 | tf_op jit(solution)/shard_map/concatenate | solution.py:198
  15.3 0.1 collective-permute-start.7
  15.4 1.7 %collective-permute-start.5 = (f32[256,1024]{1,0:T(8,128)S(1)}, f32[256,1024]{1,0:T(8,128)S(1)}, u32[]{:S(2)}, u32[]{:S(2)}) collective-permute-start(f32[256,1024]{1,0:T(8,128)S(1)} %pad_maximum_fusion.2.refs_0_), channel_id=1, source_target_pairs={{0,4},{1,97},{2,6},{3,99},{16,20},{17,113},{18,22},{19,115},{4,0},... | collective-permute-start | bytes 3145736 | tf_op jit(solution)/shard_map/ppermute | solution.py:42
  17.1 2.2 %collective-permute-start.6 = (f32[256,1024]{1,0:T(8,128)S(1)}, f32[256,1024]{1,0:T(8,128)S(1)}, u32[]{:S(2)}, u32[]{:S(2)}) collective-permute-start(f32[256,1024]{1,0:T(8,128)S(1)} %pad_maximum_fusion.2.refs_0_), channel_id=1, source_target_pairs={{0,12},{1,33},{2,14},{3,35},{16,28},{17,49},{18,30},{19,51},{4,8},... | collective-permute-start | bytes 3145736 | tf_op jit(solution)/shard_map/ppermute | solution.py:42
  19.3 11.0 %collective-permute-done.5.refs_1_.refs_0_ = f32[256,1024]{1,0:T(8,128)S(1)} collective-permute-done((f32[256,1024]{1,0:T(8,128)S(1)}, f32[256,1024]{1,0:T(8,128)S(1)}, u32[]{:S(2)}, u32[]{:S(2)}) %collective-permute-start.5) | collective-permute-done | bytes 1048608 | tf_op jit(solution)/shard_map/ppermute | solution.py:42
  30.3 2.8 %collective-permute-done.6.refs_2_.refs_1_ = f32[256,1024]{1,0:T(8,128)S(1)} collective-permute-done((f32[256,1024]{1,0:T(8,128)S(1)}, f32[256,1024]{1,0:T(8,128)S(1)}, u32[]{:S(2)}, u32[]{:S(2)}) %collective-permute-start.6) | collective-permute-done | bytes 1048608 | tf_op jit(solution)/shard_map/ppermute | solution.py:42
  33.1 5.4 %collective-permute-done.3.refs_3_.refs_4_ = f32[320,1024]{1,0:T(8,128)S(1)} collective-permute-done((f32[320,1024]{1,0:T(8,128)S(1)}, f32[320,1024]{1,0:T(8,128)S(1)}, u32[]{:S(2)}, u32[]{:S(2)}) %collective-permute-start.3) | collective-permute-done | bytes 1310752 | tf_op jit(solution)/shard_map/ppermute | solution.py:42
  38.5 2.1 %collective-permute-done.4.refs_4_.refs_5_ = f32[320,1024]{1,0:T(8,128)S(1)} collective-permute-done((f32[320,1024]{1,0:T(8,128)S(1)}, f32[320,1024]{1,0:T(8,128)S(1)}, u32[]{:S(2)}, u32[]{:S(2)}) %collective-permute-start.4) | collective-permute-done | bytes 1310752 | tf_op jit(solution)/shard_map/ppermute | solution.py:42
  40.6 0.0 collective-permute-done.7.refs_4_.refs_3_
  40.6 0.3 pad_maximum_fusion
  40.9 0.1 collective-permute-start.11
  41.0 3.0 %collective-permute-start.8 = (f32[320,1024]{1,0:T(8,128)S(1)}, f32[320,1024]{1,0:T(8,128)S(1)}, u32[]{:S(2)}, u32[]{:S(2)}) collective-permute-start(f32[320,1024]{1,0:T(8,128)S(1)} %collective-permute-done.3.refs_3_.refs_4_), channel_id=1, source_target_pairs={{0,18},{1,3},{2,16},{3,1},{16,2},{17,19},{18,0},{19,17},{4,22},{5,... | collective-permute-start | bytes 3932168 | tf_op jit(solution)/shard_map/ppermute | solution.py:42
  44.1 0.6 collective-permute-start.10
  44.8 2.7 %collective-permute-start.9 = (f32[128,1024]{1,0:T(8,128)S(1)}, f32[128,1024]{1,0:T(8,128)S(1)}, u32[]{:S(2)}, u32[]{:S(2)}) collective-permute-start(f32[128,1024]{1,0:T(8,128)S(1)} %slice.42), channel_id=1, source_target_pairs={{0,12},{1,33},{2,14},{3,35},{16,28},{17,49},{18,30},{19,51},{4,8},... | collective-permute-start | bytes 1572872 | tf_op jit(solution)/shard_map/ppermute | solution.py:42
  47.5 3.5 %shard_map.38 = (f32[256,1024]{1,0:T(8,128)S(1)}, f32[256,128]{1,0:T(8,128)S(1)}, f32[256,1024]{1,0:T(8,128)S(1)}, f32[256,128]{1,0:T(8,128)S(1)}, f32[256,1024]{1,0:T(8,128)S(1)}, /*index=5*/f32[256,128]{1,0:T(8,128)S(1)}) custom-call(f32[256,1024]{1,0:T(8,128)S(1)} %pad_maximum_fusion.2.refs_0_, f32[256,1024]{1,0:T(8,128)S(1)} %collective-permute-done.5.refs_1_.refs_0_, ...), custom_call_target="tpu_custom_call" | custom-call | flops 2415919104 | bytes 5767168 | tf_op jit(solution)/shard_map/pallas_call | solution.py:144
  51.0 0.0 collective-permute-done.11
  51.0 0.3 fusion.4
  51.3 5.9 %shard_map.39 = (f32[256,1024]{1,0:T(8,128)S(1)}, f32[256,128]{1,0:T(8,128)S(1)}, f32[256,1024]{1,0:T(8,128)S(1)}, f32[256,128]{1,0:T(8,128)S(1)}, f32[256,1024]{1,0:T(8,128)S(1)}, /*index=5*/f32[256,128]{1,0:T(8,128)S(1)}) custom-call(f32[256,1024]{1,0:T(8,128)S(1)} %pad_maximum_fusion.2.re, ...), custom_call_target="tpu_custom_call", output_to_operand_aliasing={{0}: (7, {}), {1}: (8, {}), {2}: (9, {}), {3}: (10, {}), {4... | custom-call | flops 4831838208 | bytes 8388608 | tf_op jit(solution)/shard_map/pallas_call | solution.py:144
  57.3 0.0 collective-permute-done.10.refs_1_
  57.3 0.0 collective-permute-done.9.refs_0_
  57.3 2.6 %collective-permute-done.8.refs_2_.refs_1_ = f32[320,1024]{1,0:T(8,128)S(1)} collective-permute-done((f32[320,1024]{1,0:T(8,128)S(1)}, f32[320,1024]{1,0:T(8,128)S(1)}, u32[]{:S(2)}, u32[]{:S(2)}) %collective-permute-start.8) | collective-permute-done | bytes 1310752 | tf_op jit(solution)/shard_map/ppermute | solution.py:42
  59.9 0.0 collective-permute-start.12
  59.9 3.3 %shard_map.40 = (f32[256,1024]{1,0:T(8,128)S(1)}, f32[256,128]{1,0:T(8,128)S(1)}) custom-call(f32[128,1024]{1,0:T(8,128)S(1)} %collective-permute-done.9.refs_0_, f32[128,1024]{1,0:T(8,128)S(1)} %collective-permute-done.10.refs_1_, f32[320,1024]{1,0:T(8,128)S(1)} %pad_maximum_fusion.1.refs_3_.refs_2_, ...), custom_call_target="tpu_custom_call" | custom-call | flops 2415919104 | bytes 11010048 | tf_op jit(solution)/shard_map/pallas_call | solution.py:144
  63.2 0.0 collective-permute-done.12.refs_3_.refs_2_
  63.2 1.4 %shard_map.41 = (f32[128,1024]{1,0:T(8,128)S(1)}, f32[128,1024]{1,0:T(8,128)S(1)}) custom-call(f32[128,1024]{1,0:T(8,128)S(1)} %collective-permute-done.9.refs_0_, f32[128,1024]{1,0:T(8,128)S(1)} %collective-permute-done.10.refs_1_, f32[320,1024]{1,0:T(8,128)S(1)} %collective-permute-done.8.refs_2_.refs_1_, ...), custom_call_target="tpu_custom_call" | custom-call | flops 805306368 | bytes 5767168 | tf_op jit(solution)/shard_map/pallas_call | solution.py:144
  64.7 2.5 %shard_map.43 = (f32[256,1024]{1,0:T(8,128)S(1)}, f32[256,1024]{1,0:T(8,128)S(1)}) custom-call(f32[256,1024]{1,0:T(8,128)S(1)} %collective-permute-done.5.refs_1_.refs_0_, f32[256,1024]{1,0:T(8,128)S(1)} %collective-permute-done.6.refs_2_.refs_1_, f32[320,1024]{1,0:T(8,128)S(1)} %collective-permute-done.8.refs_2_.refs_1_, ...), custom_call_target="tpu_custom_call" | custom-call | flops 1610612736 | bytes 5767168 | tf_op jit(solution)/shard_map/pallas_call | solution.py:144
  67.2 0.7 collective-permute-start.15
  67.9 2.5 %collective-permute-start.16 = (f32[128,1024]{1,0:T(8,128)S(1)}, f32[128,1024]{1,0:T(8,128)S(1)}, u32[]{:S(2)}, u32[]{:S(2)}) collective-permute-start(f32[128,1024]{1,0:T(8,128)S(1)} %slice.49), channel_id=1, source_target_pairs={{0,12},{1,33},{2,14},{3,35},{16,28},{17,49},{18,30},{19,51},{4,8},... | collective-permute-start | bytes 1572872 | tf_op jit(solution)/shard_map/ppermute | solution.py:42
  70.4 0.9 collective-permute-start.13
  71.2 0.6 collective-permute-start.14
  71.9 4.6 %collective-permute-done.15 = f32[128,1024]{1,0:T(8,128)S(1)} collective-permute-done((f32[128,1024]{1,0:T(8,128)S(1)}, f32[128,1024]{1,0:T(8,128)S(1)}, u32[]{:S(2)}, u32[]{:S(2)}) %collective-permute-start.15) | collective-permute-done | bytes 524320 | tf_op jit(solution)/shard_map/ppermute | solution.py:42
  76.5 1.9 %collective-permute-done.16 = f32[128,1024]{1,0:T(8,128)S(1)} collective-permute-done((f32[128,1024]{1,0:T(8,128)S(1)}, f32[128,1024]{1,0:T(8,128)S(1)}, u32[]{:S(2)}, u32[]{:S(2)}) %collective-permute-start.16) | collective-permute-done | bytes 524320 | tf_op jit(solution)/shard_map/ppermute | solution.py:42
  78.4 5.6 %collective-permute-done.13 = f32[128,1024]{1,0:T(8,128)S(1)} collective-permute-done((f32[128,1024]{1,0:T(8,128)S(1)}, f32[128,1024]{1,0:T(8,128)S(1)}, u32[]{:S(2)}, u32[]{:S(2)}) %collective-permute-start.13) | collective-permute-done | bytes 524320 | tf_op jit(solution)/shard_map/ppermute | solution.py:42
  84.0 0.0 collective-permute-done.14
  84.0 0.1 slice_add_fusion.2
  84.1 2.5 %collective-permute-start.19 = (f32[128,1024]{1,0:T(8,128)S(1)}, f32[128,1024]{1,0:T(8,128)S(1)}, u32[]{:S(2)}, u32[]{:S(2)}) collective-permute-start(f32[128,1024]{1,0:T(8,128)S(1)} %slice_add_fusion.2), channel_id=1, source_target_pairs={{0,12},{1,33},{2,14},{3,35},{16,28},{17,49},{18,30},{19,51},{4,8},... | collective-permute-start | bytes 1572872 | tf_op jit(solution)/shard_map/ppermute | solution.py:42
  86.5 0.1 slice_add_fusion.3
  86.6 0.3 collective-permute-start.17
  86.9 1.4 %shard_map.42 = f32[256,1024]{1,0:T(8,128)S(1)} custom-call(f32[256,1024]{1,0:T(8,128)S(1)} %pad_maximum_fusion.2.refs_0_, f32[320,1024]{1,0:T(8,128)S(1)} %collective-permute-done.8.refs_2_.refs_1_, f32[320,1024]{1,0:T(8,128)S(1)} %collective-permute-done.12.refs_3_.refs_2_, f32[256,1024]{1,0:T(8,128)S(1)} %get-tuple-element.91.refs_3_, ...), custom_call_target="tpu_custom_call" | custom-call | flops 805306368 | bytes 5767168 | tf_op jit(solution)/shard_map/pallas_call | solution.py:144
  88.3 6.2 %collective-permute-done.19 = f32[128,1024]{1,0:T(8,128)S(1)} collective-permute-done((f32[128,1024]{1,0:T(8,128)S(1)}, f32[128,1024]{1,0:T(8,128)S(1)}, u32[]{:S(2)}, u32[]{:S(2)}) %collective-permute-start.19) | collective-permute-done | bytes 524320 | tf_op jit(solution)/shard_map/ppermute | solution.py:42
  94.6 1.3 %collective-permute-done.17 = f32[128,1024]{1,0:T(8,128)S(1)} collective-permute-done((f32[128,1024]{1,0:T(8,128)S(1)}, f32[128,1024]{1,0:T(8,128)S(1)}, u32[]{:S(2)}, u32[]{:S(2)}) %collective-permute-start.17) | collective-permute-done | bytes 524320 | tf_op jit(solution)/shard_map/ppermute | solution.py:42
  95.9 0.3 fusion.1
  96.2 2.9 %collective-permute-start.20 = (f32[64,1024]{1,0:T(8,128)S(1)}, f32[64,1024]{1,0:T(8,128)S(1)}, u32[]{:S(2)}, u32[]{:S(2)}) collective-permute-start(f32[64,1024]{1,0:T(8,128)S(1)} %get-tuple-element.109), channel_id=1, source_target_pairs={{0,96},{1,5},{2,98},{3,7},{16,112},{17,21},{18,114},{19,23},{4,100... | collective-permute-start | bytes 786440 | tf_op jit(solution)/shard_map/ppermute | solution.py:42
  99.1 0.8 collective-permute-start.21
  99.9 0.6 collective-permute-start.18
  100.5 5.3 %collective-permute-done.20 = f32[64,1024]{1,0:T(8,128)S(1)} collective-permute-done((f32[64,1024]{1,0:T(8,128)S(1)}, f32[64,1024]{1,0:T(8,128)S(1)}, u32[]{:S(2)}, u32[]{:S(2)}) %collective-permute-start.20) | collective-permute-done | bytes 262176 | tf_op jit(solution)/shard_map/ppermute | solution.py:42
  105.8 1.2 %collective-permute-done.21 = f32[64,1024]{1,0:T(8,128)S(1)} collective-permute-done((f32[64,1024]{1,0:T(8,128)S(1)}, f32[64,1024]{1,0:T(8,128)S(1)}, u32[]{:S(2)}, u32[]{:S(2)}) %collective-permute-start.21) | collective-permute-done | bytes 262176 | tf_op jit(solution)/shard_map/ppermute | solution.py:42
  106.9 0.6 collective-permute-done.18
  107.6 0.8 fusion.3
  (7 shorter events, 0.2 us)
Async XLA Ops:
  0.0 6.8 %copy-start = (f32[512,1024]{1,0:T(8,128)S(1)}, f32[512,1024]{1,0:T(8,128)}, u32[]{:S(2)}) copy-start(f32[512,1024]{1,0:T(8,128)} %param.4) | copy-start | bytes 6291460
  1.8 10.7 %collective-permute-start = (f32[64,1024]{1,0:T(8,128)}, f32[64,1024]{1,0:T(8,128)}, u32[]{:S(2)}, u32[]{:S(2)}) collective-permute-start(f32[64,1024]{1,0:T(8,128)} %shard_map.37), channel_id=1, source_target_pairs={{0,32},{1,13},{2,34},{3,15},{16,48},{17,29},{18,50},{19,31},{4,36}... | collective-permute-start | bytes 786440 | tf_op jit(solution)/shard_map/ppermute | solution.py:42
  3.4 10.7 %collective-permute-start.1 = (f32[64,1024]{1,0:T(8,128)}, f32[64,1024]{1,0:T(8,128)}, u32[]{:S(2)}, u32[]{:S(2)}) collective-permute-start(f32[64,1024]{1,0:T(8,128)} %shard_map.37), channel_id=1, source_target_pairs={{0,96},{1,5},{2,98},{3,7},{16,112},{17,21},{18,114},{19,23},{4,100... | collective-permute-start | bytes 786440 | tf_op jit(solution)/shard_map/ppermute | solution.py:42
  5.5 8.6 %collective-permute-start.2 = (f32[64,1024]{1,0:T(8,128)}, f32[64,1024]{1,0:T(8,128)}, u32[]{:S(2)}, u32[]{:S(2)}) collective-permute-start(f32[64,1024]{1,0:T(8,128)} %shard_map.37), channel_id=1, source_target_pairs={{0,64},{1,9},{2,66},{3,11},{16,80},{17,25},{18,82},{19,27},{4,68},... | collective-permute-start | bytes 786440 | tf_op jit(solution)/shard_map/ppermute | solution.py:42
  6.8 1.1 copy-start.1
  8.0 30.5 %collective-permute-start.3 = (f32[320,1024]{1,0:T(8,128)S(1)}, f32[320,1024]{1,0:T(8,128)S(1)}, u32[]{:S(2)}, u32[]{:S(2)}) collective-permute-start(f32[320,1024]{1,0:T(8,128)S(1)} %pad_maximum_fusion.1.refs_3_.refs_2_), channel_id=1, source_target_pairs={{0,2},{1,19},{2,0},{3,17},{16,18},{17,3},{18,16},{19,1},{4,6},{5,2... | collective-permute-start | bytes 3932168 | tf_op jit(solution)/shard_map/ppermute | solution.py:42
  10.0 30.6 %collective-permute-start.4 = (f32[320,1024]{1,0:T(8,128)S(1)}, f32[320,1024]{1,0:T(8,128)S(1)}, u32[]{:S(2)}, u32[]{:S(2)}) collective-permute-start(f32[320,1024]{1,0:T(8,128)S(1)} %pad_maximum_fusion.1.refs_3_.refs_2_), channel_id=1, source_target_pairs={{0,18},{1,3},{2,16},{3,1},{16,2},{17,19},{18,0},{19,17},{4,22},{5,... | collective-permute-start | bytes 3932168 | tf_op jit(solution)/shard_map/ppermute | solution.py:42
  15.3 25.3 %collective-permute-start.7 = (f32[320,1024]{1,0:T(8,128)S(1)}, f32[320,1024]{1,0:T(8,128)S(1)}, u32[]{:S(2)}, u32[]{:S(2)}) collective-permute-start(f32[320,1024]{1,0:T(8,128)S(1)} %pad_maximum_fusion.1.refs_3_.refs_2_), channel_id=1, source_target_pairs={{0,1},{1,0},{2,3},{3,2},{4,5},{5,4},{6,7},{7,6},{8,9},{9,8},{10,11... | collective-permute-start | bytes 3932168 | tf_op jit(solution)/shard_map/ppermute | solution.py:46
  15.4 14.9 %collective-permute-start.5 = (f32[256,1024]{1,0:T(8,128)S(1)}, f32[256,1024]{1,0:T(8,128)S(1)}, u32[]{:S(2)}, u32[]{:S(2)}) collective-permute-start(f32[256,1024]{1,0:T(8,128)S(1)} %pad_maximum_fusion.2.refs_0_), channel_id=1, source_target_pairs={{0,4},{1,97},{2,6},{3,99},{16,20},{17,113},{18,22},{19,115},{4,0},... | collective-permute-start | bytes 3145736 | tf_op jit(solution)/shard_map/ppermute | solution.py:42
  17.1 16.0 %collective-permute-start.6 = (f32[256,1024]{1,0:T(8,128)S(1)}, f32[256,1024]{1,0:T(8,128)S(1)}, u32[]{:S(2)}, u32[]{:S(2)}) collective-permute-start(f32[256,1024]{1,0:T(8,128)S(1)} %pad_maximum_fusion.2.refs_0_), channel_id=1, source_target_pairs={{0,12},{1,33},{2,14},{3,35},{16,28},{17,49},{18,30},{19,51},{4,8},... | collective-permute-start | bytes 3145736 | tf_op jit(solution)/shard_map/ppermute | solution.py:42
  40.9 10.1 %collective-permute-start.11 = (f32[640,1024]{1,0:T(8,128)S(1)}, f32[640,1024]{1,0:T(8,128)S(1)}, u32[]{:S(2)}, u32[]{:S(2)}) collective-permute-start(f32[640,1024]{1,0:T(8,128)S(1)} %pad_maximum_fusion), channel_id=1, source_target_pairs={{0,1},{1,0},{2,3},{3,2},{4,5},{5,4},{6,7},{7,6},{8,9},{9,8},{10,11... | collective-permute-start | bytes 7864328 | tf_op jit(solution)/shard_map/ppermute | solution.py:46
  41.0 18.9 %collective-permute-start.8 = (f32[320,1024]{1,0:T(8,128)S(1)}, f32[320,1024]{1,0:T(8,128)S(1)}, u32[]{:S(2)}, u32[]{:S(2)}) collective-permute-start(f32[320,1024]{1,0:T(8,128)S(1)} %collective-permute-done.3.refs_3_.refs_4_), channel_id=1, source_target_pairs={{0,18},{1,3},{2,16},{3,1},{16,2},{17,19},{18,0},{19,17},{4,22},{5,... | collective-permute-start | bytes 3932168 | tf_op jit(solution)/shard_map/ppermute | solution.py:42
  44.1 13.2 %collective-permute-start.10 = (f32[128,1024]{1,0:T(8,128)S(1)}, f32[128,1024]{1,0:T(8,128)S(1)}, u32[]{:S(2)}, u32[]{:S(2)}) collective-permute-start(f32[128,1024]{1,0:T(8,128)S(1)} %slice.43), channel_id=1, source_target_pairs={{0,4},{1,97},{2,6},{3,99},{16,20},{17,113},{18,22},{19,115},{4,0},... | collective-permute-start | bytes 1572872 | tf_op jit(solution)/shard_map/ppermute | solution.py:42
  44.8 12.5 %collective-permute-start.9 = (f32[128,1024]{1,0:T(8,128)S(1)}, f32[128,1024]{1,0:T(8,128)S(1)}, u32[]{:S(2)}, u32[]{:S(2)}) collective-permute-start(f32[128,1024]{1,0:T(8,128)S(1)} %slice.42), channel_id=1, source_target_pairs={{0,12},{1,33},{2,14},{3,35},{16,28},{17,49},{18,30},{19,51},{4,8},... | collective-permute-start | bytes 1572872 | tf_op jit(solution)/shard_map/ppermute | solution.py:42
  59.9 3.3 %collective-permute-start.12 = (f32[320,1024]{1,0:T(8,128)S(1)}, f32[320,1024]{1,0:T(8,128)S(1)}, u32[]{:S(2)}, u32[]{:S(2)}) collective-permute-start(f32[320,1024]{1,0:T(8,128)S(1)} %collective-permute-done.8.refs_2_.refs_1_), channel_id=1, source_target_pairs={{0,1},{1,0},{2,3},{3,2},{4,5},{5,4},{6,7},{7,6},{8,9},{9,8},{10,11... | collective-permute-start | bytes 3932168 | tf_op jit(solution)/shard_map/ppermute | solution.py:46
  67.2 9.3 %collective-permute-start.15 = (f32[128,1024]{1,0:T(8,128)S(1)}, f32[128,1024]{1,0:T(8,128)S(1)}, u32[]{:S(2)}, u32[]{:S(2)}) collective-permute-start(f32[128,1024]{1,0:T(8,128)S(1)} %slice.48), channel_id=1, source_target_pairs={{0,4},{1,97},{2,6},{3,99},{16,20},{17,113},{18,22},{19,115},{4,0},... | collective-permute-start | bytes 1572872 | tf_op jit(solution)/shard_map/ppermute | solution.py:42
  67.9 10.5 %collective-permute-start.16 = (f32[128,1024]{1,0:T(8,128)S(1)}, f32[128,1024]{1,0:T(8,128)S(1)}, u32[]{:S(2)}, u32[]{:S(2)}) collective-permute-start(f32[128,1024]{1,0:T(8,128)S(1)} %slice.49), channel_id=1, source_target_pairs={{0,12},{1,33},{2,14},{3,35},{16,28},{17,49},{18,30},{19,51},{4,8},... | collective-permute-start | bytes 1572872 | tf_op jit(solution)/shard_map/ppermute | solution.py:42
  70.4 13.6 %collective-permute-start.13 = (f32[128,1024]{1,0:T(8,128)S(1)}, f32[128,1024]{1,0:T(8,128)S(1)}, u32[]{:S(2)}, u32[]{:S(2)}) collective-permute-start(f32[128,1024]{1,0:T(8,128)S(1)} %get-tuple-element.98), channel_id=1, source_target_pairs={{0,12},{1,33},{2,14},{3,35},{16,28},{17,49},{18,30},{19,51},{4,8},... | collective-permute-start | bytes 1572872 | tf_op jit(solution)/shard_map/ppermute | solution.py:42
  71.2 12.8 %collective-permute-start.14 = (f32[128,1024]{1,0:T(8,128)S(1)}, f32[128,1024]{1,0:T(8,128)S(1)}, u32[]{:S(2)}, u32[]{:S(2)}) collective-permute-start(f32[128,1024]{1,0:T(8,128)S(1)} %get-tuple-element.99), channel_id=1, source_target_pairs={{0,4},{1,97},{2,6},{3,99},{16,20},{17,113},{18,22},{19,115},{4,0},... | collective-permute-start | bytes 1572872 | tf_op jit(solution)/shard_map/ppermute | solution.py:42
  84.1 10.5 %collective-permute-start.19 = (f32[128,1024]{1,0:T(8,128)S(1)}, f32[128,1024]{1,0:T(8,128)S(1)}, u32[]{:S(2)}, u32[]{:S(2)}) collective-permute-start(f32[128,1024]{1,0:T(8,128)S(1)} %slice_add_fusion.2), channel_id=1, source_target_pairs={{0,12},{1,33},{2,14},{3,35},{16,28},{17,49},{18,30},{19,51},{4,8},... | collective-permute-start | bytes 1572872 | tf_op jit(solution)/shard_map/ppermute | solution.py:42
  86.6 9.3 %collective-permute-start.17 = (f32[128,1024]{1,0:T(8,128)S(1)}, f32[128,1024]{1,0:T(8,128)S(1)}, u32[]{:S(2)}, u32[]{:S(2)}) collective-permute-start(f32[128,1024]{1,0:T(8,128)S(1)} %slice_add_fusion.3), channel_id=1, source_target_pairs={{0,4},{1,97},{2,6},{3,99},{16,20},{17,113},{18,22},{19,115},{4,0},... | collective-permute-start | bytes 1572872 | tf_op jit(solution)/shard_map/ppermute | solution.py:42
  96.2 9.6 %collective-permute-start.20 = (f32[64,1024]{1,0:T(8,128)S(1)}, f32[64,1024]{1,0:T(8,128)S(1)}, u32[]{:S(2)}, u32[]{:S(2)}) collective-permute-start(f32[64,1024]{1,0:T(8,128)S(1)} %get-tuple-element.109), channel_id=1, source_target_pairs={{0,96},{1,5},{2,98},{3,7},{16,112},{17,21},{18,114},{19,23},{4,100... | collective-permute-start | bytes 786440 | tf_op jit(solution)/shard_map/ppermute | solution.py:42
  99.1 7.9 %collective-permute-start.21 = (f32[64,1024]{1,0:T(8,128)S(1)}, f32[64,1024]{1,0:T(8,128)S(1)}, u32[]{:S(2)}, u32[]{:S(2)}) collective-permute-start(f32[64,1024]{1,0:T(8,128)S(1)} %get-tuple-element.110), channel_id=1, source_target_pairs={{0,64},{1,9},{2,66},{3,11},{16,80},{17,25},{18,82},{19,27},{4,68},... | collective-permute-start | bytes 786440 | tf_op jit(solution)/shard_map/ppermute | solution.py:42
  99.9 7.7 %collective-permute-start.18 = (f32[64,1024]{1,0:T(8,128)S(1)}, f32[64,1024]{1,0:T(8,128)S(1)}, u32[]{:S(2)}, u32[]{:S(2)}) collective-permute-start(f32[64,1024]{1,0:T(8,128)S(1)} %slice.60), channel_id=1, source_target_pairs={{0,32},{1,13},{2,34},{3,15},{16,48},{17,29},{18,50},{19,31},{4,36}... | collective-permute-start | bytes 786440 | tf_op jit(solution)/shard_map/ppermute | solution.py:42

commit v2 on v1

--- a/solution.py
+++ b/solution.py
@@ -51,14 +51,17 @@
 
 
 def lanes(w):
+    rest = -w.shape[1] % 128
+    if rest:
+        w = jnp.concatenate([w, jnp.zeros((w.shape[0], rest), w.dtype)], axis=1)
     return sum(w[:, k : k + 128] for k in range(0, w.shape[1], 128))
 
 
-def pair_kernel(counts, spans, fresh, last, scale, *refs):
+def pair_kernel(counts, n_others, block, span, fresh, last, scale, *refs):
     take = iter(refs)
     n_batch = len(counts)
     rows_refs = [[next(take) for _ in range(count)] for count in counts]
-    other_refs = [next(take) for _ in spans]
+    other_refs = [next(take) for _ in range(n_others)]
     state_in = [None if new else (next(take), next(take)) for new in fresh]
     state_out = [[next(take) for _ in range(count if last else 2)] for count in counts]
     others_b, others_norms = take
@@ -70,23 +73,21 @@
         return jnp.transpose(jnp.broadcast_to(norms, (norms.shape[0], 128)))[:8]
 
     gens, reals = [], []
-    for ref, span in zip(other_refs, spans):
-        if span:
-            gens.append(ref[:span])
-        reals.append(ref[span:])
-    reals = jnp.concatenate(reals, axis=0)
+    for ref in other_refs:
+        for at in range(0, ref.shape[0], block):
+            gens.append(ref[at : at + span])
+            reals.append(ref[at + span : at + block])
+    gens, reals = jnp.concatenate(gens, axis=0), jnp.concatenate(reals, axis=0)
     n_real = reals.shape[0]
     others_norms[:, :n_real] = norms_of(reals)
     others_b[:n_real] = reals.astype(jnp.bfloat16)
-    n_gen = sum(spans)
+    n_gen = gens.shape[0]
     end = n_real + n_gen
-    if n_gen:
-        gens = jnp.concatenate(gens, axis=0)
-        others_norms[:, n_real:] = norms_of(gens)
-        high = gens.astype(jnp.bfloat16)
-        others_b[n_real:end] = high
-        others_b[end : end + n_gen] = (gens - high.astype(jnp.float32)).astype(jnp.bfloat16)
-        others_b[end + n_gen :] = high
+    others_norms[:, n_real:] = norms_of(gens)
+    high = gens.astype(jnp.bfloat16)
+    others_b[n_real:end] = high
+    others_b[end : end + n_gen] = (gens - high.astype(jnp.float32)).astype(jnp.bfloat16)
+    others_b[end + n_gen :] = high
 
     for k in range(n_batch):
         rows = jnp.concatenate([r[...] for r in rows_refs[k]], axis=0)
@@ -100,14 +101,11 @@
             return (0.5 * factor) * e + e2 * (factor + (2.0 * factor) * e2)
 
         acc, sums = (0.0, 0.0) if fresh[k] else (state_in[k][0][...], state_in[k][1][...])
-        w = weights(0, n_real, -1.0)
-        sums = sums + lanes(w)
-        w = [w.astype(jnp.bfloat16)]
-        if n_gen:
-            w_gen = weights(n_real, end, float(scale))
-            sums = sums + lanes(w_gen)
-            w_hi = w_gen.astype(jnp.bfloat16)
-            w += [w_hi, w_hi, (w_gen - w_hi.astype(jnp.float32)).astype(jnp.bfloat16)]
+        w_real, w_gen = weights(0, n_real, -1.0), weights(n_real, end, float(scale))
+        sums = sums + lanes(w_real) + lanes(w_gen)
+        w_hi = w_gen.astype(jnp.bfloat16)
+        w_lo = (w_gen - w_hi.astype(jnp.float32)).astype(jnp.bfloat16)
+        w = [w_real.astype(jnp.bfloat16), w_hi, w_hi, w_lo]
         w = jnp.concatenate(w, axis=1)
         acc = acc + jnp.dot(w, others_b[...], preferred_element_type=jnp.float32)
         if last:
@@ -122,7 +120,7 @@
             state_out[k][1][...] = sums
 
 
-def pairs(rows, others, spans, states, last, scale):
+def pairs(rows, others, block, span, states, last, scale):
     count, width = sum(v.shape[0] for v in rows[0]), rows[0][0].shape[1]
     f32, bf16 = jnp.float32, jnp.bfloat16
     if last:
@@ -136,13 +134,14 @@
             if not last:
                 aliases.update({len(operands): 2 * k, len(operands) + 1: 2 * k + 1})
             operands += state
-    n_gen = sum(spans)
-    n_real = sum(v.shape[0] for v in others) - n_gen
+    n_others = sum(v.shape[0] for v in others)
+    n_gen = n_others // block * span
+    n_real = n_others - n_gen
     scratch = [pltpu.VMEM((n_real + 3 * n_gen, width), bf16), pltpu.VMEM((8, n_real + n_gen), f32)]
     n_pairs = count * len(rows) * (n_real + 2 * n_gen)
     vmem = pl.BlockSpec(memory_space=pltpu.VMEM)
     outs = pl.pallas_call(
-        functools.partial(pair_kernel, [len(batch) for batch in rows], spans, [s is None for s in states], last, scale),
+        functools.partial(pair_kernel, [len(batch) for batch in rows], len(others), block, span, [s is None for s in states], last, scale),
         out_shape=[v for batch in shapes for v in batch],
         in_specs=[vmem] * len(operands),
         out_specs=[vmem] * sum(len(batch) for batch in shapes),
@@ -187,55 +186,50 @@
     total_real = subset_rows.shape[0] * devices
     n = generated.shape[0]
     scale = total_real // total_gen
-    spans = (n, n)
 
     generated = resident(generated)
     real = real_bank.at[subset_rows].get(mode="promise_in_bounds", wrap_negative_indices=False)
     own = jnp.concatenate([generated, real], axis=0)
-    x_near, x_far = move(own, "zz", "near"), move(own, "zz", "far")
+    own_two = jnp.concatenate([own, swap(own)], axis=0)
+    count = own.shape[0]
+    add = functools.partial(pairs, block=count, span=n, scale=scale)
+    x_near = move(own_two, "zz", "near")
 
     line = [generated] + [move(generated, "xy", step) for step in ("near", "far", "both")]
     line = jnp.concatenate(line, axis=0)
     half = 2 * n
-    own_swapped = swap(after(own, line))
     line_near, line_far = move(line, "yx", "near"), move(line, "yx", "far")
-
-    x_near, x_far, line_near, line_far, own_swapped = lax.optimization_barrier(
-        (x_near, x_far, line_near, line_far, own_swapped)
-    )
-    x_both = move(x_near, "zz", "far")
-    x_level = jnp.concatenate([x_near, x_far], axis=0)
-    x_level = swap(x_level)
+    x_near, line_near, line_far = lax.optimization_barrier((x_near, line_near, line_far))
+    x_both = move(x_near[:count], "zz", "far")
+    x_far = swap(x_near)
     both = [move(line_near[:half], "yx", "far"), move(line_far[half:], "yx", "near")]
-    rows = [[line], [line_near], [line_far], both]
+    near_two, far_two = (line_near[:half], line_near[half:]), (line_far[:half], line_far[half:])
+    rows = [[line], [near_two[0], far_two[1]], [near_two[1], far_two[0]], both]
     s = [None] * SIDE
-    s[:3] = pairs(rows[:3], (own, own_swapped), spans, s[:3], None, scale)
-    x_level, _ = lax.optimization_barrier((x_level, s[:3]))
-    count = own.shape[0]
-    x_level = (x_near, x_far, x_level[:count], x_level[count:])
-    s[:3] = pairs(rows[:3], x_level, spans * 2, s[:3], None, scale)
-    x_both, both, _ = lax.optimization_barrier((x_both, both, s[:3]))
+    s[:3] = add(rows[:3], [own_two], states=s[:3], last=None)
+    x_far, _ = lax.optimization_barrier((x_far, s[:3]))
+    s[:3] = add(rows[:3], [x_near, x_far], states=s[:3], last=None)
+    both, _ = lax.optimization_barrier((both, s[:3]))
     rows[3] = both
-    both_two = (x_both, swap(x_both))
-    s[3:] = pairs(rows[3:], (own, own_swapped, *x_level), spans * 3, s[3:], None, scale)
-    both_two, s = lax.optimization_barrier((both_two, s))
-    part = [None] * SIDE
-    part[3:] = pairs(rows[3:], both_two, spans, s[3:], 1.0 / total_real, scale)
-    s, part[3] = lax.optimization_barrier((s, part[3]))
-    part[1:3] = pairs(rows[1:3], both_two, spans, s[1:3], 1.0 / total_real, scale)
-    part[:1] = pairs(rows[:1], both_two, spans, s[:1], 1.0 / total_real, scale)
-
-    (total,), (part_near,), (part_far,), both = part
-    add_near, add_far = move(both[0], "yx", "far"), move(both[1], "yx", "near")
-    near_rest, far_rest = move(part_near[half:], "yx", "near"), move(part_far[:half], "yx", "far")
-    add_near, add_far, near_rest, far_rest = lax.optimization_barrier((add_near, add_far, near_rest, far_rest))
-    to_near = move(part_near[:half] + add_near, "yx", "near")
-    to_far = move(part_far[half:] + add_far, "yx", "far")
-    total = jnp.concatenate([total[:half] + to_near + far_rest, total[half:] + near_rest + to_far], axis=0)
-    out = total[:n]
-    for k, step in enumerate(("near", "far", "both")):
-        out = out + move(total[(k + 1) * n : (k + 2) * n], "xy", step)
-    return out
+    s[3:] = add(rows[3:], [own_two, x_near, x_far], states=s[3:], last=None)
+    x_both, _ = lax.optimization_barrier((x_both, s))
+    both_swapped = swap(x_both)
+    s[2:] = add(rows[2:], [x_both], states=s[2:], last=None)
+    both_swapped, _ = lax.optimization_barrier((both_swapped, s))
+    near_rest, both = add(rows[2:], [both_swapped], states=s[2:], last=1.0 / total_real)
+    near_rest, far_rest = near_rest
+    line, near_far = add(rows[:2], [x_both, both_swapped], states=s[:2], last=1.0 / total_real)
+
+    first_near = move(jnp.concatenate([both[1], near_rest], axis=0), "yx", "near")
+    first_far = move(jnp.concatenate([both[0], far_rest], axis=0), "yx", "far")
+    first_near, first_far = lax.optimization_barrier((first_near, first_far))
+    to_near = move(near_far[0] + first_far[:half], "yx", "near")
+    to_far = move(near_far[1] + first_near[:half], "yx", "far")
+    (line,) = line
+    upper = line[:half] + first_far[half:] + to_near
+    lower = line[half:] + first_near[half:] + to_far
+    out = move(lower[n:], "xy", "both") + move(lower[:n], "xy", "far")
+    return upper[:n] + move(upper[n:], "xy", "near") + out
 
 
 def solution(mesh):

time: 110 us -> 105 us (0.955); the launches traced: 108 us -> 105 us
  starting transfers between devices: 30.8 us -> 27.1 us
    ppermute x19 -> x16, starting transfers between devices: 30.6 us -> 25.3 us  [move(): return lax.ppermute(v, AXES, STEPS[axes, step])]
    ppermute x3, waiting for transfers between devices: 0.01 us -> 4.34 us  [swap(): return lax.ppermute(v, AXES, SWAP)]
    ppermute x19 -> x16, waiting for transfers between devices: 52.3 us -> 48.8 us  [move(): return lax.ppermute(v, AXES, STEPS[axes, step])]
    ppermute x3, starting transfers between devices: 0.17 us -> 1.74 us  [swap(): return lax.ppermute(v, AXES, SWAP)]
    concatenate x1, other arithmetic: 1.21 us -> 0.1 us  [on_device(): line = jnp.concatenate(line, axis=0)]
  transfers between devices with their start and end apart: 22 -> 19, of which waited for: 14 -> 13; matrix products, arithmetic and copies ran while one was open for 3% -> 1% of each run, Pallas kernels for 13% -> 16%
where the time goes in v2:
time: 105 us
  waiting for transfers between devices  53.2 us (51%)
  starting transfers between devices  27.1 us (26%)
  Pallas kernels  20.5 us (20%)
  other arithmetic  2.52 us (2%)
  local copies, waits for them, and re-layouts  1.47 us (1%)
    ppermute x16, waiting for transfers between devices, move(): return lax.ppermute(v, AXES, STEPS[axes, step])  48.8 us
    ppermute x16, starting transfers between devices, move(): return lax.ppermute(v, AXES, STEPS[axes, step])  25.3 us
    pallas_call x6, Pallas kernels, pairs(): pl.pallas_call(functools.partial(pair_kernel, [len(batch) for batch in ro...  18.7 us
    ppermute x3, waiting for transfers between devices, swap(): return lax.ppermute(v, AXES, SWAP)  4.34 us
  transfers between devices with their start and end apart: 19, of which 13 were waited for; matrix products, arithmetic and copies ran while one was open for 1% of the time, Pallas kernels for 16%

profile of v2, /device:TPU:0, one launch (start us, length us, event | category | flops | bytes accessed | tf_op | source)
XLA Modules:
  0.0 105.0 jit_solution(926253663571945271)
XLA Ops:
  0.0 0.0 copy-start
  0.0 1.8 %shard_map.37 = f32[64,1024]{1,0:T(8,128)} custom-call(f32[64,1024]{1,0:T(8,128)} %v_ref.1), custom_call_target="tpu_custom_call" | custom-call | tf_op jit(solution)/shard_map/pallas_call | solution.py:176
  1.8 0.7 pad_clamp_fusion
  2.5 0.0 copy-done
  2.5 0.0 copy-start.1
  2.5 1.1 %gather_fusion = f32[256,1024]{1,0:T(8,128)S(1)} fusion(f32[512,1024]{1,0:T(8,128)S(1)} %copy-done, s32[1024]{0:T(1024)S(1)} %pad_clamp_fusion), kind=kCustom, calls=%fused_computation | custom fusion | bytes 2098176 | tf_op jit(solution)/shard_map/gather | solution.py:191
  3.6 0.0 copy-done.1
  3.6 0.1 pad_maximum_fusion.1
  3.7 0.1 collective-permute-start.3
  3.8 3.0 %collective-permute-done.3 = f32[320,1024]{1,0:T(8,128)S(1)} collective-permute-done((f32[320,1024]{1,0:T(8,128)S(1)}, f32[320,1024]{1,0:T(8,128)S(1)}, u32[]{:S(2)}, u32[]{:S(2)}) %collective-permute-start.3) | collective-permute-done | bytes 1310752 | tf_op jit(solution)/shard_map/ppermute | solution.py:46
  6.9 0.2 pad_maximum_fusion.refs_5_.refs_2_
  7.1 2.1 %collective-permute-start.4 = (f32[640,1024]{1,0:T(8,128)S(1)}, f32[640,1024]{1,0:T(8,128)S(1)}, u32[]{:S(2)}, u32[]{:S(2)}) collective-permute-start(f32[640,1024]{1,0:T(8,128)S(1)} %pad_maximum_fusion.refs_5_.refs_2_), channel_id=1, source_target_pairs={{0,2},{1,19},{2,0},{3,17},{16,18},{17,3},{18,16},{19,1},{4,6},{5,2... | collective-permute-start | bytes 7864328 | tf_op jit(solution)/shard_map/ppermute | solution.py:42
  9.2 1.5 %collective-permute-start = (f32[64,1024]{1,0:T(8,128)S(1)}, f32[64,1024]{1,0:T(8,128)S(1)}, u32[]{:S(2)}, u32[]{:S(2)}) collective-permute-start(f32[64,1024]{1,0:T(8,128)S(1)} %copy-done.1), channel_id=1, source_target_pairs={{0,32},{1,13},{2,34},{3,15},{16,48},{17,29},{18,50},{19,31},{4,36}... | collective-permute-start | bytes 786440 | tf_op jit(solution)/shard_map/ppermute | solution.py:42
  10.7 2.1 %collective-permute-start.1 = (f32[64,1024]{1,0:T(8,128)S(1)}, f32[64,1024]{1,0:T(8,128)S(1)}, u32[]{:S(2)}, u32[]{:S(2)}) collective-permute-start(f32[64,1024]{1,0:T(8,128)S(1)} %copy-done.1), channel_id=1, source_target_pairs={{0,96},{1,5},{2,98},{3,7},{16,112},{17,21},{18,114},{19,23},{4,100... | collective-permute-start | bytes 786440 | tf_op jit(solution)/shard_map/ppermute | solution.py:42
  12.8 0.6 collective-permute-start.2
  13.4 2.1 %collective-permute-done = f32[64,1024]{1,0:T(8,128)S(1)} collective-permute-done((f32[64,1024]{1,0:T(8,128)S(1)}, f32[64,1024]{1,0:T(8,128)S(1)}, u32[]{:S(2)}, u32[]{:S(2)}) %collective-permute-start) | collective-permute-done | bytes 262176 | tf_op jit(solution)/shard_map/ppermute | solution.py:42
  15.6 5.5 %collective-permute-done.1 = f32[64,1024]{1,0:T(8,128)S(1)} collective-permute-done((f32[64,1024]{1,0:T(8,128)S(1)}, f32[64,1024]{1,0:T(8,128)S(1)}, u32[]{:S(2)}, u32[]{:S(2)}) %collective-permute-start.1) | collective-permute-done | bytes 262176 | tf_op jit(solution)/shard_map/ppermute | solution.py:42
  21.1 0.0 collective-permute-done.2
  21.1 0.1 pad_maximum_fusion.2.refs_0_
  21.2 1.7 %collective-permute-start.5 = (f32[256,1024]{1,0:T(8,128)S(1)}, f32[256,1024]{1,0:T(8,128)S(1)}, u32[]{:S(2)}, u32[]{:S(2)}) collective-permute-start(f32[256,1024]{1,0:T(8,128)S(1)} %pad_maximum_fusion.2.refs_0_), channel_id=1, source_target_pairs={{0,4},{1,97},{2,6},{3,99},{16,20},{17,113},{18,22},{19,115},{4,0},... | collective-permute-start | bytes 3145736 | tf_op jit(solution)/shard_map/ppermute | solution.py:42
  22.8 2.2 %collective-permute-start.6 = (f32[256,1024]{1,0:T(8,128)S(1)}, f32[256,1024]{1,0:T(8,128)S(1)}, u32[]{:S(2)}, u32[]{:S(2)}) collective-permute-start(f32[256,1024]{1,0:T(8,128)S(1)} %pad_maximum_fusion.2.refs_0_), channel_id=1, source_target_pairs={{0,12},{1,33},{2,14},{3,35},{16,28},{17,49},{18,30},{19,51},{4,8},... | collective-permute-start | bytes 3145736 | tf_op jit(solution)/shard_map/ppermute | solution.py:42
  25.0 11.0 %collective-permute-done.5 = f32[256,1024]{1,0:T(8,128)S(1)} collective-permute-done((f32[256,1024]{1,0:T(8,128)S(1)}, f32[256,1024]{1,0:T(8,128)S(1)}, u32[]{:S(2)}, u32[]{:S(2)}) %collective-permute-start.5) | collective-permute-done | bytes 1048608 | tf_op jit(solution)/shard_map/ppermute | solution.py:42
  36.1 2.8 %collective-permute-done.6 = f32[256,1024]{1,0:T(8,128)S(1)} collective-permute-done((f32[256,1024]{1,0:T(8,128)S(1)}, f32[256,1024]{1,0:T(8,128)S(1)}, u32[]{:S(2)}, u32[]{:S(2)}) %collective-permute-start.6) | collective-permute-done | bytes 1048608 | tf_op jit(solution)/shard_map/ppermute | solution.py:42
  38.8 0.0 collective-permute-done.4.refs_5_.refs_3_
  38.9 1.4 %collective-permute-start.8 = (f32[640,1024]{1,0:T(8,128)S(1)}, f32[640,1024]{1,0:T(8,128)S(1)}, u32[]{:S(2)}, u32[]{:S(2)}) collective-permute-start(f32[640,1024]{1,0:T(8,128)S(1)} %collective-permute-done.4.refs_5_.refs_3_), channel_id=1, source_target_pairs={{0,1},{1,0},{2,3},{3,2},{4,5},{5,4},{6,7},{7,6},{8,9},{9,8},{10,11... | collective-permute-start | bytes 7864328 | tf_op jit(solution)/shard_map/ppermute | solution.py:46
  40.2 0.1 slice.49
  40.3 3.0 %collective-permute-start.7 = (f32[320,1024]{1,0:T(8,128)S(1)}, f32[320,1024]{1,0:T(8,128)S(1)}, u32[]{:S(2)}, u32[]{:S(2)}) collective-permute-start(f32[320,1024]{1,0:T(8,128)S(1)} %slice.49), channel_id=1, source_target_pairs={{0,18},{1,3},{2,16},{3,1},{16,2},{17,19},{18,0},{19,17},{4,22},{5,... | collective-permute-start | bytes 3932168 | tf_op jit(solution)/shard_map/ppermute | solution.py:42
  43.4 0.1 fusion.1
  43.5 1.7 %collective-permute-start.10 = (f32[128,1024]{1,0:T(8,128)S(1)}, f32[128,1024]{1,0:T(8,128)S(1)}, u32[]{:S(2)}, u32[]{:S(2)}) collective-permute-start(f32[128,1024]{1,0:T(8,128)S(1)} %get-tuple-element.78.refs_2_), channel_id=1, source_target_pairs={{0,4},{1,97},{2,6},{3,99},{16,20},{17,113},{18,22},{19,115},{4,0},... | collective-permute-start | bytes 1572872 | tf_op jit(solution)/shard_map/ppermute | solution.py:42
  45.1 0.1 fusion.2
  45.3 2.4 %collective-permute-start.9 = (f32[128,1024]{1,0:T(8,128)S(1)}, f32[128,1024]{1,0:T(8,128)S(1)}, u32[]{:S(2)}, u32[]{:S(2)}) collective-permute-start(f32[128,1024]{1,0:T(8,128)S(1)} %get-tuple-element.80.refs_1_), channel_id=1, source_target_pairs={{0,12},{1,33},{2,14},{3,35},{16,28},{17,49},{18,30},{19,51},{4,8},... | collective-permute-start | bytes 1572872 | tf_op jit(solution)/shard_map/ppermute | solution.py:42
  47.7 3.5 %shard_map.38 = (f32[256,1024]{1,0:T(8,128)S(1)}, f32[256,128]{1,0:T(8,128)S(1)}, f32[256,1024]{1,0:T(8,128)S(1)}, f32[256,128]{1,0:T(8,128)S(1)}, f32[256,1024]{1,0:T(8,128)S(1)}, /*index=5*/f32[256,128]{1,0:T(8,128)S(1)}) custom-call(f32[256,1024]{1,0:T(8,128)S(1)} %pad_maximum_fusion.2.refs_0_, f32[128,1024]{1,0:T(8,128)S(1)} %get-tuple-element.80.refs_1_, ...), custom_call_target="tpu_custom_call" | custom-call | flops 2415919104 | bytes 5767168 | tf_op jit(solution)/shard_map/pallas_call | solution.py:143
  51.2 0.0 collective-permute-done.8.refs_6_.refs_4_
  51.3 5.9 %shard_map.39 = (f32[256,1024]{1,0:T(8,128)S(1)}, f32[256,128]{1,0:T(8,128)S(1)}, f32[256,1024]{1,0:T(8,128)S(1)}, f32[256,128]{1,0:T(8,128)S(1)}, f32[256,1024]{1,0:T(8,128)S(1)}, /*index=5*/f32[256,128]{1,0:T(8,128)S(1)}) custom-call(f32[256,1024]{1,0:T(8,128)S(1)} %pad_maximum_fusion.2.re, ...), custom_call_target="tpu_custom_call", output_to_operand_aliasing={{0}: (7, {}), {1}: (8, {}), {2}: (9, {}), {3}: (10, {}), {4... | custom-call | flops 4831838208 | bytes 8388608 | tf_op jit(solution)/shard_map/pallas_call | solution.py:143
  57.2 0.0 collective-permute-done.10.refs_1_.refs_3_
  57.2 0.0 collective-permute-done.9.refs_0_.refs_2_
  57.2 3.3 %shard_map.40 = (f32[256,1024]{1,0:T(8,128)S(1)}, f32[256,128]{1,0:T(8,128)S(1)}) custom-call(f32[128,1024]{1,0:T(8,128)S(1)} %collective-permute-done.9.refs_0_.refs_2_, f32[128,1024]{1,0:T(8,128)S(1)} %collective-permute-done.10.refs_1_.refs_3_, f32[640,1024]{1,0:T(8,128)S(1)} %pad_maximum_fusion.refs_5_.refs_2_, ...), custom_call_target="tpu_custom_call" | custom-call | flops 2415919104 | bytes 11010048 | tf_op jit(solution)/shard_map/pallas_call | solution.py:143
  60.5 0.0 collective-permute-done.7.refs_4_.refs_3_
  60.5 0.3 collective-permute-start.11
  60.8 1.7 %shard_map.41 = (f32[256,1024]{1,0:T(8,128)S(1)}, f32[256,128]{1,0:T(8,128)S(1)}, f32[256,1024]{1,0:T(8,128)S(1)}, f32[256,128]{1,0:T(8,128)S(1)}) custom-call(f32[128,1024]{1,0:T(8,128)S(1)} %get-tuple-element.79.refs_3_.refs_0_, ...), custom_call_target="tpu_custom_call", output_to_operand_aliasing={{0}: (5, {}), {1}: (6, {}), {2}: (7, {}), {3}: (8, {})} | custom-call | flops 805306368 | bytes 4456448 | tf_op jit(solution)/shard_map/pallas_call | solution.py:143
  62.5 1.3 %collective-permute-done.11.refs_4_ = f32[320,1024]{1,0:T(8,128)S(1)} collective-permute-done((f32[320,1024]{1,0:T(8,128)S(1)}, f32[320,1024]{1,0:T(8,128)S(1)}, u32[]{:S(2)}, u32[]{:S(2)}) %collective-permute-start.11) | collective-permute-done | bytes 1310752 | tf_op jit(solution)/shard_map/ppermute | solution.py:46
  63.9 1.7 %shard_map.43 = (f32[128,1024]{1,0:T(8,128)S(1)}, f32[128,1024]{1,0:T(8,128)S(1)}, f32[128,1024]{1,0:T(8,128)S(1)}, f32[128,1024]{1,0:T(8,128)S(1)}) custom-call(f32[128,1024]{1,0:T(8,128)S(1)} %get-tuple-element.79.refs_3_.refs_0_, f32[128,1024]{1,0:T(8,128)S(1)} %get-tuple-element.77.refs_4_.refs_1_, ...), custom_call_target="tpu_custom_call" | custom-call | flops 805306368 | bytes 4456448 | tf_op jit(solution)/shard_map/pallas_call | solution.py:143
  65.6 0.1 pad_maximum_fusion.4
  65.7 1.5 %collective-permute-start.13 = (f32[256,1024]{1,0:T(8,128)S(1)}, f32[256,1024]{1,0:T(8,128)S(1)}, u32[]{:S(2)}, u32[]{:S(2)}) collective-permute-start(f32[256,1024]{1,0:T(8,128)S(1)} %pad_maximum_fusion.4), channel_id=1, source_target_pairs={{0,12},{1,33},{2,14},{3,35},{16,28},{17,49},{18,30},{19,51},{4,8},... | collective-permute-start | bytes 3145736 | tf_op jit(solution)/shard_map/ppermute | solution.py:42
  67.2 0.1 pad_maximum_fusion.3
  67.3 0.2 collective-permute-start.12
  67.6 2.5 %shard_map.42 = (f32[256,1024]{1,0:T(8,128)S(1)}, f32[128,1024]{1,0:T(8,128)S(1)}, f32[128,1024]{1,0:T(8,128)S(1)}) custom-call(f32[256,1024]{1,0:T(8,128)S(1)} %pad_maximum_fusion.2.refs_0_, f32[128,1024]{1,0:T(8,128)S(1)} %get-tuple-element.80.refs_1_, f32[128,1024]{1,0:T(8,128)S(1)} %get-tuple-element.78.refs_2_, ...), custom_call_target="tpu_custom_call" | custom-call | flops 1610612736 | bytes 5767168 | tf_op jit(solution)/shard_map/pallas_call | solution.py:143
  70.1 11.7 %collective-permute-done.13 = f32[256,1024]{1,0:T(8,128)S(1)} collective-permute-done((f32[256,1024]{1,0:T(8,128)S(1)}, f32[256,1024]{1,0:T(8,128)S(1)}, u32[]{:S(2)}, u32[]{:S(2)}) %collective-permute-start.13) | collective-permute-done | bytes 1048608 | tf_op jit(solution)/shard_map/ppermute | solution.py:42
  81.8 0.4 collective-permute-done.12
  82.2 0.1 slice_add_fusion.1
  82.3 0.2 collective-permute-start.14
  82.5 0.1 slice_add_fusion
  82.6 1.8 %collective-permute-start.16 = (f32[128,1024]{1,0:T(8,128)S(1)}, f32[128,1024]{1,0:T(8,128)S(1)}, u32[]{:S(2)}, u32[]{:S(2)}) collective-permute-start(f32[128,1024]{1,0:T(8,128)S(1)} %slice_add_fusion), channel_id=1, source_target_pairs={{0,12},{1,33},{2,14},{3,35},{16,28},{17,49},{18,30},{19,51},{4,8},... | collective-permute-start | bytes 1572872 | tf_op jit(solution)/shard_map/ppermute | solution.py:42
  84.4 7.2 %collective-permute-done.14 = f32[128,1024]{1,0:T(8,128)S(1)} collective-permute-done((f32[128,1024]{1,0:T(8,128)S(1)}, f32[128,1024]{1,0:T(8,128)S(1)}, u32[]{:S(2)}, u32[]{:S(2)}) %collective-permute-start.14) | collective-permute-done | bytes 524320 | tf_op jit(solution)/shard_map/ppermute | solution.py:42
  91.5 1.5 %collective-permute-done.16 = f32[128,1024]{1,0:T(8,128)S(1)} collective-permute-done((f32[128,1024]{1,0:T(8,128)S(1)}, f32[128,1024]{1,0:T(8,128)S(1)}, u32[]{:S(2)}, u32[]{:S(2)}) %collective-permute-start.16) | collective-permute-done | bytes 524320 | tf_op jit(solution)/shard_map/ppermute | solution.py:42
  93.0 0.3 add_add_fusion
  93.4 3.1 %collective-permute-start.17 = (f32[64,1024]{1,0:T(8,128)S(1)}, f32[64,1024]{1,0:T(8,128)S(1)}, u32[]{:S(2)}, u32[]{:S(2)}) collective-permute-start(f32[64,1024]{1,0:T(8,128)S(1)} %get-tuple-element.82), channel_id=1, source_target_pairs={{0,64},{1,9},{2,66},{3,11},{16,80},{17,25},{18,82},{19,27},{4,68},... | collective-permute-start | bytes 786440 | tf_op jit(solution)/shard_map/ppermute | solution.py:42
  96.5 1.1 %collective-permute-start.18 = (f32[64,1024]{1,0:T(8,128)S(1)}, f32[64,1024]{1,0:T(8,128)S(1)}, u32[]{:S(2)}, u32[]{:S(2)}) collective-permute-start(f32[64,1024]{1,0:T(8,128)S(1)} %get-tuple-element.81), channel_id=1, source_target_pairs={{0,96},{1,5},{2,98},{3,7},{16,112},{17,21},{18,114},{19,23},{4,100... | collective-permute-start | bytes 786440 | tf_op jit(solution)/shard_map/ppermute | solution.py:42
  97.6 0.1 collective-permute-start.15
  97.7 3.6 %collective-permute-done.17 = f32[64,1024]{1,0:T(8,128)S(1)} collective-permute-done((f32[64,1024]{1,0:T(8,128)S(1)}, f32[64,1024]{1,0:T(8,128)S(1)}, u32[]{:S(2)}, u32[]{:S(2)}) %collective-permute-start.17) | collective-permute-done | bytes 262176 | tf_op jit(solution)/shard_map/ppermute | solution.py:42
  101.3 2.8 %collective-permute-done.18 = f32[64,1024]{1,0:T(8,128)S(1)} collective-permute-done((f32[64,1024]{1,0:T(8,128)S(1)}, f32[64,1024]{1,0:T(8,128)S(1)}, u32[]{:S(2)}, u32[]{:S(2)}) %collective-permute-start.18) | collective-permute-done | bytes 262176 | tf_op jit(solution)/shard_map/ppermute | solution.py:42
  104.1 0.1 collective-permute-done.15
  104.2 0.8 fusion
  (2 shorter events, 0.1 us)
Async XLA Ops:
  0.0 2.5 %copy-start = (f32[512,1024]{1,0:T(8,128)S(1)}, f32[512,1024]{1,0:T(8,128)}, u32[]{:S(2)}) copy-start(f32[512,1024]{1,0:T(8,128)} %param.4) | copy-start | bytes 6291460
  2.5 1.1 %copy-start.1 = (f32[64,1024]{1,0:T(8,128)S(1)}, f32[64,1024]{1,0:T(8,128)}, u32[]{:S(2)}) copy-start(f32[64,1024]{1,0:T(8,128)} %shard_map.37) | copy-start | bytes 786436
  3.7 3.1 %collective-permute-start.3 = (f32[320,1024]{1,0:T(8,128)S(1)}, f32[320,1024]{1,0:T(8,128)S(1)}, u32[]{:S(2)}, u32[]{:S(2)}) collective-permute-start(f32[320,1024]{1,0:T(8,128)S(1)} %pad_maximum_fusion.1), channel_id=1, source_target_pairs={{0,1},{1,0},{2,3},{3,2},{4,5},{5,4},{6,7},{7,6},{8,9},{9,8},{10,11... | collective-permute-start | bytes 3932168 | tf_op jit(solution)/shard_map/ppermute | solution.py:46
  7.1 31.7 %collective-permute-start.4 = (f32[640,1024]{1,0:T(8,128)S(1)}, f32[640,1024]{1,0:T(8,128)S(1)}, u32[]{:S(2)}, u32[]{:S(2)}) collective-permute-start(f32[640,1024]{1,0:T(8,128)S(1)} %pad_maximum_fusion.refs_5_.refs_2_), channel_id=1, source_target_pairs={{0,2},{1,19},{2,0},{3,17},{16,18},{17,3},{18,16},{19,1},{4,6},{5,2... | collective-permute-start | bytes 7864328 | tf_op jit(solution)/shard_map/ppermute | solution.py:42
  9.2 6.4 %collective-permute-start = (f32[64,1024]{1,0:T(8,128)S(1)}, f32[64,1024]{1,0:T(8,128)S(1)}, u32[]{:S(2)}, u32[]{:S(2)}) collective-permute-start(f32[64,1024]{1,0:T(8,128)S(1)} %copy-done.1), channel_id=1, source_target_pairs={{0,32},{1,13},{2,34},{3,15},{16,48},{17,29},{18,50},{19,31},{4,36}... | collective-permute-start | bytes 786440 | tf_op jit(solution)/shard_map/ppermute | solution.py:42
  10.7 10.4 %collective-permute-start.1 = (f32[64,1024]{1,0:T(8,128)S(1)}, f32[64,1024]{1,0:T(8,128)S(1)}, u32[]{:S(2)}, u32[]{:S(2)}) collective-permute-start(f32[64,1024]{1,0:T(8,128)S(1)} %copy-done.1), channel_id=1, source_target_pairs={{0,96},{1,5},{2,98},{3,7},{16,112},{17,21},{18,114},{19,23},{4,100... | collective-permute-start | bytes 786440 | tf_op jit(solution)/shard_map/ppermute | solution.py:42
  12.8 8.3 %collective-permute-start.2 = (f32[64,1024]{1,0:T(8,128)S(1)}, f32[64,1024]{1,0:T(8,128)S(1)}, u32[]{:S(2)}, u32[]{:S(2)}) collective-permute-start(f32[64,1024]{1,0:T(8,128)S(1)} %copy-done.1), channel_id=1, source_target_pairs={{0,64},{1,9},{2,66},{3,11},{16,80},{17,25},{18,82},{19,27},{4,68},... | collective-permute-start | bytes 786440 | tf_op jit(solution)/shard_map/ppermute | solution.py:42
  21.2 14.9 %collective-permute-start.5 = (f32[256,1024]{1,0:T(8,128)S(1)}, f32[256,1024]{1,0:T(8,128)S(1)}, u32[]{:S(2)}, u32[]{:S(2)}) collective-permute-start(f32[256,1024]{1,0:T(8,128)S(1)} %pad_maximum_fusion.2.refs_0_), channel_id=1, source_target_pairs={{0,4},{1,97},{2,6},{3,99},{16,20},{17,113},{18,22},{19,115},{4,0},... | collective-permute-start | bytes 3145736 | tf_op jit(solution)/shard_map/ppermute | solution.py:42
  22.8 16.0 %collective-permute-start.6 = (f32[256,1024]{1,0:T(8,128)S(1)}, f32[256,1024]{1,0:T(8,128)S(1)}, u32[]{:S(2)}, u32[]{:S(2)}) collective-permute-start(f32[256,1024]{1,0:T(8,128)S(1)} %pad_maximum_fusion.2.refs_0_), channel_id=1, source_target_pairs={{0,12},{1,33},{2,14},{3,35},{16,28},{17,49},{18,30},{19,51},{4,8},... | collective-permute-start | bytes 3145736 | tf_op jit(solution)/shard_map/ppermute | solution.py:42
  38.9 12.4 %collective-permute-start.8 = (f32[640,1024]{1,0:T(8,128)S(1)}, f32[640,1024]{1,0:T(8,128)S(1)}, u32[]{:S(2)}, u32[]{:S(2)}) collective-permute-start(f32[640,1024]{1,0:T(8,128)S(1)} %collective-permute-done.4.refs_5_.refs_3_), channel_id=1, source_target_pairs={{0,1},{1,0},{2,3},{3,2},{4,5},{5,4},{6,7},{7,6},{8,9},{9,8},{10,11... | collective-permute-start | bytes 7864328 | tf_op jit(solution)/shard_map/ppermute | solution.py:46
  40.3 20.2 %collective-permute-start.7 = (f32[320,1024]{1,0:T(8,128)S(1)}, f32[320,1024]{1,0:T(8,128)S(1)}, u32[]{:S(2)}, u32[]{:S(2)}) collective-permute-start(f32[320,1024]{1,0:T(8,128)S(1)} %slice.49), channel_id=1, source_target_pairs={{0,18},{1,3},{2,16},{3,1},{16,2},{17,19},{18,0},{19,17},{4,22},{5,... | collective-permute-start | bytes 3932168 | tf_op jit(solution)/shard_map/ppermute | solution.py:42
  43.5 13.7 %collective-permute-start.10 = (f32[128,1024]{1,0:T(8,128)S(1)}, f32[128,1024]{1,0:T(8,128)S(1)}, u32[]{:S(2)}, u32[]{:S(2)}) collective-permute-start(f32[128,1024]{1,0:T(8,128)S(1)} %get-tuple-element.78.refs_2_), channel_id=1, source_target_pairs={{0,4},{1,97},{2,6},{3,99},{16,20},{17,113},{18,22},{19,115},{4,0},... | collective-permute-start | bytes 1572872 | tf_op jit(solution)/shard_map/ppermute | solution.py:42
  45.3 12.0 %collective-permute-start.9 = (f32[128,1024]{1,0:T(8,128)S(1)}, f32[128,1024]{1,0:T(8,128)S(1)}, u32[]{:S(2)}, u32[]{:S(2)}) collective-permute-start(f32[128,1024]{1,0:T(8,128)S(1)} %get-tuple-element.80.refs_1_), channel_id=1, source_target_pairs={{0,12},{1,33},{2,14},{3,35},{16,28},{17,49},{18,30},{19,51},{4,8},... | collective-permute-start | bytes 1572872 | tf_op jit(solution)/shard_map/ppermute | solution.py:42
  60.5 3.3 %collective-permute-start.11 = (f32[320,1024]{1,0:T(8,128)S(1)}, f32[320,1024]{1,0:T(8,128)S(1)}, u32[]{:S(2)}, u32[]{:S(2)}) collective-permute-start(f32[320,1024]{1,0:T(8,128)S(1)} %collective-permute-done.7.refs_4_.refs_3_), channel_id=1, source_target_pairs={{0,1},{1,0},{2,3},{3,2},{4,5},{5,4},{6,7},{7,6},{8,9},{9,8},{10,11... | collective-permute-start | bytes 3932168 | tf_op jit(solution)/shard_map/ppermute | solution.py:46
  65.7 16.1 %collective-permute-start.13 = (f32[256,1024]{1,0:T(8,128)S(1)}, f32[256,1024]{1,0:T(8,128)S(1)}, u32[]{:S(2)}, u32[]{:S(2)}) collective-permute-start(f32[256,1024]{1,0:T(8,128)S(1)} %pad_maximum_fusion.4), channel_id=1, source_target_pairs={{0,12},{1,33},{2,14},{3,35},{16,28},{17,49},{18,30},{19,51},{4,8},... | collective-permute-start | bytes 3145736 | tf_op jit(solution)/shard_map/ppermute | solution.py:42
  67.3 14.9 %collective-permute-start.12 = (f32[256,1024]{1,0:T(8,128)S(1)}, f32[256,1024]{1,0:T(8,128)S(1)}, u32[]{:S(2)}, u32[]{:S(2)}) collective-permute-start(f32[256,1024]{1,0:T(8,128)S(1)} %pad_maximum_fusion.3), channel_id=1, source_target_pairs={{0,4},{1,97},{2,6},{3,99},{16,20},{17,113},{18,22},{19,115},{4,0},... | collective-permute-start | bytes 3145736 | tf_op jit(solution)/shard_map/ppermute | solution.py:42
  82.3 9.3 %collective-permute-start.14 = (f32[128,1024]{1,0:T(8,128)S(1)}, f32[128,1024]{1,0:T(8,128)S(1)}, u32[]{:S(2)}, u32[]{:S(2)}) collective-permute-start(f32[128,1024]{1,0:T(8,128)S(1)} %slice_add_fusion.1), channel_id=1, source_target_pairs={{0,4},{1,97},{2,6},{3,99},{16,20},{17,113},{18,22},{19,115},{4,0},... | collective-permute-start | bytes 1572872 | tf_op jit(solution)/shard_map/ppermute | solution.py:42
  82.6 10.5 %collective-permute-start.16 = (f32[128,1024]{1,0:T(8,128)S(1)}, f32[128,1024]{1,0:T(8,128)S(1)}, u32[]{:S(2)}, u32[]{:S(2)}) collective-permute-start(f32[128,1024]{1,0:T(8,128)S(1)} %slice_add_fusion), channel_id=1, source_target_pairs={{0,12},{1,33},{2,14},{3,35},{16,28},{17,49},{18,30},{19,51},{4,8},... | collective-permute-start | bytes 1572872 | tf_op jit(solution)/shard_map/ppermute | solution.py:42
  93.4 8.0 %collective-permute-start.17 = (f32[64,1024]{1,0:T(8,128)S(1)}, f32[64,1024]{1,0:T(8,128)S(1)}, u32[]{:S(2)}, u32[]{:S(2)}) collective-permute-start(f32[64,1024]{1,0:T(8,128)S(1)} %get-tuple-element.82), channel_id=1, source_target_pairs={{0,64},{1,9},{2,66},{3,11},{16,80},{17,25},{18,82},{19,27},{4,68},... | collective-permute-start | bytes 786440 | tf_op jit(solution)/shard_map/ppermute | solution.py:42
  96.5 7.7 %collective-permute-start.18 = (f32[64,1024]{1,0:T(8,128)S(1)}, f32[64,1024]{1,0:T(8,128)S(1)}, u32[]{:S(2)}, u32[]{:S(2)}) collective-permute-start(f32[64,1024]{1,0:T(8,128)S(1)} %get-tuple-element.81), channel_id=1, source_target_pairs={{0,96},{1,5},{2,98},{3,7},{16,112},{17,21},{18,114},{19,23},{4,100... | collective-permute-start | bytes 786440 | tf_op jit(solution)/shard_map/ppermute | solution.py:42
  97.6 6.6 %collective-permute-start.15 = (f32[64,1024]{1,0:T(8,128)S(1)}, f32[64,1024]{1,0:T(8,128)S(1)}, u32[]{:S(2)}, u32[]{:S(2)}) collective-permute-start(f32[64,1024]{1,0:T(8,128)S(1)} %slice.65), channel_id=1, source_target_pairs={{0,32},{1,13},{2,34},{3,15},{16,48},{17,29},{18,50},{19,31},{4,36}... | collective-permute-start | bytes 786440 | tf_op jit(solution)/shard_map/ppermute | solution.py:42

commit v3 on v2

--- a/solution.py
+++ b/solution.py
@@ -203,8 +203,7 @@
     x_both = move(x_near[:count], "zz", "far")
     x_far = swap(x_near)
     both = [move(line_near[:half], "yx", "far"), move(line_far[half:], "yx", "near")]
-    near_two, far_two = (line_near[:half], line_near[half:]), (line_far[:half], line_far[half:])
-    rows = [[line], [near_two[0], far_two[1]], [near_two[1], far_two[0]], both]
+    rows = [[line], [line_near], [line_far], both]
     s = [None] * SIDE
     s[:3] = add(rows[:3], [own_two], states=s[:3], last=None)
     x_far, _ = lax.optimization_barrier((x_far, s[:3]))
@@ -214,20 +213,23 @@
     s[3:] = add(rows[3:], [own_two, x_near, x_far], states=s[3:], last=None)
     x_both, _ = lax.optimization_barrier((x_both, s))
     both_swapped = swap(x_both)
-    s[2:] = add(rows[2:], [x_both], states=s[2:], last=None)
+    s[1:] = add(rows[1:], [x_both], states=s[1:], last=None)
     both_swapped, _ = lax.optimization_barrier((both_swapped, s))
-    near_rest, both = add(rows[2:], [both_swapped], states=s[2:], last=1.0 / total_real)
-    near_rest, far_rest = near_rest
-    line, near_far = add(rows[:2], [x_both, both_swapped], states=s[:2], last=1.0 / total_real)
-
-    first_near = move(jnp.concatenate([both[1], near_rest], axis=0), "yx", "near")
-    first_far = move(jnp.concatenate([both[0], far_rest], axis=0), "yx", "far")
-    first_near, first_far = lax.optimization_barrier((first_near, first_far))
-    to_near = move(near_far[0] + first_far[:half], "yx", "near")
-    to_far = move(near_far[1] + first_near[:half], "yx", "far")
-    (line,) = line
-    upper = line[:half] + first_far[half:] + to_near
-    lower = line[half:] + first_near[half:] + to_far
+    (both,) = add(rows[3:], [both_swapped], states=s[3:], last=1.0 / total_real)
+    s, both = lax.optimization_barrier((s, both))
+    (line_near,), (line_far,) = add(rows[1:3], [both_swapped], states=s[1:3], last=1.0 / total_real)
+    ((line,),) = add(rows[:1], [x_both, both_swapped], states=s[:1], last=1.0 / total_real)
+
+    add_near, add_far = move(both[0], "yx", "far"), move(both[1], "yx", "near")
+    extra = 16
+    near_rest = move(line_near[half - extra :], "yx", "near")
+    far_rest = move(line_far[: half + extra], "yx", "far")
+    add_near, add_far, line = lax.optimization_barrier((add_near, add_far, line))
+    to_near = move(line_near[:half] + add_near, "yx", "near")
+    to_far = move(line_far[half:] + add_far, "yx", "far")
+    line = line + jnp.concatenate([far_rest[:half], near_rest[extra:]], axis=0)
+    line, to_near, to_far = lax.optimization_barrier((line, to_near, to_far))
+    upper, lower = line[:half] + to_near, line[half:] + to_far
     out = move(lower[n:], "xy", "both") + move(lower[:n], "xy", "far")
     return upper[:n] + move(upper[n:], "xy", "near") + out
 

time: 105 us -> 99.4 us (0.947)
  waiting for transfers between devices: 53.2 us -> 44.4 us
  starting transfers between devices: 27.1 us -> 29.5 us
    ppermute x16 -> x18, waiting for transfers between devices: 48.8 us -> 40.9 us  [move(): return lax.ppermute(v, AXES, STEPS[axes, step])]
    ppermute x16 -> x18, starting transfers between devices: 25.3 us -> 27.8 us  [move(): return lax.ppermute(v, AXES, STEPS[axes, step])]
    pallas_call x6 -> x7, Pallas kernels: 18.7 us -> 19.4 us  [pairs(): pl.pallas_call(functools.partial(pair_kernel, [len(batch) for batch in ro...]
  transfers between devices with their start and end apart: 19 -> 21, of which waited for: 13 -> 15; matrix products, arithmetic and copies ran while one was open for 1% -> 1% of each run, Pallas kernels for 16% -> 19%
where the time goes in v3:
time: 99.4 us; the launch traced here: 99.2 us
  waiting for transfers between devices  44.4 us (45%)
  starting transfers between devices  29.5 us (30%)
  Pallas kernels  21.2 us (21%)
  other arithmetic  2.34 us (2%)
  local copies, waits for them, and re-layouts  1.52 us (2%)
    ppermute x18, waiting for transfers between devices, move(): return lax.ppermute(v, AXES, STEPS[axes, step])  40.9 us
    ppermute x18, starting transfers between devices, move(): return lax.ppermute(v, AXES, STEPS[axes, step])  27.8 us
    pallas_call x7, Pallas kernels, pairs(): pl.pallas_call(functools.partial(pair_kernel, [len(batch) for batch in ro...  19.4 us
    ppermute x3, waiting for transfers between devices, swap(): return lax.ppermute(v, AXES, SWAP)  3.52 us
  transfers between devices with their start and end apart: 21, of which 15 were waited for; matrix products, arithmetic and copies ran while one was open for 1% of the time, Pallas kernels for 19%

profile of v3, /device:TPU:0, one launch (start us, length us, event | category | flops | bytes accessed | tf_op | source)
XLA Modules:
  0.0 99.2 jit_solution(17223785037127413015)
XLA Ops:
  0.0 0.0 copy-start
  0.0 1.8 %shard_map.37 = f32[64,1024]{1,0:T(8,128)} custom-call(f32[64,1024]{1,0:T(8,128)} %v_ref.1), custom_call_target="tpu_custom_call" | custom-call | tf_op jit(solution)/shard_map/pallas_call | solution.py:176
  1.8 0.7 pad_clamp_fusion
  2.5 0.0 copy-done
  2.5 1.1 %gather_fusion = f32[256,1024]{1,0:T(8,128)S(1)} fusion(f32[512,1024]{1,0:T(8,128)S(1)} %copy-done, s32[1024]{0:T(1024)S(1)} %pad_clamp_fusion), kind=kCustom, calls=%fused_computation | custom fusion | bytes 2098176 | tf_op jit(solution)/shard_map/gather | solution.py:191
  3.6 0.0 copy-done.1
  3.6 0.1 pad_maximum_fusion.1
  3.7 0.1 collective-permute-start.3
  3.8 3.0 %collective-permute-done.3 = f32[320,1024]{1,0:T(8,128)S(1)} collective-permute-done((f32[320,1024]{1,0:T(8,128)S(1)}, f32[320,1024]{1,0:T(8,128)S(1)}, u32[]{:S(2)}, u32[]{:S(2)}) %collective-permute-start.3) | collective-permute-done | bytes 1310752 | tf_op jit(solution)/shard_map/ppermute | solution.py:46
  6.8 0.3 pad_maximum_fusion.refs_3_.refs_2_
  7.1 2.1 %collective-permute-start.4 = (f32[640,1024]{1,0:T(8,128)S(1)}, f32[640,1024]{1,0:T(8,128)S(1)}, u32[]{:S(2)}, u32[]{:S(2)}) collective-permute-start(f32[640,1024]{1,0:T(8,128)S(1)} %pad_maximum_fusion.refs_3_.refs_2_), channel_id=1, source_target_pairs={{0,2},{1,19},{2,0},{3,17},{16,18},{17,3},{18,16},{19,1},{4,6},{5,2... | collective-permute-start | bytes 7864328 | tf_op jit(solution)/shard_map/ppermute | solution.py:42
  9.2 1.5 %collective-permute-start = (f32[64,1024]{1,0:T(8,128)S(1)}, f32[64,1024]{1,0:T(8,128)S(1)}, u32[]{:S(2)}, u32[]{:S(2)}) collective-permute-start(f32[64,1024]{1,0:T(8,128)S(1)} %copy-done.1), channel_id=1, source_target_pairs={{0,32},{1,13},{2,34},{3,15},{16,48},{17,29},{18,50},{19,31},{4,36}... | collective-permute-start | bytes 786440 | tf_op jit(solution)/shard_map/ppermute | solution.py:42
  10.7 2.1 %collective-permute-start.1 = (f32[64,1024]{1,0:T(8,128)S(1)}, f32[64,1024]{1,0:T(8,128)S(1)}, u32[]{:S(2)}, u32[]{:S(2)}) collective-permute-start(f32[64,1024]{1,0:T(8,128)S(1)} %copy-done.1), channel_id=1, source_target_pairs={{0,96},{1,5},{2,98},{3,7},{16,112},{17,21},{18,114},{19,23},{4,100... | collective-permute-start | bytes 786440 | tf_op jit(solution)/shard_map/ppermute | solution.py:42
  12.8 0.6 collective-permute-start.2
  13.4 2.1 %collective-permute-done = f32[64,1024]{1,0:T(8,128)S(1)} collective-permute-done((f32[64,1024]{1,0:T(8,128)S(1)}, f32[64,1024]{1,0:T(8,128)S(1)}, u32[]{:S(2)}, u32[]{:S(2)}) %collective-permute-start) | collective-permute-done | bytes 262176 | tf_op jit(solution)/shard_map/ppermute | solution.py:42
  15.5 5.5 %collective-permute-done.1 = f32[64,1024]{1,0:T(8,128)S(1)} collective-permute-done((f32[64,1024]{1,0:T(8,128)S(1)}, f32[64,1024]{1,0:T(8,128)S(1)}, u32[]{:S(2)}, u32[]{:S(2)}) %collective-permute-start.1) | collective-permute-done | bytes 262176 | tf_op jit(solution)/shard_map/ppermute | solution.py:42
  21.0 0.0 collective-permute-done.2
  21.1 0.1 pad_maximum_fusion.2.refs_0_
  21.2 1.7 %collective-permute-start.5 = (f32[256,1024]{1,0:T(8,128)S(1)}, f32[256,1024]{1,0:T(8,128)S(1)}, u32[]{:S(2)}, u32[]{:S(2)}) collective-permute-start(f32[256,1024]{1,0:T(8,128)S(1)} %pad_maximum_fusion.2.refs_0_), channel_id=1, source_target_pairs={{0,4},{1,97},{2,6},{3,99},{16,20},{17,113},{18,22},{19,115},{4,0},... | collective-permute-start | bytes 3145736 | tf_op jit(solution)/shard_map/ppermute | solution.py:42
  22.8 2.2 %collective-permute-start.6 = (f32[256,1024]{1,0:T(8,128)S(1)}, f32[256,1024]{1,0:T(8,128)S(1)}, u32[]{:S(2)}, u32[]{:S(2)}) collective-permute-start(f32[256,1024]{1,0:T(8,128)S(1)} %pad_maximum_fusion.2.refs_0_), channel_id=1, source_target_pairs={{0,12},{1,33},{2,14},{3,35},{16,28},{17,49},{18,30},{19,51},{4,8},... | collective-permute-start | bytes 3145736 | tf_op jit(solution)/shard_map/ppermute | solution.py:42
  25.0 11.0 %collective-permute-done.5.refs_1_.refs_0_ = f32[256,1024]{1,0:T(8,128)S(1)} collective-permute-done((f32[256,1024]{1,0:T(8,128)S(1)}, f32[256,1024]{1,0:T(8,128)S(1)}, u32[]{:S(2)}, u32[]{:S(2)}) %collective-permute-start.5) | collective-permute-done | bytes 1048608 | tf_op jit(solution)/shard_map/ppermute | solution.py:42
  36.0 2.8 %collective-permute-done.6.refs_2_.refs_1_ = f32[256,1024]{1,0:T(8,128)S(1)} collective-permute-done((f32[256,1024]{1,0:T(8,128)S(1)}, f32[256,1024]{1,0:T(8,128)S(1)}, u32[]{:S(2)}, u32[]{:S(2)}) %collective-permute-start.6) | collective-permute-done | bytes 1048608 | tf_op jit(solution)/shard_map/ppermute | solution.py:42
  38.8 0.0 collective-permute-done.4.refs_3_
  38.8 1.4 %collective-permute-start.7 = (f32[640,1024]{1,0:T(8,128)S(1)}, f32[640,1024]{1,0:T(8,128)S(1)}, u32[]{:S(2)}, u32[]{:S(2)}) collective-permute-start(f32[640,1024]{1,0:T(8,128)S(1)} %collective-permute-done.4.refs_3_), channel_id=1, source_target_pairs={{0,1},{1,0},{2,3},{3,2},{4,5},{5,4},{6,7},{7,6},{8,9},{9,8},{10,11... | collective-permute-start | bytes 7864328 | tf_op jit(solution)/shard_map/ppermute | solution.py:46
  40.2 0.1 slice.47
  40.3 3.0 %collective-permute-start.10 = (f32[320,1024]{1,0:T(8,128)S(1)}, f32[320,1024]{1,0:T(8,128)S(1)}, u32[]{:S(2)}, u32[]{:S(2)}) collective-permute-start(f32[320,1024]{1,0:T(8,128)S(1)} %slice.47), channel_id=1, source_target_pairs={{0,18},{1,3},{2,16},{3,1},{16,2},{17,19},{18,0},{19,17},{4,22},{5,... | collective-permute-start | bytes 3932168 | tf_op jit(solution)/shard_map/ppermute | solution.py:42
  43.4 3.1 %collective-permute-start.8 = (f32[128,1024]{1,0:T(8,128)S(1)}, f32[128,1024]{1,0:T(8,128)S(1)}, u32[]{:S(2)}, u32[]{:S(2)}) collective-permute-start(f32[128,1024]{1,0:T(8,128)S(1)} %slice.45), channel_id=1, source_target_pairs={{0,12},{1,33},{2,14},{3,35},{16,28},{17,49},{18,30},{19,51},{4,8},... | collective-permute-start | bytes 1572872 | tf_op jit(solution)/shard_map/ppermute | solution.py:42
  46.6 0.4 collective-permute-start.9
  46.9 3.5 %shard_map.38 = (f32[256,1024]{1,0:T(8,128)S(1)}, f32[256,128]{1,0:T(8,128)S(1)}, f32[256,1024]{1,0:T(8,128)S(1)}, f32[256,128]{1,0:T(8,128)S(1)}, f32[256,1024]{1,0:T(8,128)S(1)}, /*index=5*/f32[256,128]{1,0:T(8,128)S(1)}) custom-call(f32[256,1024]{1,0:T(8,128)S(1)} %pad_maximum_fusion.2.refs_0_, f32[256,1024]{1,0:T(8,128)S(1)} %collective-permute-done.5.refs_1_.refs_0_, ...), custom_call_target="tpu_custom_call" | custom-call | flops 2415919104 | bytes 5767168 | tf_op jit(solution)/shard_map/pallas_call | solution.py:143
  50.5 0.0 collective-permute-done.7.refs_4_
  50.5 5.9 %shard_map.39 = (f32[256,1024]{1,0:T(8,128)S(1)}, f32[256,128]{1,0:T(8,128)S(1)}, f32[256,1024]{1,0:T(8,128)S(1)}, f32[256,128]{1,0:T(8,128)S(1)}, f32[256,1024]{1,0:T(8,128)S(1)}, /*index=5*/f32[256,128]{1,0:T(8,128)S(1)}) custom-call(f32[256,1024]{1,0:T(8,128)S(1)} %pad_maximum_fusion.2.re, ...), custom_call_target="tpu_custom_call", output_to_operand_aliasing={{0}: (5, {}), {1}: (6, {}), {2}: (7, {}), {3}: (8, {}), {4}... | custom-call | flops 4831838208 | bytes 8388608 | tf_op jit(solution)/shard_map/pallas_call | solution.py:143
  56.5 0.0 collective-permute-done.8.refs_0_.refs_2_
  56.5 0.0 collective-permute-done.9.refs_1_.refs_3_
  56.5 3.3 %shard_map.40 = (f32[256,1024]{1,0:T(8,128)S(1)}, f32[256,128]{1,0:T(8,128)S(1)}) custom-call(f32[128,1024]{1,0:T(8,128)S(1)} %collective-permute-done.8.refs_0_.refs_2_, f32[128,1024]{1,0:T(8,128)S(1)} %collective-permute-done.9.refs_1_.refs_3_, f32[640,1024]{1,0:T(8,128)S(1)} %pad_maximum_fusion.refs_3_.refs_2_, ...), custom_call_target="tpu_custom_call" | custom-call | flops 2415919104 | bytes 11010048 | tf_op jit(solution)/shard_map/pallas_call | solution.py:143
  59.8 0.0 collective-permute-done.10.refs_4_.refs_1_
  59.8 0.3 collective-permute-start.11
  60.1 2.5 %shard_map.41 = (f32[256,1024]{1,0:T(8,128)S(1)}, f32[256,128]{1,0:T(8,128)S(1)}, f32[256,1024]{1,0:T(8,128)S(1)}, f32[256,128]{1,0:T(8,128)S(1)}, f32[256,1024]{1,0:T(8,128)S(1)}, /*index=5*/f32[256,128]{1,0:T(8,128)S(1)}) custom-call(f32[256,1024]{1,0:T(8,128)S(1)} %collective-permute-done, ...), custom_call_target="tpu_custom_call", output_to_operand_aliasing={{0}: (5, {}), {1}: (6, {}), {2}: (7, {}), {3}: (8, {}), {4}... | custom-call | flops 1207959552 | bytes 4456448 | tf_op jit(solution)/shard_map/pallas_call | solution.py:143
  62.6 0.5 collective-permute-done.11.refs_2_
  63.1 0.9 shard_map.42
  64.0 2.2 %collective-permute-start.12 = (f32[128,1024]{1,0:T(8,128)S(1)}, f32[128,1024]{1,0:T(8,128)S(1)}, u32[]{:S(2)}, u32[]{:S(2)}) collective-permute-start(f32[128,1024]{1,0:T(8,128)S(1)} %get-tuple-element.81), channel_id=1, source_target_pairs={{0,12},{1,33},{2,14},{3,35},{16,28},{17,49},{18,30},{19,51},{4,8},... | collective-permute-start | bytes 1572872 | tf_op jit(solution)/shard_map/ppermute | solution.py:42
  66.3 0.1 collective-permute-start.13
  66.4 1.7 %shard_map.44 = (f32[256,1024]{1,0:T(8,128)S(1)}, f32[256,1024]{1,0:T(8,128)S(1)}) custom-call(f32[256,1024]{1,0:T(8,128)S(1)} %collective-permute-done.5.refs_1_.refs_0_, f32[256,1024]{1,0:T(8,128)S(1)} %collective-permute-done.6.refs_2_.refs_1_, f32[320,1024]{1,0:T(8,128)S(1)} %collective-permute-done.11.refs_2_, ...), custom_call_target="tpu_custom_call" | custom-call | flops 805306368 | bytes 4456448 | tf_op jit(solution)/shard_map/pallas_call | solution.py:143
  68.2 2.3 %collective-permute-start.14 = (f32[144,1024]{1,0:T(8,128)S(1)}, f32[144,1024]{1,0:T(8,128)S(1)}, u32[]{:S(2)}, u32[]{:S(2)}) collective-permute-start(f32[144,1024]{1,0:T(8,128)S(1)} %slice.48), channel_id=1, source_target_pairs={{0,12},{1,33},{2,14},{3,35},{16,28},{17,49},{18,30},{19,51},{4,8},... | collective-permute-start | bytes 1769480 | tf_op jit(solution)/shard_map/ppermute | solution.py:42
  70.6 0.2 collective-permute-start.15
  70.8 1.4 %shard_map.43 = f32[256,1024]{1,0:T(8,128)S(1)} custom-call(f32[256,1024]{1,0:T(8,128)S(1)} %pad_maximum_fusion.2.refs_0_, f32[320,1024]{1,0:T(8,128)S(1)} %collective-permute-done.10.refs_4_.refs_1_, f32[320,1024]{1,0:T(8,128)S(1)} %collective-permute-done.11.refs_2_, f32[256,1024]{1,0:T(8,128)S(1)} %get-tuple-element.83.refs_3_, ...), custom_call_target="tpu_custom_call" | custom-call | flops 805306368 | bytes 5767168 | tf_op jit(solution)/shard_map/pallas_call | solution.py:143
  72.2 2.3 %collective-permute-done.12 = f32[128,1024]{1,0:T(8,128)S(1)} collective-permute-done((f32[128,1024]{1,0:T(8,128)S(1)}, f32[128,1024]{1,0:T(8,128)S(1)}, u32[]{:S(2)}, u32[]{:S(2)}) %collective-permute-start.12) | collective-permute-done | bytes 524320 | tf_op jit(solution)/shard_map/ppermute | solution.py:42
  74.5 1.0 collective-permute-done.13
  75.5 0.1 slice_add_fusion.2
  75.5 1.3 %collective-permute-start.17 = (f32[128,1024]{1,0:T(8,128)S(1)}, f32[128,1024]{1,0:T(8,128)S(1)}, u32[]{:S(2)}, u32[]{:S(2)}) collective-permute-start(f32[128,1024]{1,0:T(8,128)S(1)} %slice_add_fusion.2), channel_id=1, source_target_pairs={{0,12},{1,33},{2,14},{3,35},{16,28},{17,49},{18,30},{19,51},{4,8},... | collective-permute-start | bytes 1572872 | tf_op jit(solution)/shard_map/ppermute | solution.py:42
  76.8 0.1 slice_add_fusion.3
  76.9 0.6 collective-permute-start.16
  77.5 3.3 %collective-permute-done.14 = f32[144,1024]{1,0:T(8,128)S(1)} collective-permute-done((f32[144,1024]{1,0:T(8,128)S(1)}, f32[144,1024]{1,0:T(8,128)S(1)}, u32[]{:S(2)}, u32[]{:S(2)}) %collective-permute-start.14) | collective-permute-done | bytes 589856 | tf_op jit(solution)/shard_map/ppermute | solution.py:42
  80.9 0.9 collective-permute-done.15
  81.8 0.2 maximum_add_fusion
  82.0 4.4 %collective-permute-done.17 = f32[128,1024]{1,0:T(8,128)S(1)} collective-permute-done((f32[128,1024]{1,0:T(8,128)S(1)}, f32[128,1024]{1,0:T(8,128)S(1)}, u32[]{:S(2)}, u32[]{:S(2)}) %collective-permute-start.17) | collective-permute-done | bytes 524320 | tf_op jit(solution)/shard_map/ppermute | solution.py:42
  86.5 1.0 collective-permute-done.16
  87.4 0.1 slice_add_fusion
  87.6 3.1 %collective-permute-start.19 = (f32[64,1024]{1,0:T(8,128)S(1)}, f32[64,1024]{1,0:T(8,128)S(1)}, u32[]{:S(2)}, u32[]{:S(2)}) collective-permute-start(f32[64,1024]{1,0:T(8,128)S(1)} %get-tuple-element.100), channel_id=1, source_target_pairs={{0,64},{1,9},{2,66},{3,11},{16,80},{17,25},{18,82},{19,27},{4,68},... | collective-permute-start | bytes 786440 | tf_op jit(solution)/shard_map/ppermute | solution.py:42
  90.7 1.1 %collective-permute-start.20 = (f32[64,1024]{1,0:T(8,128)S(1)}, f32[64,1024]{1,0:T(8,128)S(1)}, u32[]{:S(2)}, u32[]{:S(2)}) collective-permute-start(f32[64,1024]{1,0:T(8,128)S(1)} %get-tuple-element.99), channel_id=1, source_target_pairs={{0,96},{1,5},{2,98},{3,7},{16,112},{17,21},{18,114},{19,23},{4,100... | collective-permute-start | bytes 786440 | tf_op jit(solution)/shard_map/ppermute | solution.py:42
  91.9 0.1 collective-permute-start.18
  92.0 3.6 %collective-permute-done.19 = f32[64,1024]{1,0:T(8,128)S(1)} collective-permute-done((f32[64,1024]{1,0:T(8,128)S(1)}, f32[64,1024]{1,0:T(8,128)S(1)}, u32[]{:S(2)}, u32[]{:S(2)}) %collective-permute-start.19) | collective-permute-done | bytes 262176 | tf_op jit(solution)/shard_map/ppermute | solution.py:42
  95.6 2.8 %collective-permute-done.20 = f32[64,1024]{1,0:T(8,128)S(1)} collective-permute-done((f32[64,1024]{1,0:T(8,128)S(1)}, f32[64,1024]{1,0:T(8,128)S(1)}, u32[]{:S(2)}, u32[]{:S(2)}) %collective-permute-start.20) | collective-permute-done | bytes 262176 | tf_op jit(solution)/shard_map/ppermute | solution.py:42
  98.4 0.1 collective-permute-done.18
  98.5 0.8 fusion
  (9 shorter events, 0.3 us)
Async XLA Ops:
  0.0 2.5 %copy-start = (f32[512,1024]{1,0:T(8,128)S(1)}, f32[512,1024]{1,0:T(8,128)}, u32[]{:S(2)}) copy-start(f32[512,1024]{1,0:T(8,128)} %param.4) | copy-start | bytes 6291460
  2.5 1.1 %copy-start.1 = (f32[64,1024]{1,0:T(8,128)S(1)}, f32[64,1024]{1,0:T(8,128)}, u32[]{:S(2)}) copy-start(f32[64,1024]{1,0:T(8,128)} %shard_map.37) | copy-start | bytes 786436
  3.7 3.1 %collective-permute-start.3 = (f32[320,1024]{1,0:T(8,128)S(1)}, f32[320,1024]{1,0:T(8,128)S(1)}, u32[]{:S(2)}, u32[]{:S(2)}) collective-permute-start(f32[320,1024]{1,0:T(8,128)S(1)} %pad_maximum_fusion.1), channel_id=1, source_target_pairs={{0,1},{1,0},{2,3},{3,2},{4,5},{5,4},{6,7},{7,6},{8,9},{9,8},{10,11... | collective-permute-start | bytes 3932168 | tf_op jit(solution)/shard_map/ppermute | solution.py:46
  7.1 31.7 %collective-permute-start.4 = (f32[640,1024]{1,0:T(8,128)S(1)}, f32[640,1024]{1,0:T(8,128)S(1)}, u32[]{:S(2)}, u32[]{:S(2)}) collective-permute-start(f32[640,1024]{1,0:T(8,128)S(1)} %pad_maximum_fusion.refs_3_.refs_2_), channel_id=1, source_target_pairs={{0,2},{1,19},{2,0},{3,17},{16,18},{17,3},{18,16},{19,1},{4,6},{5,2... | collective-permute-start | bytes 7864328 | tf_op jit(solution)/shard_map/ppermute | solution.py:42
  9.2 6.4 %collective-permute-start = (f32[64,1024]{1,0:T(8,128)S(1)}, f32[64,1024]{1,0:T(8,128)S(1)}, u32[]{:S(2)}, u32[]{:S(2)}) collective-permute-start(f32[64,1024]{1,0:T(8,128)S(1)} %copy-done.1), channel_id=1, source_target_pairs={{0,32},{1,13},{2,34},{3,15},{16,48},{17,29},{18,50},{19,31},{4,36}... | collective-permute-start | bytes 786440 | tf_op jit(solution)/shard_map/ppermute | solution.py:42
  10.7 10.4 %collective-permute-start.1 = (f32[64,1024]{1,0:T(8,128)S(1)}, f32[64,1024]{1,0:T(8,128)S(1)}, u32[]{:S(2)}, u32[]{:S(2)}) collective-permute-start(f32[64,1024]{1,0:T(8,128)S(1)} %copy-done.1), channel_id=1, source_target_pairs={{0,96},{1,5},{2,98},{3,7},{16,112},{17,21},{18,114},{19,23},{4,100... | collective-permute-start | bytes 786440 | tf_op jit(solution)/shard_map/ppermute | solution.py:42
  12.8 8.3 %collective-permute-start.2 = (f32[64,1024]{1,0:T(8,128)S(1)}, f32[64,1024]{1,0:T(8,128)S(1)}, u32[]{:S(2)}, u32[]{:S(2)}) collective-permute-start(f32[64,1024]{1,0:T(8,128)S(1)} %copy-done.1), channel_id=1, source_target_pairs={{0,64},{1,9},{2,66},{3,11},{16,80},{17,25},{18,82},{19,27},{4,68},... | collective-permute-start | bytes 786440 | tf_op jit(solution)/shard_map/ppermute | solution.py:42
  21.2 14.9 %collective-permute-start.5 = (f32[256,1024]{1,0:T(8,128)S(1)}, f32[256,1024]{1,0:T(8,128)S(1)}, u32[]{:S(2)}, u32[]{:S(2)}) collective-permute-start(f32[256,1024]{1,0:T(8,128)S(1)} %pad_maximum_fusion.2.refs_0_), channel_id=1, source_target_pairs={{0,4},{1,97},{2,6},{3,99},{16,20},{17,113},{18,22},{19,115},{4,0},... | collective-permute-start | bytes 3145736 | tf_op jit(solution)/shard_map/ppermute | solution.py:42
  22.8 16.0 %collective-permute-start.6 = (f32[256,1024]{1,0:T(8,128)S(1)}, f32[256,1024]{1,0:T(8,128)S(1)}, u32[]{:S(2)}, u32[]{:S(2)}) collective-permute-start(f32[256,1024]{1,0:T(8,128)S(1)} %pad_maximum_fusion.2.refs_0_), channel_id=1, source_target_pairs={{0,12},{1,33},{2,14},{3,35},{16,28},{17,49},{18,30},{19,51},{4,8},... | collective-permute-start | bytes 3145736 | tf_op jit(solution)/shard_map/ppermute | solution.py:42
  38.8 11.7 %collective-permute-start.7 = (f32[640,1024]{1,0:T(8,128)S(1)}, f32[640,1024]{1,0:T(8,128)S(1)}, u32[]{:S(2)}, u32[]{:S(2)}) collective-permute-start(f32[640,1024]{1,0:T(8,128)S(1)} %collective-permute-done.4.refs_3_), channel_id=1, source_target_pairs={{0,1},{1,0},{2,3},{3,2},{4,5},{5,4},{6,7},{7,6},{8,9},{9,8},{10,11... | collective-permute-start | bytes 7864328 | tf_op jit(solution)/shard_map/ppermute | solution.py:46
  40.3 19.4 %collective-permute-start.10 = (f32[320,1024]{1,0:T(8,128)S(1)}, f32[320,1024]{1,0:T(8,128)S(1)}, u32[]{:S(2)}, u32[]{:S(2)}) collective-permute-start(f32[320,1024]{1,0:T(8,128)S(1)} %slice.47), channel_id=1, source_target_pairs={{0,18},{1,3},{2,16},{3,1},{16,2},{17,19},{18,0},{19,17},{4,22},{5,... | collective-permute-start | bytes 3932168 | tf_op jit(solution)/shard_map/ppermute | solution.py:42
  43.4 13.1 %collective-permute-start.8 = (f32[128,1024]{1,0:T(8,128)S(1)}, f32[128,1024]{1,0:T(8,128)S(1)}, u32[]{:S(2)}, u32[]{:S(2)}) collective-permute-start(f32[128,1024]{1,0:T(8,128)S(1)} %slice.45), channel_id=1, source_target_pairs={{0,12},{1,33},{2,14},{3,35},{16,28},{17,49},{18,30},{19,51},{4,8},... | collective-permute-start | bytes 1572872 | tf_op jit(solution)/shard_map/ppermute | solution.py:42
  46.6 9.9 %collective-permute-start.9 = (f32[128,1024]{1,0:T(8,128)S(1)}, f32[128,1024]{1,0:T(8,128)S(1)}, u32[]{:S(2)}, u32[]{:S(2)}) collective-permute-start(f32[128,1024]{1,0:T(8,128)S(1)} %slice.46), channel_id=1, source_target_pairs={{0,4},{1,97},{2,6},{3,99},{16,20},{17,113},{18,22},{19,115},{4,0},... | collective-permute-start | bytes 1572872 | tf_op jit(solution)/shard_map/ppermute | solution.py:42
  59.8 3.3 %collective-permute-start.11 = (f32[320,1024]{1,0:T(8,128)S(1)}, f32[320,1024]{1,0:T(8,128)S(1)}, u32[]{:S(2)}, u32[]{:S(2)}) collective-permute-start(f32[320,1024]{1,0:T(8,128)S(1)} %collective-permute-done.10.refs_4_.refs_1_), channel_id=1, source_target_pairs={{0,1},{1,0},{2,3},{3,2},{4,5},{5,4},{6,7},{7,6},{8,9},{9,8},{10,11... | collective-permute-start | bytes 3932168 | tf_op jit(solution)/shard_map/ppermute | solution.py:46
  64.0 10.5 %collective-permute-start.12 = (f32[128,1024]{1,0:T(8,128)S(1)}, f32[128,1024]{1,0:T(8,128)S(1)}, u32[]{:S(2)}, u32[]{:S(2)}) collective-permute-start(f32[128,1024]{1,0:T(8,128)S(1)} %get-tuple-element.81), channel_id=1, source_target_pairs={{0,12},{1,33},{2,14},{3,35},{16,28},{17,49},{18,30},{19,51},{4,8},... | collective-permute-start | bytes 1572872 | tf_op jit(solution)/shard_map/ppermute | solution.py:42
  66.3 9.2 %collective-permute-start.13 = (f32[128,1024]{1,0:T(8,128)S(1)}, f32[128,1024]{1,0:T(8,128)S(1)}, u32[]{:S(2)}, u32[]{:S(2)}) collective-permute-start(f32[128,1024]{1,0:T(8,128)S(1)} %get-tuple-element.82), channel_id=1, source_target_pairs={{0,4},{1,97},{2,6},{3,99},{16,20},{17,113},{18,22},{19,115},{4,0},... | collective-permute-start | bytes 1572872 | tf_op jit(solution)/shard_map/ppermute | solution.py:42
  68.2 12.6 %collective-permute-start.14 = (f32[144,1024]{1,0:T(8,128)S(1)}, f32[144,1024]{1,0:T(8,128)S(1)}, u32[]{:S(2)}, u32[]{:S(2)}) collective-permute-start(f32[144,1024]{1,0:T(8,128)S(1)} %slice.48), channel_id=1, source_target_pairs={{0,12},{1,33},{2,14},{3,35},{16,28},{17,49},{18,30},{19,51},{4,8},... | collective-permute-start | bytes 1769480 | tf_op jit(solution)/shard_map/ppermute | solution.py:42
  70.6 11.2 %collective-permute-start.15 = (f32[144,1024]{1,0:T(8,128)S(1)}, f32[144,1024]{1,0:T(8,128)S(1)}, u32[]{:S(2)}, u32[]{:S(2)}) collective-permute-start(f32[144,1024]{1,0:T(8,128)S(1)} %slice.50), channel_id=1, source_target_pairs={{0,4},{1,97},{2,6},{3,99},{16,20},{17,113},{18,22},{19,115},{4,0},... | collective-permute-start | bytes 1769480 | tf_op jit(solution)/shard_map/ppermute | solution.py:42
  75.5 10.9 %collective-permute-start.17 = (f32[128,1024]{1,0:T(8,128)S(1)}, f32[128,1024]{1,0:T(8,128)S(1)}, u32[]{:S(2)}, u32[]{:S(2)}) collective-permute-start(f32[128,1024]{1,0:T(8,128)S(1)} %slice_add_fusion.2), channel_id=1, source_target_pairs={{0,12},{1,33},{2,14},{3,35},{16,28},{17,49},{18,30},{19,51},{4,8},... | collective-permute-start | bytes 1572872 | tf_op jit(solution)/shard_map/ppermute | solution.py:42
  76.9 10.5 %collective-permute-start.16 = (f32[128,1024]{1,0:T(8,128)S(1)}, f32[128,1024]{1,0:T(8,128)S(1)}, u32[]{:S(2)}, u32[]{:S(2)}) collective-permute-start(f32[128,1024]{1,0:T(8,128)S(1)} %slice_add_fusion.3), channel_id=1, source_target_pairs={{0,4},{1,97},{2,6},{3,99},{16,20},{17,113},{18,22},{19,115},{4,0},... | collective-permute-start | bytes 1572872 | tf_op jit(solution)/shard_map/ppermute | solution.py:42
  87.6 8.0 %collective-permute-start.19 = (f32[64,1024]{1,0:T(8,128)S(1)}, f32[64,1024]{1,0:T(8,128)S(1)}, u32[]{:S(2)}, u32[]{:S(2)}) collective-permute-start(f32[64,1024]{1,0:T(8,128)S(1)} %get-tuple-element.100), channel_id=1, source_target_pairs={{0,64},{1,9},{2,66},{3,11},{16,80},{17,25},{18,82},{19,27},{4,68},... | collective-permute-start | bytes 786440 | tf_op jit(solution)/shard_map/ppermute | solution.py:42
  90.7 7.7 %collective-permute-start.20 = (f32[64,1024]{1,0:T(8,128)S(1)}, f32[64,1024]{1,0:T(8,128)S(1)}, u32[]{:S(2)}, u32[]{:S(2)}) collective-permute-start(f32[64,1024]{1,0:T(8,128)S(1)} %get-tuple-element.99), channel_id=1, source_target_pairs={{0,96},{1,5},{2,98},{3,7},{16,112},{17,21},{18,114},{19,23},{4,100... | collective-permute-start | bytes 786440 | tf_op jit(solution)/shard_map/ppermute | solution.py:42
  91.9 6.6 %collective-permute-start.18 = (f32[64,1024]{1,0:T(8,128)S(1)}, f32[64,1024]{1,0:T(8,128)S(1)}, u32[]{:S(2)}, u32[]{:S(2)}) collective-permute-start(f32[64,1024]{1,0:T(8,128)S(1)} %slice.65), channel_id=1, source_target_pairs={{0,32},{1,13},{2,34},{3,15},{16,48},{17,29},{18,50},{19,31},{4,36}... | collective-permute-start | bytes 786440 | tf_op jit(solution)/shard_map/ppermute | solution.py:42

commit v4 on v3

--- a/solution.py
+++ b/solution.py
@@ -190,27 +190,32 @@
     generated = resident(generated)
     real = real_bank.at[subset_rows].get(mode="promise_in_bounds", wrap_negative_indices=False)
     own = jnp.concatenate([generated, real], axis=0)
-    own_two = jnp.concatenate([own, swap(own)], axis=0)
+    own_swapped = swap(own)
     count = own.shape[0]
     add = functools.partial(pairs, block=count, span=n, scale=scale)
-    x_near = move(own_two, "zz", "near")
+    x_near = move(own, "zz", "near")
+    x_far = move(own, "zz", "far")
+    x_both = move(x_near, "zz", "far")
 
     line = [generated] + [move(generated, "xy", step) for step in ("near", "far", "both")]
     line = jnp.concatenate(line, axis=0)
     half = 2 * n
     line_near, line_far = move(line, "yx", "near"), move(line, "yx", "far")
-    x_near, line_near, line_far = lax.optimization_barrier((x_near, line_near, line_far))
-    x_both = move(x_near[:count], "zz", "far")
-    x_far = swap(x_near)
     both = [move(line_near[:half], "yx", "far"), move(line_far[half:], "yx", "near")]
     rows = [[line], [line_near], [line_far], both]
     s = [None] * SIDE
-    s[:3] = add(rows[:3], [own_two], states=s[:3], last=None)
-    x_far, _ = lax.optimization_barrier((x_far, s[:3]))
-    s[:3] = add(rows[:3], [x_near, x_far], states=s[:3], last=None)
+    s[:3] = add(rows[:3], [own, own_swapped], states=s[:3], last=None)
+    x_near_swapped = swap(after(x_near, line_near, line_far))
+    x_far, x_near_swapped, _ = lax.optimization_barrier((x_far, x_near_swapped, s[:3]))
+    cuts = [0, 160, 320]
+    x_far_swapped = tuple(swap(x_far[a:b]) for a, b in zip(cuts, cuts[1:]))
+    s[:3] = add(rows[:3], [x_near, x_near_swapped], states=s[:3], last=None)
     both, _ = lax.optimization_barrier((both, s[:3]))
     rows[3] = both
-    s[3:] = add(rows[3:], [own_two, x_near, x_far], states=s[3:], last=None)
+    s[3:] = add(rows[3:], [own, own_swapped, x_near, x_near_swapped], states=s[3:], last=None)
+    x_far_swapped, _ = lax.optimization_barrier((x_far_swapped, s))
+    x_far_swapped = jnp.concatenate(x_far_swapped, axis=0)
+    s = add(rows, [x_far, x_far_swapped], states=s, last=None)
     x_both, _ = lax.optimization_barrier((x_both, s))
     both_swapped = swap(x_both)
     s[1:] = add(rows[1:], [x_both], states=s[1:], last=None)

time: 99.4 us -> 94.8 us (0.954)
  waiting for transfers between devices: 44.4 us -> 33.2 us
  starting transfers between devices: 29.5 us -> 33.1 us
  Pallas kernels: 21.2 us -> 23.1 us
  other arithmetic: 2.34 us -> 3.35 us
    ppermute x18 -> x19, waiting for transfers between devices: 40.9 us -> 32.9 us  [move(): return lax.ppermute(v, AXES, STEPS[axes, step])]
    ppermute x18 -> x19, starting transfers between devices: 27.8 us -> 32 us  [move(): return lax.ppermute(v, AXES, STEPS[axes, step])]
    ppermute x3 -> x5, waiting for transfers between devices: 3.52 us -> 0.26 us  [swap(): return lax.ppermute(v, AXES, SWAP)]
    pallas_call x7 -> x8, Pallas kernels: 19.4 us -> 21.3 us  [pairs(): pl.pallas_call(functools.partial(pair_kernel, [len(batch) for batch in ro...]
    concatenate x1, other arithmetic: 0.1 us -> 1.21 us  [on_device(): line = jnp.concatenate(line, axis=0)]
  transfers between devices with their start and end apart: 21 -> 24, of which waited for: 15 -> 13; matrix products, arithmetic and copies ran while one was open for 1% -> 4% of each run, Pallas kernels for 19% -> 22%
where the time goes in v4:
time: 94.8 us; the launch traced here: 94.6 us
  waiting for transfers between devices  33.2 us (35%)
  starting transfers between devices  33.1 us (35%)
  Pallas kernels  23.1 us (24%)
  other arithmetic  3.35 us (4%)
  local copies, waits for them, and re-layouts  1.52 us (2%)
    ppermute x19, waiting for transfers between devices, move(): return lax.ppermute(v, AXES, STEPS[axes, step])  32.9 us
    ppermute x19, starting transfers between devices, move(): return lax.ppermute(v, AXES, STEPS[axes, step])  32 us
    pallas_call x8, Pallas kernels, pairs(): pl.pallas_call(functools.partial(pair_kernel, [len(batch) for batch in ro...  21.3 us
  transfers between devices with their start and end apart: 24, of which 13 were waited for; matrix products, arithmetic and copies ran while one was open for 4% of the time, Pallas kernels for 22%

profile of v4, /device:TPU:0, one launch (start us, length us, event | category | flops | bytes accessed | tf_op | source)
XLA Modules:
  0.0 94.6 jit_solution(16255319205913116354)
XLA Ops:
  0.0 1.8 %shard_map.37 = f32[64,1024]{1,0:T(8,128)} custom-call(f32[64,1024]{1,0:T(8,128)} %v_ref.1), custom_call_target="tpu_custom_call" | custom-call | tf_op jit(solution)/shard_map/pallas_call | solution.py:176
  1.8 1.6 %collective-permute-start = (f32[64,1024]{1,0:T(8,128)}, f32[64,1024]{1,0:T(8,128)}, u32[]{:S(2)}, u32[]{:S(2)}) collective-permute-start(f32[64,1024]{1,0:T(8,128)} %shard_map.37), channel_id=1, source_target_pairs={{0,32},{1,13},{2,34},{3,15},{16,48},{17,29},{18,50},{19,31},{4,36}... | collective-permute-start | bytes 786440 | tf_op jit(solution)/shard_map/ppermute | solution.py:42
  3.4 2.1 %collective-permute-start.1 = (f32[64,1024]{1,0:T(8,128)}, f32[64,1024]{1,0:T(8,128)}, u32[]{:S(2)}, u32[]{:S(2)}) collective-permute-start(f32[64,1024]{1,0:T(8,128)} %shard_map.37), channel_id=1, source_target_pairs={{0,96},{1,5},{2,98},{3,7},{16,112},{17,21},{18,114},{19,23},{4,100... | collective-permute-start | bytes 786440 | tf_op jit(solution)/shard_map/ppermute | solution.py:42
  5.5 0.6 collective-permute-start.2
  6.1 0.7 pad_clamp_fusion
  6.8 1.1 %gather_fusion = f32[256,1024]{1,0:T(8,128)S(1)} fusion(f32[512,1024]{1,0:T(8,128)S(1)} %copy-done, s32[1024]{0:T(1024)S(1)} %pad_clamp_fusion), kind=kCustom, calls=%fused_computation | custom fusion | bytes 2098176 | tf_op jit(solution)/shard_map/gather | solution.py:191
  7.9 0.1 pad_maximum_fusion.refs_3_.refs_2_
  8.0 2.0 %collective-permute-start.7 = (f32[320,1024]{1,0:T(8,128)S(1)}, f32[320,1024]{1,0:T(8,128)S(1)}, u32[]{:S(2)}, u32[]{:S(2)}) collective-permute-start(f32[320,1024]{1,0:T(8,128)S(1)} %pad_maximum_fusion.refs_3_.refs_2_), channel_id=1, source_target_pairs={{0,2},{1,19},{2,0},{3,17},{16,18},{17,3},{18,16},{19,1},{4,6},{5,2... | collective-permute-start | bytes 3932168 | tf_op jit(solution)/shard_map/ppermute | solution.py:42
  10.0 4.1 %collective-permute-done.1 = f32[64,1024]{1,0:T(8,128)} collective-permute-done((f32[64,1024]{1,0:T(8,128)}, f32[64,1024]{1,0:T(8,128)}, u32[]{:S(2)}, u32[]{:S(2)}) %collective-permute-start.1) | collective-permute-done | bytes 262176 | tf_op jit(solution)/shard_map/ppermute | solution.py:42
  14.1 0.0 collective-permute-done.2
  14.1 1.2 %pad_maximum_fusion.2.refs_0_ = f32[256,1024]{1,0:T(8,128)S(1)} fusion(f32[64,1024]{1,0:T(8,128)} %collective-permute-done.2, f32[64,1024]{1,0:T(8,128)} %collective-permute-done.1, f32[64,1024]{1,0:T(8,128)} %collective-permute-done, f32[64,1024]{1,0:T(8,128)S(1)} %copy-done.1), kind=kLoop, calls=%fused_computation.3 | loop fusion | flops 786432 | bytes 2097152 | tf_op jit(solution)/shard_map/concatenate | solution.py:201
  15.3 1.7 %collective-permute-start.3 = (f32[256,1024]{1,0:T(8,128)S(1)}, f32[256,1024]{1,0:T(8,128)S(1)}, u32[]{:S(2)}, u32[]{:S(2)}) collective-permute-start(f32[256,1024]{1,0:T(8,128)S(1)} %pad_maximum_fusion.2.refs_0_), channel_id=1, source_target_pairs={{0,4},{1,97},{2,6},{3,99},{16,20},{17,113},{18,22},{19,115},{4,0},... | collective-permute-start | bytes 3145736 | tf_op jit(solution)/shard_map/ppermute | solution.py:42
  17.0 2.2 %collective-permute-start.4 = (f32[256,1024]{1,0:T(8,128)S(1)}, f32[256,1024]{1,0:T(8,128)S(1)}, u32[]{:S(2)}, u32[]{:S(2)}) collective-permute-start(f32[256,1024]{1,0:T(8,128)S(1)} %pad_maximum_fusion.2.refs_0_), channel_id=1, source_target_pairs={{0,12},{1,33},{2,14},{3,35},{16,28},{17,49},{18,30},{19,51},{4,8},... | collective-permute-start | bytes 3145736 | tf_op jit(solution)/shard_map/ppermute | solution.py:42
  19.2 0.0 collective-permute-start.10
  19.2 4.0 %collective-permute-start.8 = (f32[320,1024]{1,0:T(8,128)S(1)}, f32[320,1024]{1,0:T(8,128)S(1)}, u32[]{:S(2)}, u32[]{:S(2)}) collective-permute-start(f32[320,1024]{1,0:T(8,128)S(1)} %pad_maximum_fusion.refs_3_.refs_2_), channel_id=1, source_target_pairs={{0,18},{1,3},{2,16},{3,1},{16,2},{17,19},{18,0},{19,17},{4,22},{5,... | collective-permute-start | bytes 3932168 | tf_op jit(solution)/shard_map/ppermute | solution.py:42
  23.2 7.0 %collective-permute-done.3.refs_1_.refs_0_ = f32[256,1024]{1,0:T(8,128)S(1)} collective-permute-done((f32[256,1024]{1,0:T(8,128)S(1)}, f32[256,1024]{1,0:T(8,128)S(1)}, u32[]{:S(2)}, u32[]{:S(2)}) %collective-permute-start.3) | collective-permute-done | bytes 1048608 | tf_op jit(solution)/shard_map/ppermute | solution.py:42
  30.2 2.8 %collective-permute-done.4.refs_2_.refs_1_ = f32[256,1024]{1,0:T(8,128)S(1)} collective-permute-done((f32[256,1024]{1,0:T(8,128)S(1)}, f32[256,1024]{1,0:T(8,128)S(1)}, u32[]{:S(2)}, u32[]{:S(2)}) %collective-permute-start.4) | collective-permute-done | bytes 1048608 | tf_op jit(solution)/shard_map/ppermute | solution.py:42
  33.0 0.0 collective-permute-done.7.refs_3_.refs_4_
  33.0 0.0 collective-permute-start.9
  33.0 2.3 %collective-permute-start.5 = (f32[128,1024]{1,0:T(8,128)S(1)}, f32[128,1024]{1,0:T(8,128)S(1)}, u32[]{:S(2)}, u32[]{:S(2)}) collective-permute-start(f32[128,1024]{1,0:T(8,128)S(1)} %slice.66), channel_id=1, source_target_pairs={{0,12},{1,33},{2,14},{3,35},{16,28},{17,49},{18,30},{19,51},{4,8},... | collective-permute-start | bytes 1572872 | tf_op jit(solution)/shard_map/ppermute | solution.py:42
  35.4 0.1 collective-permute-start.6
  35.4 0.0 collective-permute-done.10.refs_4_.refs_3_
  35.5 4.1 %collective-permute-start.13 = (f32[320,1024]{1,0:T(8,128)S(1)}, f32[320,1024]{1,0:T(8,128)S(1)}, u32[]{:S(2)}, u32[]{:S(2)}) collective-permute-start(f32[320,1024]{1,0:T(8,128)S(1)} %collective-permute-done.7.refs_3_.refs_4_), channel_id=1, source_target_pairs={{0,18},{1,3},{2,16},{3,1},{16,2},{17,19},{18,0},{19,17},{4,22},{5,... | collective-permute-start | bytes 3932168 | tf_op jit(solution)/shard_map/ppermute | solution.py:42
  39.6 3.5 %shard_map.38 = (f32[256,1024]{1,0:T(8,128)S(1)}, f32[256,128]{1,0:T(8,128)S(1)}, f32[256,1024]{1,0:T(8,128)S(1)}, f32[256,128]{1,0:T(8,128)S(1)}, f32[256,1024]{1,0:T(8,128)S(1)}, /*index=5*/f32[256,128]{1,0:T(8,128)S(1)}) custom-call(f32[256,1024]{1,0:T(8,128)S(1)} %pad_maximum_fusion.2.refs_0_, f32[256,1024]{1,0:T(8,128)S(1)} %collective-permute-done.3.refs_1_.refs_0_, ...), custom_call_target="tpu_custom_call" | custom-call | flops 2415919104 | bytes 5767168 | tf_op jit(solution)/shard_map/pallas_call | solution.py:143
  43.1 0.0 collective-permute-done.8.refs_5_
  43.1 0.1 fusion.1
  43.3 0.1 collective-permute-start.11
  43.4 0.5 collective-permute-start.12
  43.9 4.1 %shard_map.39 = (f32[256,1024]{1,0:T(8,128)S(1)}, f32[256,128]{1,0:T(8,128)S(1)}, f32[256,1024]{1,0:T(8,128)S(1)}, f32[256,128]{1,0:T(8,128)S(1)}, f32[256,1024]{1,0:T(8,128)S(1)}, /*index=5*/f32[256,128]{1,0:T(8,128)S(1)}) custom-call(f32[256,1024]{1,0:T(8,128)S(1)} %pad_maximum_fusion.2.re, ...), custom_call_target="tpu_custom_call", output_to_operand_aliasing={{0}: (5, {}), {1}: (6, {}), {2}: (7, {}), {3}: (8, {}), {4}... | custom-call | flops 2415919104 | bytes 5767168 | tf_op jit(solution)/shard_map/pallas_call | solution.py:143
  48.0 0.0 collective-permute-done.5.refs_0_.refs_3_.refs_2_
  48.0 0.0 collective-permute-done.6.refs_1_.refs_4_.refs_3_
  48.0 2.2 %shard_map.40 = (f32[256,1024]{1,0:T(8,128)S(1)}, f32[256,128]{1,0:T(8,128)S(1)}) custom-call(f32[128,1024]{1,0:T(8,128)S(1)} %collective-permute-done.5.refs_0_.refs_3_.refs_2_, f32[128,1024]{1,0:T(8,128)S(1)} %collective-permute-done.6.refs_1_.refs_4_.refs_3_, f32[320,1024]{1,0:T(8,128)S(1)} %pad_maximum_fusion.refs_3_.refs_2_, ...), custom_call_target="tpu_custom_call" | custom-call | flops 1610612736 | bytes 8388608 | tf_op jit(solution)/shard_map/pallas_call | solution.py:143
  50.2 0.0 collective-permute-done.12
  50.2 0.1 pad_maximum_fusion.1.refs_6_
  50.3 5.0 %shard_map.41 = (f32[256,1024]{1,0:T(8,128)S(1)}, f32[256,128]{1,0:T(8,128)S(1)}, f32[256,1024]{1,0:T(8,128)S(1)}, f32[256,128]{1,0:T(8,128)S(1)}, f32[256,1024]...) custom-call(f32[256,1024]{1,0:T(8,128)S(1)} %pad_maximum_fusion.2.re, ...), custom_call_target="tpu_custom_call", output_to_operand_aliasing={{0}: (7, {}), {1}: (8, {}), {2}: (9, {}), {3}: (10, {}), {4... | custom-call | flops 3221225472 | bytes 5767168 | tf_op jit(solution)/shard_map/pallas_call | solution.py:143
  55.3 0.6 collective-permute-start.14
  55.9 2.5 %shard_map.42 = (f32[256,1024]{1,0:T(8,128)S(1)}, f32[256,128]{1,0:T(8,128)S(1)}, f32[256,1024]{1,0:T(8,128)S(1)}, f32[256,128]{1,0:T(8,128)S(1)}, f32[256,1024]{1,0:T(8,128)S(1)}, /*index=5*/f32[256,128]{1,0:T(8,128)S(1)}) custom-call(f32[256,1024]{1,0:T(8,128)S(1)} %collective-permute-done, ...), custom_call_target="tpu_custom_call", output_to_operand_aliasing={{0}: (5, {}), {1}: (6, {}), {2}: (7, {}), {3}: (8, {}), {4}... | custom-call | flops 1207959552 | bytes 4456448 | tf_op jit(solution)/shard_map/pallas_call | solution.py:143
  58.4 0.2 collective-permute-done.14.refs_2_
  58.6 0.9 shard_map.43
  59.6 2.1 %collective-permute-start.15 = (f32[128,1024]{1,0:T(8,128)S(1)}, f32[128,1024]{1,0:T(8,128)S(1)}, u32[]{:S(2)}, u32[]{:S(2)}) collective-permute-start(f32[128,1024]{1,0:T(8,128)S(1)} %get-tuple-element.99), channel_id=1, source_target_pairs={{0,12},{1,33},{2,14},{3,35},{16,28},{17,49},{18,30},{19,51},{4,8},... | collective-permute-start | bytes 1572872 | tf_op jit(solution)/shard_map/ppermute | solution.py:42
  61.6 0.4 collective-permute-start.16
  62.0 1.7 %shard_map.45 = (f32[256,1024]{1,0:T(8,128)S(1)}, f32[256,1024]{1,0:T(8,128)S(1)}) custom-call(f32[256,1024]{1,0:T(8,128)S(1)} %collective-permute-done.3.refs_1_.refs_0_, f32[256,1024]{1,0:T(8,128)S(1)} %collective-permute-done.4.refs_2_.refs_1_, f32[320,1024]{1,0:T(8,128)S(1)} %collective-permute-done.14.refs_2_, ...), custom_call_target="tpu_custom_call" | custom-call | flops 805306368 | bytes 4456448 | tf_op jit(solution)/shard_map/pallas_call | solution.py:143
  63.8 2.3 %collective-permute-start.17 = (f32[144,1024]{1,0:T(8,128)S(1)}, f32[144,1024]{1,0:T(8,128)S(1)}, u32[]{:S(2)}, u32[]{:S(2)}) collective-permute-start(f32[144,1024]{1,0:T(8,128)S(1)} %slice.52), channel_id=1, source_target_pairs={{0,12},{1,33},{2,14},{3,35},{16,28},{17,49},{18,30},{19,51},{4,8},... | collective-permute-start | bytes 1769480 | tf_op jit(solution)/shard_map/ppermute | solution.py:42
  66.1 0.2 collective-permute-start.18
  66.3 1.4 %shard_map.44 = f32[256,1024]{1,0:T(8,128)S(1)} custom-call(f32[256,1024]{1,0:T(8,128)S(1)} %pad_maximum_fusion.2.refs_0_, f32[320,1024]{1,0:T(8,128)S(1)} %collective-permute-done.13.refs_4_.refs_1_, f32[320,1024]{1,0:T(8,128)S(1)} %collective-permute-done.14.refs_2_, f32[256,1024]{1,0:T(8,128)S(1)} %get-tuple-element.101.refs_3_, ...), custom_call_target="tpu_custom_call" | custom-call | flops 805306368 | bytes 5767168 | tf_op jit(solution)/shard_map/pallas_call | solution.py:143
  67.7 2.3 %collective-permute-done.15 = f32[128,1024]{1,0:T(8,128)S(1)} collective-permute-done((f32[128,1024]{1,0:T(8,128)S(1)}, f32[128,1024]{1,0:T(8,128)S(1)}, u32[]{:S(2)}, u32[]{:S(2)}) %collective-permute-start.15) | collective-permute-done | bytes 524320 | tf_op jit(solution)/shard_map/ppermute | solution.py:42
  70.0 0.8 collective-permute-done.16
  70.8 0.1 slice_add_fusion.2
  70.9 1.3 %collective-permute-start.20 = (f32[128,1024]{1,0:T(8,128)S(1)}, f32[128,1024]{1,0:T(8,128)S(1)}, u32[]{:S(2)}, u32[]{:S(2)}) collective-permute-start(f32[128,1024]{1,0:T(8,128)S(1)} %slice_add_fusion.2), channel_id=1, source_target_pairs={{0,12},{1,33},{2,14},{3,35},{16,28},{17,49},{18,30},{19,51},{4,8},... | collective-permute-start | bytes 1572872 | tf_op jit(solution)/shard_map/ppermute | solution.py:42
  72.2 0.1 slice_add_fusion.3
  72.3 0.8 collective-permute-start.19
  73.1 3.3 %collective-permute-done.17 = f32[144,1024]{1,0:T(8,128)S(1)} collective-permute-done((f32[144,1024]{1,0:T(8,128)S(1)}, f32[144,1024]{1,0:T(8,128)S(1)}, u32[]{:S(2)}, u32[]{:S(2)}) %collective-permute-start.17) | collective-permute-done | bytes 589856 | tf_op jit(solution)/shard_map/ppermute | solution.py:42
  76.4 0.7 collective-permute-done.18
  77.2 0.2 maximum_add_fusion
  77.4 4.6 %collective-permute-done.20 = f32[128,1024]{1,0:T(8,128)S(1)} collective-permute-done((f32[128,1024]{1,0:T(8,128)S(1)}, f32[128,1024]{1,0:T(8,128)S(1)}, u32[]{:S(2)}, u32[]{:S(2)}) %collective-permute-start.20) | collective-permute-done | bytes 524320 | tf_op jit(solution)/shard_map/ppermute | solution.py:42
  82.0 0.8 collective-permute-done.19
  82.8 0.2 slice_add_fusion
  83.0 3.1 %collective-permute-start.22 = (f32[64,1024]{1,0:T(8,128)S(1)}, f32[64,1024]{1,0:T(8,128)S(1)}, u32[]{:S(2)}, u32[]{:S(2)}) collective-permute-start(f32[64,1024]{1,0:T(8,128)S(1)} %get-tuple-element.120), channel_id=1, source_target_pairs={{0,64},{1,9},{2,66},{3,11},{16,80},{17,25},{18,82},{19,27},{4,68},... | collective-permute-start | bytes 786440 | tf_op jit(solution)/shard_map/ppermute | solution.py:42
  86.1 1.1 %collective-permute-start.23 = (f32[64,1024]{1,0:T(8,128)S(1)}, f32[64,1024]{1,0:T(8,128)S(1)}, u32[]{:S(2)}, u32[]{:S(2)}) collective-permute-start(f32[64,1024]{1,0:T(8,128)S(1)} %get-tuple-element.119), channel_id=1, source_target_pairs={{0,96},{1,5},{2,98},{3,7},{16,112},{17,21},{18,114},{19,23},{4,100... | collective-permute-start | bytes 786440 | tf_op jit(solution)/shard_map/ppermute | solution.py:42
  87.2 0.1 collective-permute-start.21
  87.3 3.6 %collective-permute-done.22 = f32[64,1024]{1,0:T(8,128)S(1)} collective-permute-done((f32[64,1024]{1,0:T(8,128)S(1)}, f32[64,1024]{1,0:T(8,128)S(1)}, u32[]{:S(2)}, u32[]{:S(2)}) %collective-permute-start.22) | collective-permute-done | bytes 262176 | tf_op jit(solution)/shard_map/ppermute | solution.py:42
  90.9 2.8 %collective-permute-done.23 = f32[64,1024]{1,0:T(8,128)S(1)} collective-permute-done((f32[64,1024]{1,0:T(8,128)S(1)}, f32[64,1024]{1,0:T(8,128)S(1)}, u32[]{:S(2)}, u32[]{:S(2)}) %collective-permute-start.23) | collective-permute-done | bytes 262176 | tf_op jit(solution)/shard_map/ppermute | solution.py:42
  93.7 0.1 collective-permute-done.21
  93.9 0.8 fusion
  (16 shorter events, 0.3 us)
Async XLA Ops:
  0.0 6.8 %copy-start = (f32[512,1024]{1,0:T(8,128)S(1)}, f32[512,1024]{1,0:T(8,128)}, u32[]{:S(2)}) copy-start(f32[512,1024]{1,0:T(8,128)} %param.4) | copy-start | bytes 6291460
  1.8 8.2 %collective-permute-start = (f32[64,1024]{1,0:T(8,128)}, f32[64,1024]{1,0:T(8,128)}, u32[]{:S(2)}, u32[]{:S(2)}) collective-permute-start(f32[64,1024]{1,0:T(8,128)} %shard_map.37), channel_id=1, source_target_pairs={{0,32},{1,13},{2,34},{3,15},{16,48},{17,29},{18,50},{19,31},{4,36}... | collective-permute-start | bytes 786440 | tf_op jit(solution)/shard_map/ppermute | solution.py:42
  3.4 10.7 %collective-permute-start.1 = (f32[64,1024]{1,0:T(8,128)}, f32[64,1024]{1,0:T(8,128)}, u32[]{:S(2)}, u32[]{:S(2)}) collective-permute-start(f32[64,1024]{1,0:T(8,128)} %shard_map.37), channel_id=1, source_target_pairs={{0,96},{1,5},{2,98},{3,7},{16,112},{17,21},{18,114},{19,23},{4,100... | collective-permute-start | bytes 786440 | tf_op jit(solution)/shard_map/ppermute | solution.py:42
  5.5 8.6 %collective-permute-start.2 = (f32[64,1024]{1,0:T(8,128)}, f32[64,1024]{1,0:T(8,128)}, u32[]{:S(2)}, u32[]{:S(2)}) collective-permute-start(f32[64,1024]{1,0:T(8,128)} %shard_map.37), channel_id=1, source_target_pairs={{0,64},{1,9},{2,66},{3,11},{16,80},{17,25},{18,82},{19,27},{4,68},... | collective-permute-start | bytes 786440 | tf_op jit(solution)/shard_map/ppermute | solution.py:42
  6.8 1.1 %copy-start.1 = (f32[64,1024]{1,0:T(8,128)S(1)}, f32[64,1024]{1,0:T(8,128)}, u32[]{:S(2)}) copy-start(f32[64,1024]{1,0:T(8,128)} %shard_map.37) | copy-start | bytes 786436
  8.0 25.0 %collective-permute-start.7 = (f32[320,1024]{1,0:T(8,128)S(1)}, f32[320,1024]{1,0:T(8,128)S(1)}, u32[]{:S(2)}, u32[]{:S(2)}) collective-permute-start(f32[320,1024]{1,0:T(8,128)S(1)} %pad_maximum_fusion.refs_3_.refs_2_), channel_id=1, source_target_pairs={{0,2},{1,19},{2,0},{3,17},{16,18},{17,3},{18,16},{19,1},{4,6},{5,2... | collective-permute-start | bytes 3932168 | tf_op jit(solution)/shard_map/ppermute | solution.py:42
  15.3 14.9 %collective-permute-start.3 = (f32[256,1024]{1,0:T(8,128)S(1)}, f32[256,1024]{1,0:T(8,128)S(1)}, u32[]{:S(2)}, u32[]{:S(2)}) collective-permute-start(f32[256,1024]{1,0:T(8,128)S(1)} %pad_maximum_fusion.2.refs_0_), channel_id=1, source_target_pairs={{0,4},{1,97},{2,6},{3,99},{16,20},{17,113},{18,22},{19,115},{4,0},... | collective-permute-start | bytes 3145736 | tf_op jit(solution)/shard_map/ppermute | solution.py:42
  17.0 16.0 %collective-permute-start.4 = (f32[256,1024]{1,0:T(8,128)S(1)}, f32[256,1024]{1,0:T(8,128)S(1)}, u32[]{:S(2)}, u32[]{:S(2)}) collective-permute-start(f32[256,1024]{1,0:T(8,128)S(1)} %pad_maximum_fusion.2.refs_0_), channel_id=1, source_target_pairs={{0,12},{1,33},{2,14},{3,35},{16,28},{17,49},{18,30},{19,51},{4,8},... | collective-permute-start | bytes 3145736 | tf_op jit(solution)/shard_map/ppermute | solution.py:42
  19.2 16.3 %collective-permute-start.10 = (f32[320,1024]{1,0:T(8,128)S(1)}, f32[320,1024]{1,0:T(8,128)S(1)}, u32[]{:S(2)}, u32[]{:S(2)}) collective-permute-start(f32[320,1024]{1,0:T(8,128)S(1)} %pad_maximum_fusion.refs_3_.refs_2_), channel_id=1, source_target_pairs={{0,1},{1,0},{2,3},{3,2},{4,5},{5,4},{6,7},{7,6},{8,9},{9,8},{10,11... | collective-permute-start | bytes 3932168 | tf_op jit(solution)/shard_map/ppermute | solution.py:46
  19.2 24.0 %collective-permute-start.8 = (f32[320,1024]{1,0:T(8,128)S(1)}, f32[320,1024]{1,0:T(8,128)S(1)}, u32[]{:S(2)}, u32[]{:S(2)}) collective-permute-start(f32[320,1024]{1,0:T(8,128)S(1)} %pad_maximum_fusion.refs_3_.refs_2_), channel_id=1, source_target_pairs={{0,18},{1,3},{2,16},{3,1},{16,2},{17,19},{18,0},{19,17},{4,22},{5,... | collective-permute-start | bytes 3932168 | tf_op jit(solution)/shard_map/ppermute | solution.py:42
  33.0 10.1 %collective-permute-start.9 = (f32[320,1024]{1,0:T(8,128)S(1)}, f32[320,1024]{1,0:T(8,128)S(1)}, u32[]{:S(2)}, u32[]{:S(2)}) collective-permute-start(f32[320,1024]{1,0:T(8,128)S(1)} %collective-permute-done.7.refs_3_.refs_4_), channel_id=1, source_target_pairs={{0,1},{1,0},{2,3},{3,2},{4,5},{5,4},{6,7},{7,6},{8,9},{9,8},{10,11... | collective-permute-start | bytes 3932168 | tf_op jit(solution)/shard_map/ppermute | solution.py:46
  33.0 14.9 %collective-permute-start.5 = (f32[128,1024]{1,0:T(8,128)S(1)}, f32[128,1024]{1,0:T(8,128)S(1)}, u32[]{:S(2)}, u32[]{:S(2)}) collective-permute-start(f32[128,1024]{1,0:T(8,128)S(1)} %slice.66), channel_id=1, source_target_pairs={{0,12},{1,33},{2,14},{3,35},{16,28},{17,49},{18,30},{19,51},{4,8},... | collective-permute-start | bytes 1572872 | tf_op jit(solution)/shard_map/ppermute | solution.py:42
  35.4 12.6 %collective-permute-start.6 = (f32[128,1024]{1,0:T(8,128)S(1)}, f32[128,1024]{1,0:T(8,128)S(1)}, u32[]{:S(2)}, u32[]{:S(2)}) collective-permute-start(f32[128,1024]{1,0:T(8,128)S(1)} %slice.67), channel_id=1, source_target_pairs={{0,4},{1,97},{2,6},{3,99},{16,20},{17,113},{18,22},{19,115},{4,0},... | collective-permute-start | bytes 1572872 | tf_op jit(solution)/shard_map/ppermute | solution.py:42
  35.5 19.8 %collective-permute-start.13 = (f32[320,1024]{1,0:T(8,128)S(1)}, f32[320,1024]{1,0:T(8,128)S(1)}, u32[]{:S(2)}, u32[]{:S(2)}) collective-permute-start(f32[320,1024]{1,0:T(8,128)S(1)} %collective-permute-done.7.refs_3_.refs_4_), channel_id=1, source_target_pairs={{0,18},{1,3},{2,16},{3,1},{16,2},{17,19},{18,0},{19,17},{4,22},{5,... | collective-permute-start | bytes 3932168 | tf_op jit(solution)/shard_map/ppermute | solution.py:42
  43.3 6.9 %collective-permute-start.11 = (f32[160,1024]{1,0:T(8,128)S(1)}, f32[160,1024]{1,0:T(8,128)S(1)}, u32[]{:S(2)}, u32[]{:S(2)}) collective-permute-start(f32[160,1024]{1,0:T(8,128)S(1)} %get-tuple-element.116), channel_id=1, source_target_pairs={{0,1},{1,0},{2,3},{3,2},{4,5},{5,4},{6,7},{7,6},{8,9},{9,8},{10,11... | collective-permute-start | bytes 1966088 | tf_op jit(solution)/shard_map/ppermute | solution.py:46
  43.4 6.8 %collective-permute-start.12 = (f32[160,1024]{1,0:T(8,128)S(1)}, f32[160,1024]{1,0:T(8,128)S(1)}, u32[]{:S(2)}, u32[]{:S(2)}) collective-permute-start(f32[160,1024]{1,0:T(8,128)S(1)} %get-tuple-element.115), channel_id=1, source_target_pairs={{0,1},{1,0},{2,3},{3,2},{4,5},{5,4},{6,7},{7,6},{8,9},{9,8},{10,11... | collective-permute-start | bytes 1966088 | tf_op jit(solution)/shard_map/ppermute | solution.py:46
  55.3 3.3 %collective-permute-start.14 = (f32[320,1024]{1,0:T(8,128)S(1)}, f32[320,1024]{1,0:T(8,128)S(1)}, u32[]{:S(2)}, u32[]{:S(2)}) collective-permute-start(f32[320,1024]{1,0:T(8,128)S(1)} %collective-permute-done.13.refs_4_.refs_1_), channel_id=1, source_target_pairs={{0,1},{1,0},{2,3},{3,2},{4,5},{5,4},{6,7},{7,6},{8,9},{9,8},{10,11... | collective-permute-start | bytes 3932168 | tf_op jit(solution)/shard_map/ppermute | solution.py:46
  59.6 10.5 %collective-permute-start.15 = (f32[128,1024]{1,0:T(8,128)S(1)}, f32[128,1024]{1,0:T(8,128)S(1)}, u32[]{:S(2)}, u32[]{:S(2)}) collective-permute-start(f32[128,1024]{1,0:T(8,128)S(1)} %get-tuple-element.99), channel_id=1, source_target_pairs={{0,12},{1,33},{2,14},{3,35},{16,28},{17,49},{18,30},{19,51},{4,8},... | collective-permute-start | bytes 1572872 | tf_op jit(solution)/shard_map/ppermute | solution.py:42
  61.6 9.2 %collective-permute-start.16 = (f32[128,1024]{1,0:T(8,128)S(1)}, f32[128,1024]{1,0:T(8,128)S(1)}, u32[]{:S(2)}, u32[]{:S(2)}) collective-permute-start(f32[128,1024]{1,0:T(8,128)S(1)} %get-tuple-element.100), channel_id=1, source_target_pairs={{0,4},{1,97},{2,6},{3,99},{16,20},{17,113},{18,22},{19,115},{4,0},... | collective-permute-start | bytes 1572872 | tf_op jit(solution)/shard_map/ppermute | solution.py:42
  63.8 12.5 %collective-permute-start.17 = (f32[144,1024]{1,0:T(8,128)S(1)}, f32[144,1024]{1,0:T(8,128)S(1)}, u32[]{:S(2)}, u32[]{:S(2)}) collective-permute-start(f32[144,1024]{1,0:T(8,128)S(1)} %slice.52), channel_id=1, source_target_pairs={{0,12},{1,33},{2,14},{3,35},{16,28},{17,49},{18,30},{19,51},{4,8},... | collective-permute-start | bytes 1769480 | tf_op jit(solution)/shard_map/ppermute | solution.py:42
  66.1 11.0 %collective-permute-start.18 = (f32[144,1024]{1,0:T(8,128)S(1)}, f32[144,1024]{1,0:T(8,128)S(1)}, u32[]{:S(2)}, u32[]{:S(2)}) collective-permute-start(f32[144,1024]{1,0:T(8,128)S(1)} %slice.54), channel_id=1, source_target_pairs={{0,4},{1,97},{2,6},{3,99},{16,20},{17,113},{18,22},{19,115},{4,0},... | collective-permute-start | bytes 1769480 | tf_op jit(solution)/shard_map/ppermute | solution.py:42
  70.9 11.1 %collective-permute-start.20 = (f32[128,1024]{1,0:T(8,128)S(1)}, f32[128,1024]{1,0:T(8,128)S(1)}, u32[]{:S(2)}, u32[]{:S(2)}) collective-permute-start(f32[128,1024]{1,0:T(8,128)S(1)} %slice_add_fusion.2), channel_id=1, source_target_pairs={{0,12},{1,33},{2,14},{3,35},{16,28},{17,49},{18,30},{19,51},{4,8},... | collective-permute-start | bytes 1572872 | tf_op jit(solution)/shard_map/ppermute | solution.py:42
  72.3 10.5 %collective-permute-start.19 = (f32[128,1024]{1,0:T(8,128)S(1)}, f32[128,1024]{1,0:T(8,128)S(1)}, u32[]{:S(2)}, u32[]{:S(2)}) collective-permute-start(f32[128,1024]{1,0:T(8,128)S(1)} %slice_add_fusion.3), channel_id=1, source_target_pairs={{0,4},{1,97},{2,6},{3,99},{16,20},{17,113},{18,22},{19,115},{4,0},... | collective-permute-start | bytes 1572872 | tf_op jit(solution)/shard_map/ppermute | solution.py:42
  83.0 8.0 %collective-permute-start.22 = (f32[64,1024]{1,0:T(8,128)S(1)}, f32[64,1024]{1,0:T(8,128)S(1)}, u32[]{:S(2)}, u32[]{:S(2)}) collective-permute-start(f32[64,1024]{1,0:T(8,128)S(1)} %get-tuple-element.120), channel_id=1, source_target_pairs={{0,64},{1,9},{2,66},{3,11},{16,80},{17,25},{18,82},{19,27},{4,68},... | collective-permute-start | bytes 786440 | tf_op jit(solution)/shard_map/ppermute | solution.py:42
  86.1 7.7 %collective-permute-start.23 = (f32[64,1024]{1,0:T(8,128)S(1)}, f32[64,1024]{1,0:T(8,128)S(1)}, u32[]{:S(2)}, u32[]{:S(2)}) collective-permute-start(f32[64,1024]{1,0:T(8,128)S(1)} %get-tuple-element.119), channel_id=1, source_target_pairs={{0,96},{1,5},{2,98},{3,7},{16,112},{17,21},{18,114},{19,23},{4,100... | collective-permute-start | bytes 786440 | tf_op jit(solution)/shard_map/ppermute | solution.py:42
  87.2 6.6 %collective-permute-start.21 = (f32[64,1024]{1,0:T(8,128)S(1)}, f32[64,1024]{1,0:T(8,128)S(1)}, u32[]{:S(2)}, u32[]{:S(2)}) collective-permute-start(f32[64,1024]{1,0:T(8,128)S(1)} %slice.71), channel_id=1, source_target_pairs={{0,32},{1,13},{2,34},{3,15},{16,48},{17,29},{18,50},{19,31},{4,36}... | collective-permute-start | bytes 786440 | tf_op jit(solution)/shard_map/ppermute | solution.py:42

commit v5 on v4

--- a/solution.py
+++ b/solution.py
@@ -215,7 +215,7 @@
     s[3:] = add(rows[3:], [own, own_swapped, x_near, x_near_swapped], states=s[3:], last=None)
     x_far_swapped, _ = lax.optimization_barrier((x_far_swapped, s))
     x_far_swapped = jnp.concatenate(x_far_swapped, axis=0)
-    s = add(rows, [x_far, x_far_swapped], states=s, last=None)
+    s[1:] = add(rows[1:], [x_far, x_far_swapped], states=s[1:], last=None)
     x_both, _ = lax.optimization_barrier((x_both, s))
     both_swapped = swap(x_both)
     s[1:] = add(rows[1:], [x_both], states=s[1:], last=None)
@@ -223,10 +223,10 @@
     (both,) = add(rows[3:], [both_swapped], states=s[3:], last=1.0 / total_real)
     s, both = lax.optimization_barrier((s, both))
     (line_near,), (line_far,) = add(rows[1:3], [both_swapped], states=s[1:3], last=1.0 / total_real)
-    ((line,),) = add(rows[:1], [x_both, both_swapped], states=s[:1], last=1.0 / total_real)
+    ((line,),) = add(rows[:1], [x_far, x_far_swapped, x_both, both_swapped], states=s[:1], last=1.0 / total_real)
 
     add_near, add_far = move(both[0], "yx", "far"), move(both[1], "yx", "near")
-    extra = 16
+    extra = 8
     near_rest = move(line_near[half - extra :], "yx", "near")
     far_rest = move(line_far[: half + extra], "yx", "far")
     add_near, add_far, line = lax.optimization_barrier((add_near, add_far, line))

time: 94.8 us -> 94.4 us (level)
  starting transfers between devices: 33.1 us -> 31.8 us
  transfers between devices with their start and end apart: 24 -> 24, of which waited for: 13 -> 14; matrix products, arithmetic and copies ran while one was open for 4% -> 4% of each run, Pallas kernels for 22% -> 22%
where the time goes in v5:
time: 94.4 us; the launch traced here: 94.3 us
  waiting for transfers between devices  34 us (36%)
  starting transfers between devices  31.8 us (34%)
  Pallas kernels  23.3 us (25%)
  other arithmetic  3.2 us (3%)
  local copies, waits for them, and re-layouts  1.63 us (2%)
    ppermute x19, waiting for transfers between devices, move(): return lax.ppermute(v, AXES, STEPS[axes, step])  33.5 us
    ppermute x19, starting transfers between devices, move(): return lax.ppermute(v, AXES, STEPS[axes, step])  31.2 us
    pallas_call x8, Pallas kernels, pairs(): pl.pallas_call(functools.partial(pair_kernel, [len(batch) for batch in ro...  21.5 us
  transfers between devices with their start and end apart: 24, of which 14 were waited for; matrix products, arithmetic and copies ran while one was open for 4% of the time, Pallas kernels for 22%

profile of v5, /device:TPU:0, one launch (start us, length us, event | category | flops | bytes accessed | tf_op | source)
XLA Modules:
  0.0 94.3 jit_solution(8969383053102541681)
XLA Ops:
  0.0 1.8 %shard_map.37 = f32[64,1024]{1,0:T(8,128)} custom-call(f32[64,1024]{1,0:T(8,128)} %v_ref.1), custom_call_target="tpu_custom_call" | custom-call | tf_op jit(solution)/shard_map/pallas_call | solution.py:176
  1.8 1.6 %collective-permute-start = (f32[64,1024]{1,0:T(8,128)}, f32[64,1024]{1,0:T(8,128)}, u32[]{:S(2)}, u32[]{:S(2)}) collective-permute-start(f32[64,1024]{1,0:T(8,128)} %shard_map.37), channel_id=1, source_target_pairs={{0,32},{1,13},{2,34},{3,15},{16,48},{17,29},{18,50},{19,31},{4,36}... | collective-permute-start | bytes 786440 | tf_op jit(solution)/shard_map/ppermute | solution.py:42
  3.4 2.1 %collective-permute-start.1 = (f32[64,1024]{1,0:T(8,128)}, f32[64,1024]{1,0:T(8,128)}, u32[]{:S(2)}, u32[]{:S(2)}) collective-permute-start(f32[64,1024]{1,0:T(8,128)} %shard_map.37), channel_id=1, source_target_pairs={{0,96},{1,5},{2,98},{3,7},{16,112},{17,21},{18,114},{19,23},{4,100... | collective-permute-start | bytes 786440 | tf_op jit(solution)/shard_map/ppermute | solution.py:42
  5.5 0.6 collective-permute-start.2
  6.1 0.7 pad_clamp_fusion
  6.8 1.1 %gather_fusion = f32[256,1024]{1,0:T(8,128)S(1)} fusion(f32[512,1024]{1,0:T(8,128)S(1)} %copy-done, s32[1024]{0:T(1024)S(1)} %pad_clamp_fusion), kind=kCustom, calls=%fused_computation | custom fusion | bytes 2098176 | tf_op jit(solution)/shard_map/gather | solution.py:191
  7.9 0.1 pad_maximum_fusion.refs_3_.refs_2_
  8.0 2.0 %collective-permute-start.5 = (f32[320,1024]{1,0:T(8,128)S(1)}, f32[320,1024]{1,0:T(8,128)S(1)}, u32[]{:S(2)}, u32[]{:S(2)}) collective-permute-start(f32[320,1024]{1,0:T(8,128)S(1)} %pad_maximum_fusion.refs_3_.refs_2_), channel_id=1, source_target_pairs={{0,2},{1,19},{2,0},{3,17},{16,18},{17,3},{18,16},{19,1},{4,6},{5,2... | collective-permute-start | bytes 3932168 | tf_op jit(solution)/shard_map/ppermute | solution.py:42
  10.0 4.1 %collective-permute-done.1 = f32[64,1024]{1,0:T(8,128)} collective-permute-done((f32[64,1024]{1,0:T(8,128)}, f32[64,1024]{1,0:T(8,128)}, u32[]{:S(2)}, u32[]{:S(2)}) %collective-permute-start.1) | collective-permute-done | bytes 262176 | tf_op jit(solution)/shard_map/ppermute | solution.py:42
  14.1 0.0 collective-permute-done.2
  14.1 1.2 %pad_maximum_fusion.1.refs_0_ = f32[256,1024]{1,0:T(8,128)S(1)} fusion(f32[64,1024]{1,0:T(8,128)} %collective-permute-done.2, f32[64,1024]{1,0:T(8,128)} %collective-permute-done.1, f32[64,1024]{1,0:T(8,128)} %collective-permute-done, f32[64,1024]{1,0:T(8,128)S(1)} %copy-done.1), kind=kLoop, calls=%fused_computation.2 | loop fusion | flops 786432 | bytes 2097152 | tf_op jit(solution)/shard_map/concatenate | solution.py:201
  15.3 1.7 %collective-permute-start.3 = (f32[256,1024]{1,0:T(8,128)S(1)}, f32[256,1024]{1,0:T(8,128)S(1)}, u32[]{:S(2)}, u32[]{:S(2)}) collective-permute-start(f32[256,1024]{1,0:T(8,128)S(1)} %pad_maximum_fusion.1.refs_0_), channel_id=1, source_target_pairs={{0,4},{1,97},{2,6},{3,99},{16,20},{17,113},{18,22},{19,115},{4,0},... | collective-permute-start | bytes 3145736 | tf_op jit(solution)/shard_map/ppermute | solution.py:42
  17.0 2.2 %collective-permute-start.4 = (f32[256,1024]{1,0:T(8,128)S(1)}, f32[256,1024]{1,0:T(8,128)S(1)}, u32[]{:S(2)}, u32[]{:S(2)}) collective-permute-start(f32[256,1024]{1,0:T(8,128)S(1)} %pad_maximum_fusion.1.refs_0_), channel_id=1, source_target_pairs={{0,12},{1,33},{2,14},{3,35},{16,28},{17,49},{18,30},{19,51},{4,8},... | collective-permute-start | bytes 3145736 | tf_op jit(solution)/shard_map/ppermute | solution.py:42
  19.2 0.0 collective-permute-start.8
  19.2 4.0 %collective-permute-start.6 = (f32[320,1024]{1,0:T(8,128)S(1)}, f32[320,1024]{1,0:T(8,128)S(1)}, u32[]{:S(2)}, u32[]{:S(2)}) collective-permute-start(f32[320,1024]{1,0:T(8,128)S(1)} %pad_maximum_fusion.refs_3_.refs_2_), channel_id=1, source_target_pairs={{0,18},{1,3},{2,16},{3,1},{16,2},{17,19},{18,0},{19,17},{4,22},{5,... | collective-permute-start | bytes 3932168 | tf_op jit(solution)/shard_map/ppermute | solution.py:42
  23.2 7.0 %collective-permute-done.3.refs_1_.refs_0_ = f32[256,1024]{1,0:T(8,128)S(1)} collective-permute-done((f32[256,1024]{1,0:T(8,128)S(1)}, f32[256,1024]{1,0:T(8,128)S(1)}, u32[]{:S(2)}, u32[]{:S(2)}) %collective-permute-start.3) | collective-permute-done | bytes 1048608 | tf_op jit(solution)/shard_map/ppermute | solution.py:42
  30.2 2.8 %collective-permute-done.4.refs_2_.refs_1_ = f32[256,1024]{1,0:T(8,128)S(1)} collective-permute-done((f32[256,1024]{1,0:T(8,128)S(1)}, f32[256,1024]{1,0:T(8,128)S(1)}, u32[]{:S(2)}, u32[]{:S(2)}) %collective-permute-start.4) | collective-permute-done | bytes 1048608 | tf_op jit(solution)/shard_map/ppermute | solution.py:42
  33.0 0.0 collective-permute-done.5.refs_3_.refs_4_
  33.0 0.0 collective-permute-start.7
  33.0 0.1 collective-permute-start.10
  33.2 2.3 %collective-permute-start.9 = (f32[128,1024]{1,0:T(8,128)S(1)}, f32[128,1024]{1,0:T(8,128)S(1)}, u32[]{:S(2)}, u32[]{:S(2)}) collective-permute-start(f32[128,1024]{1,0:T(8,128)S(1)} %slice.66), channel_id=1, source_target_pairs={{0,12},{1,33},{2,14},{3,35},{16,28},{17,49},{18,30},{19,51},{4,8},... | collective-permute-start | bytes 1572872 | tf_op jit(solution)/shard_map/ppermute | solution.py:42
  35.5 4.1 %collective-permute-start.11 = (f32[320,1024]{1,0:T(8,128)S(1)}, f32[320,1024]{1,0:T(8,128)S(1)}, u32[]{:S(2)}, u32[]{:S(2)}) collective-permute-start(f32[320,1024]{1,0:T(8,128)S(1)} %collective-permute-done.5.refs_3_.refs_4_), channel_id=1, source_target_pairs={{0,18},{1,3},{2,16},{3,1},{16,2},{17,19},{18,0},{19,17},{4,22},{5,... | collective-permute-start | bytes 3932168 | tf_op jit(solution)/shard_map/ppermute | solution.py:42
  39.6 3.5 %shard_map.38 = (f32[256,1024]{1,0:T(8,128)S(1)}, f32[256,128]{1,0:T(8,128)S(1)}, f32[256,1024]{1,0:T(8,128)S(1)}, f32[256,128]{1,0:T(8,128)S(1)}, f32[256,1024]{1,0:T(8,128)S(1)}, /*index=5*/f32[256,128]{1,0:T(8,128)S(1)}) custom-call(f32[256,1024]{1,0:T(8,128)S(1)} %pad_maximum_fusion.1.refs_0_, f32[256,1024]{1,0:T(8,128)S(1)} %collective-permute-done.3.refs_1_.refs_0_, ...), custom_call_target="tpu_custom_call" | custom-call | flops 2415919104 | bytes 5767168 | tf_op jit(solution)/shard_map/pallas_call | solution.py:143
  43.1 0.0 collective-permute-done.6.refs_4_.refs_1_
  43.1 0.0 collective-permute-done.7.refs_4_.refs_5_
  43.1 0.1 fusion.1
  43.3 0.1 collective-permute-start.12
  43.4 0.5 collective-permute-start.13
  43.9 4.1 %shard_map.39 = (f32[256,1024]{1,0:T(8,128)S(1)}, f32[256,128]{1,0:T(8,128)S(1)}, f32[256,1024]{1,0:T(8,128)S(1)}, f32[256,128]{1,0:T(8,128)S(1)}, f32[256,1024]{1,0:T(8,128)S(1)}, /*index=5*/f32[256,128]{1,0:T(8,128)S(1)}) custom-call(f32[256,1024]{1,0:T(8,128)S(1)} %pad_maximum_fusion.1.re, ...), custom_call_target="tpu_custom_call", output_to_operand_aliasing={{0}: (5, {}), {1}: (6, {}), {2}: (7, {}), {3}: (8, {}), {4}... | custom-call | flops 2415919104 | bytes 5767168 | tf_op jit(solution)/shard_map/pallas_call | solution.py:143
  48.0 2.2 %shard_map.40 = (f32[256,1024]{1,0:T(8,128)S(1)}, f32[256,128]{1,0:T(8,128)S(1)}) custom-call(f32[128,1024]{1,0:T(8,128)S(1)} %collective-permute-done.9.refs_0_.refs_2_, f32[128,1024]{1,0:T(8,128)S(1)} %collective-permute-done.10.refs_1_.refs_3_, f32[320,1024]{1,0:T(8,128)S(1)} %pad_maximum_fusion.refs_3_.refs_2_, ...), custom_call_target="tpu_custom_call" | custom-call | flops 1610612736 | bytes 8388608 | tf_op jit(solution)/shard_map/pallas_call | solution.py:143
  50.2 0.0 collective-permute-done.12
  50.2 0.1 constant_dynamic-update-slice_fusion.1
  50.2 0.1 constant_dynamic-update-slice_fusion.refs_5_.refs_2_
  50.3 4.1 %shard_map.41 = (f32[256,1024]{1,0:T(8,128)S(1)}, f32[256,128]{1,0:T(8,128)S(1)}, f32[256,1024]{1,0:T(8,128)S(1)}, f32[256,128]{1,0:T(8,128)S(1)}, f32[256,1024]{1,0:T(8,128)S(1)}, /*index=5*/f32[256,128]{1,0:T(8,128)S(1)}) custom-call(f32[256,1024]{1,0:T(8,128)S(1)} %collective-permute-done, ...), custom_call_target="tpu_custom_call", output_to_operand_aliasing={{0}: (6, {}), {1}: (7, {}), {2}: (8, {}), {3}: (9, {}), {4}... | custom-call | flops 2415919104 | bytes 5767168 | tf_op jit(solution)/shard_map/pallas_call | solution.py:143
  54.4 0.8 collective-permute-done.11.refs_4_.refs_3_
  55.2 0.0 collective-permute-start.14
  55.2 2.5 %shard_map.42 = (f32[256,1024]{1,0:T(8,128)S(1)}, f32[256,128]{1,0:T(8,128)S(1)}, f32[256,1024]{1,0:T(8,128)S(1)}, f32[256,128]{1,0:T(8,128)S(1)}, f32[256,1024]{1,0:T(8,128)S(1)}, /*index=5*/f32[256,128]{1,0:T(8,128)S(1)}) custom-call(f32[256,1024]{1,0:T(8,128)S(1)} %collective-permute-done, ...), custom_call_target="tpu_custom_call", output_to_operand_aliasing={{0}: (5, {}), {1}: (6, {}), {2}: (7, {}), {3}: (8, {}), {4}... | custom-call | flops 1207959552 | bytes 4456448 | tf_op jit(solution)/shard_map/pallas_call | solution.py:143
  57.7 0.5 collective-permute-done.14.refs_2_.refs_4_
  58.2 0.9 shard_map.43
  59.1 2.5 %collective-permute-start.15 = (f32[128,1024]{1,0:T(8,128)S(1)}, f32[128,1024]{1,0:T(8,128)S(1)}, u32[]{:S(2)}, u32[]{:S(2)}) collective-permute-start(f32[128,1024]{1,0:T(8,128)S(1)} %get-tuple-element.95), channel_id=1, source_target_pairs={{0,12},{1,33},{2,14},{3,35},{16,28},{17,49},{18,30},{19,51},{4,8},... | collective-permute-start | bytes 1572872 | tf_op jit(solution)/shard_map/ppermute | solution.py:42
  61.6 0.0 collective-permute-start.16
  61.6 1.7 %shard_map.45 = (f32[256,1024]{1,0:T(8,128)S(1)}, f32[256,1024]{1,0:T(8,128)S(1)}) custom-call(f32[256,1024]{1,0:T(8,128)S(1)} %collective-permute-done.3.refs_1_.refs_0_, f32[256,1024]{1,0:T(8,128)S(1)} %collective-permute-done.4.refs_2_.refs_1_, f32[320,1024]{1,0:T(8,128)S(1)} %collective-permute-done.14.refs_2_.refs_4_, ...), custom_call_target="tpu_custom_call" | custom-call | flops 805306368 | bytes 4456448 | tf_op jit(solution)/shard_map/pallas_call | solution.py:143
  63.4 1.6 %collective-permute-start.17 = (f32[136,1024]{1,0:T(8,128)S(1)}, f32[136,1024]{1,0:T(8,128)S(1)}, u32[]{:S(2)}, u32[]{:S(2)}) collective-permute-start(f32[136,1024]{1,0:T(8,128)S(1)} %slice.52), channel_id=1, source_target_pairs={{0,12},{1,33},{2,14},{3,35},{16,28},{17,49},{18,30},{19,51},{4,8},... | collective-permute-start | bytes 1671176 | tf_op jit(solution)/shard_map/ppermute | solution.py:42
  65.1 0.8 collective-permute-start.18
  65.9 2.4 %shard_map.44 = f32[256,1024]{1,0:T(8,128)S(1)} custom-call(f32[256,1024]{1,0:T(8,128)S(1)} %pad_maximum_fusion.1.refs_0_, f32[320,1024]{1,0:T(8,128)S(1)} %collective-permute-done.6.refs_4_.refs_1_, f32[320,1024]{1,0:T(8,128)S(1)} %constant_dynamic-update-slice_fusion.refs_5_.refs_2_, f32[320,1024]{1,0:T(8,128)S(1)} %collective-permute-done.11.refs_4_.refs_3_, ...), custom_call_target="tpu_custom_call" | custom-call | flops 1610612736 | bytes 8388608 | tf_op jit(solution)/shard_map/pallas_call | solution.py:143
  68.3 1.3 %collective-permute-done.15 = f32[128,1024]{1,0:T(8,128)S(1)} collective-permute-done((f32[128,1024]{1,0:T(8,128)S(1)}, f32[128,1024]{1,0:T(8,128)S(1)}, u32[]{:S(2)}, u32[]{:S(2)}) %collective-permute-start.15) | collective-permute-done | bytes 524320 | tf_op jit(solution)/shard_map/ppermute | solution.py:42
  69.6 1.2 %collective-permute-done.16 = f32[128,1024]{1,0:T(8,128)S(1)} collective-permute-done((f32[128,1024]{1,0:T(8,128)S(1)}, f32[128,1024]{1,0:T(8,128)S(1)}, u32[]{:S(2)}, u32[]{:S(2)}) %collective-permute-start.16) | collective-permute-done | bytes 524320 | tf_op jit(solution)/shard_map/ppermute | solution.py:42
  70.8 0.1 slice_add_fusion.2
  70.9 1.3 %collective-permute-start.20 = (f32[128,1024]{1,0:T(8,128)S(1)}, f32[128,1024]{1,0:T(8,128)S(1)}, u32[]{:S(2)}, u32[]{:S(2)}) collective-permute-start(f32[128,1024]{1,0:T(8,128)S(1)} %slice_add_fusion.2), channel_id=1, source_target_pairs={{0,12},{1,33},{2,14},{3,35},{16,28},{17,49},{18,30},{19,51},{4,8},... | collective-permute-start | bytes 1572872 | tf_op jit(solution)/shard_map/ppermute | solution.py:42
  72.2 0.1 slice_add_fusion.3
  72.2 0.1 collective-permute-start.19
  72.3 3.2 %collective-permute-done.17 = f32[136,1024]{1,0:T(8,128)S(1)} collective-permute-done((f32[136,1024]{1,0:T(8,128)S(1)}, f32[136,1024]{1,0:T(8,128)S(1)}, u32[]{:S(2)}, u32[]{:S(2)}) %collective-permute-start.17) | collective-permute-done | bytes 557088 | tf_op jit(solution)/shard_map/ppermute | solution.py:42
  75.6 1.2 %collective-permute-done.18 = f32[136,1024]{1,0:T(8,128)S(1)} collective-permute-done((f32[136,1024]{1,0:T(8,128)S(1)}, f32[136,1024]{1,0:T(8,128)S(1)}, u32[]{:S(2)}, u32[]{:S(2)}) %collective-permute-start.18) | collective-permute-done | bytes 557088 | tf_op jit(solution)/shard_map/ppermute | solution.py:42
  76.8 0.2 maximum_add_fusion
  77.0 4.3 %collective-permute-done.20 = f32[128,1024]{1,0:T(8,128)S(1)} collective-permute-done((f32[128,1024]{1,0:T(8,128)S(1)}, f32[128,1024]{1,0:T(8,128)S(1)}, u32[]{:S(2)}, u32[]{:S(2)}) %collective-permute-start.20) | collective-permute-done | bytes 524320 | tf_op jit(solution)/shard_map/ppermute | solution.py:42
  81.4 1.0 %collective-permute-done.19 = f32[128,1024]{1,0:T(8,128)S(1)} collective-permute-done((f32[128,1024]{1,0:T(8,128)S(1)}, f32[128,1024]{1,0:T(8,128)S(1)}, u32[]{:S(2)}, u32[]{:S(2)}) %collective-permute-start.19) | collective-permute-done | bytes 524320 | tf_op jit(solution)/shard_map/ppermute | solution.py:42
  82.4 0.2 slice_add_fusion
  82.6 3.1 %collective-permute-start.22 = (f32[64,1024]{1,0:T(8,128)S(1)}, f32[64,1024]{1,0:T(8,128)S(1)}, u32[]{:S(2)}, u32[]{:S(2)}) collective-permute-start(f32[64,1024]{1,0:T(8,128)S(1)} %get-tuple-element.116), channel_id=1, source_target_pairs={{0,64},{1,9},{2,66},{3,11},{16,80},{17,25},{18,82},{19,27},{4,68},... | collective-permute-start | bytes 786440 | tf_op jit(solution)/shard_map/ppermute | solution.py:42
  85.7 1.1 %collective-permute-start.23 = (f32[64,1024]{1,0:T(8,128)S(1)}, f32[64,1024]{1,0:T(8,128)S(1)}, u32[]{:S(2)}, u32[]{:S(2)}) collective-permute-start(f32[64,1024]{1,0:T(8,128)S(1)} %get-tuple-element.115), channel_id=1, source_target_pairs={{0,96},{1,5},{2,98},{3,7},{16,112},{17,21},{18,114},{19,23},{4,100... | collective-permute-start | bytes 786440 | tf_op jit(solution)/shard_map/ppermute | solution.py:42
  86.9 0.1 collective-permute-start.21
  87.0 3.6 %collective-permute-done.22 = f32[64,1024]{1,0:T(8,128)S(1)} collective-permute-done((f32[64,1024]{1,0:T(8,128)S(1)}, f32[64,1024]{1,0:T(8,128)S(1)}, u32[]{:S(2)}, u32[]{:S(2)}) %collective-permute-start.22) | collective-permute-done | bytes 262176 | tf_op jit(solution)/shard_map/ppermute | solution.py:42
  90.6 2.8 %collective-permute-done.23 = f32[64,1024]{1,0:T(8,128)S(1)} collective-permute-done((f32[64,1024]{1,0:T(8,128)S(1)}, f32[64,1024]{1,0:T(8,128)S(1)}, u32[]{:S(2)}, u32[]{:S(2)}) %collective-permute-start.23) | collective-permute-done | bytes 262176 | tf_op jit(solution)/shard_map/ppermute | solution.py:42
  93.4 0.1 collective-permute-done.21
  93.5 0.8 fusion
  (17 shorter events, 0.3 us)
Async XLA Ops:
  0.0 6.8 %copy-start = (f32[512,1024]{1,0:T(8,128)S(1)}, f32[512,1024]{1,0:T(8,128)}, u32[]{:S(2)}) copy-start(f32[512,1024]{1,0:T(8,128)} %param.4) | copy-start | bytes 6291460
  1.8 8.2 %collective-permute-start = (f32[64,1024]{1,0:T(8,128)}, f32[64,1024]{1,0:T(8,128)}, u32[]{:S(2)}, u32[]{:S(2)}) collective-permute-start(f32[64,1024]{1,0:T(8,128)} %shard_map.37), channel_id=1, source_target_pairs={{0,32},{1,13},{2,34},{3,15},{16,48},{17,29},{18,50},{19,31},{4,36}... | collective-permute-start | bytes 786440 | tf_op jit(solution)/shard_map/ppermute | solution.py:42
  3.4 10.7 %collective-permute-start.1 = (f32[64,1024]{1,0:T(8,128)}, f32[64,1024]{1,0:T(8,128)}, u32[]{:S(2)}, u32[]{:S(2)}) collective-permute-start(f32[64,1024]{1,0:T(8,128)} %shard_map.37), channel_id=1, source_target_pairs={{0,96},{1,5},{2,98},{3,7},{16,112},{17,21},{18,114},{19,23},{4,100... | collective-permute-start | bytes 786440 | tf_op jit(solution)/shard_map/ppermute | solution.py:42
  5.5 8.6 %collective-permute-start.2 = (f32[64,1024]{1,0:T(8,128)}, f32[64,1024]{1,0:T(8,128)}, u32[]{:S(2)}, u32[]{:S(2)}) collective-permute-start(f32[64,1024]{1,0:T(8,128)} %shard_map.37), channel_id=1, source_target_pairs={{0,64},{1,9},{2,66},{3,11},{16,80},{17,25},{18,82},{19,27},{4,68},... | collective-permute-start | bytes 786440 | tf_op jit(solution)/shard_map/ppermute | solution.py:42
  6.8 1.1 %copy-start.1 = (f32[64,1024]{1,0:T(8,128)S(1)}, f32[64,1024]{1,0:T(8,128)}, u32[]{:S(2)}) copy-start(f32[64,1024]{1,0:T(8,128)} %shard_map.37) | copy-start | bytes 786436
  8.0 25.0 %collective-permute-start.5 = (f32[320,1024]{1,0:T(8,128)S(1)}, f32[320,1024]{1,0:T(8,128)S(1)}, u32[]{:S(2)}, u32[]{:S(2)}) collective-permute-start(f32[320,1024]{1,0:T(8,128)S(1)} %pad_maximum_fusion.refs_3_.refs_2_), channel_id=1, source_target_pairs={{0,2},{1,19},{2,0},{3,17},{16,18},{17,3},{18,16},{19,1},{4,6},{5,2... | collective-permute-start | bytes 3932168 | tf_op jit(solution)/shard_map/ppermute | solution.py:42
  15.3 14.9 %collective-permute-start.3 = (f32[256,1024]{1,0:T(8,128)S(1)}, f32[256,1024]{1,0:T(8,128)S(1)}, u32[]{:S(2)}, u32[]{:S(2)}) collective-permute-start(f32[256,1024]{1,0:T(8,128)S(1)} %pad_maximum_fusion.1.refs_0_), channel_id=1, source_target_pairs={{0,4},{1,97},{2,6},{3,99},{16,20},{17,113},{18,22},{19,115},{4,0},... | collective-permute-start | bytes 3145736 | tf_op jit(solution)/shard_map/ppermute | solution.py:42
  17.0 16.0 %collective-permute-start.4 = (f32[256,1024]{1,0:T(8,128)S(1)}, f32[256,1024]{1,0:T(8,128)S(1)}, u32[]{:S(2)}, u32[]{:S(2)}) collective-permute-start(f32[256,1024]{1,0:T(8,128)S(1)} %pad_maximum_fusion.1.refs_0_), channel_id=1, source_target_pairs={{0,12},{1,33},{2,14},{3,35},{16,28},{17,49},{18,30},{19,51},{4,8},... | collective-permute-start | bytes 3145736 | tf_op jit(solution)/shard_map/ppermute | solution.py:42
  19.2 16.3 %collective-permute-start.8 = (f32[320,1024]{1,0:T(8,128)S(1)}, f32[320,1024]{1,0:T(8,128)S(1)}, u32[]{:S(2)}, u32[]{:S(2)}) collective-permute-start(f32[320,1024]{1,0:T(8,128)S(1)} %pad_maximum_fusion.refs_3_.refs_2_), channel_id=1, source_target_pairs={{0,1},{1,0},{2,3},{3,2},{4,5},{5,4},{6,7},{7,6},{8,9},{9,8},{10,11... | collective-permute-start | bytes 3932168 | tf_op jit(solution)/shard_map/ppermute | solution.py:46
  19.2 24.0 %collective-permute-start.6 = (f32[320,1024]{1,0:T(8,128)S(1)}, f32[320,1024]{1,0:T(8,128)S(1)}, u32[]{:S(2)}, u32[]{:S(2)}) collective-permute-start(f32[320,1024]{1,0:T(8,128)S(1)} %pad_maximum_fusion.refs_3_.refs_2_), channel_id=1, source_target_pairs={{0,18},{1,3},{2,16},{3,1},{16,2},{17,19},{18,0},{19,17},{4,22},{5,... | collective-permute-start | bytes 3932168 | tf_op jit(solution)/shard_map/ppermute | solution.py:42
  33.0 10.1 %collective-permute-start.7 = (f32[320,1024]{1,0:T(8,128)S(1)}, f32[320,1024]{1,0:T(8,128)S(1)}, u32[]{:S(2)}, u32[]{:S(2)}) collective-permute-start(f32[320,1024]{1,0:T(8,128)S(1)} %collective-permute-done.5.refs_3_.refs_4_), channel_id=1, source_target_pairs={{0,1},{1,0},{2,3},{3,2},{4,5},{5,4},{6,7},{7,6},{8,9},{9,8},{10,11... | collective-permute-start | bytes 3932168 | tf_op jit(solution)/shard_map/ppermute | solution.py:46
  33.0 14.9 %collective-permute-start.10 = (f32[128,1024]{1,0:T(8,128)S(1)}, f32[128,1024]{1,0:T(8,128)S(1)}, u32[]{:S(2)}, u32[]{:S(2)}) collective-permute-start(f32[128,1024]{1,0:T(8,128)S(1)} %slice.67), channel_id=1, source_target_pairs={{0,4},{1,97},{2,6},{3,99},{16,20},{17,113},{18,22},{19,115},{4,0},... | collective-permute-start | bytes 1572872 | tf_op jit(solution)/shard_map/ppermute | solution.py:42
  33.2 14.8 %collective-permute-start.9 = (f32[128,1024]{1,0:T(8,128)S(1)}, f32[128,1024]{1,0:T(8,128)S(1)}, u32[]{:S(2)}, u32[]{:S(2)}) collective-permute-start(f32[128,1024]{1,0:T(8,128)S(1)} %slice.66), channel_id=1, source_target_pairs={{0,12},{1,33},{2,14},{3,35},{16,28},{17,49},{18,30},{19,51},{4,8},... | collective-permute-start | bytes 1572872 | tf_op jit(solution)/shard_map/ppermute | solution.py:42
  35.5 19.6 %collective-permute-start.11 = (f32[320,1024]{1,0:T(8,128)S(1)}, f32[320,1024]{1,0:T(8,128)S(1)}, u32[]{:S(2)}, u32[]{:S(2)}) collective-permute-start(f32[320,1024]{1,0:T(8,128)S(1)} %collective-permute-done.5.refs_3_.refs_4_), channel_id=1, source_target_pairs={{0,18},{1,3},{2,16},{3,1},{16,2},{17,19},{18,0},{19,17},{4,22},{5,... | collective-permute-start | bytes 3932168 | tf_op jit(solution)/shard_map/ppermute | solution.py:42
  43.3 6.9 %collective-permute-start.12 = (f32[160,1024]{1,0:T(8,128)S(1)}, f32[160,1024]{1,0:T(8,128)S(1)}, u32[]{:S(2)}, u32[]{:S(2)}) collective-permute-start(f32[160,1024]{1,0:T(8,128)S(1)} %get-tuple-element.112), channel_id=1, source_target_pairs={{0,1},{1,0},{2,3},{3,2},{4,5},{5,4},{6,7},{7,6},{8,9},{9,8},{10,11... | collective-permute-start | bytes 1966088 | tf_op jit(solution)/shard_map/ppermute | solution.py:46
  43.4 6.8 %collective-permute-start.13 = (f32[160,1024]{1,0:T(8,128)S(1)}, f32[160,1024]{1,0:T(8,128)S(1)}, u32[]{:S(2)}, u32[]{:S(2)}) collective-permute-start(f32[160,1024]{1,0:T(8,128)S(1)} %get-tuple-element.111), channel_id=1, source_target_pairs={{0,1},{1,0},{2,3},{3,2},{4,5},{5,4},{6,7},{7,6},{8,9},{9,8},{10,11... | collective-permute-start | bytes 1966088 | tf_op jit(solution)/shard_map/ppermute | solution.py:46
  55.2 3.0 %collective-permute-start.14 = (f32[320,1024]{1,0:T(8,128)S(1)}, f32[320,1024]{1,0:T(8,128)S(1)}, u32[]{:S(2)}, u32[]{:S(2)}) collective-permute-start(f32[320,1024]{1,0:T(8,128)S(1)} %collective-permute-done.11.refs_4_.refs_3_), channel_id=1, source_target_pairs={{0,1},{1,0},{2,3},{3,2},{4,5},{5,4},{6,7},{7,6},{8,9},{9,8},{10,11... | collective-permute-start | bytes 3932168 | tf_op jit(solution)/shard_map/ppermute | solution.py:46
  59.1 10.5 %collective-permute-start.15 = (f32[128,1024]{1,0:T(8,128)S(1)}, f32[128,1024]{1,0:T(8,128)S(1)}, u32[]{:S(2)}, u32[]{:S(2)}) collective-permute-start(f32[128,1024]{1,0:T(8,128)S(1)} %get-tuple-element.95), channel_id=1, source_target_pairs={{0,12},{1,33},{2,14},{3,35},{16,28},{17,49},{18,30},{19,51},{4,8},... | collective-permute-start | bytes 1572872 | tf_op jit(solution)/shard_map/ppermute | solution.py:42
  61.6 9.2 %collective-permute-start.16 = (f32[128,1024]{1,0:T(8,128)S(1)}, f32[128,1024]{1,0:T(8,128)S(1)}, u32[]{:S(2)}, u32[]{:S(2)}) collective-permute-start(f32[128,1024]{1,0:T(8,128)S(1)} %get-tuple-element.96), channel_id=1, source_target_pairs={{0,4},{1,97},{2,6},{3,99},{16,20},{17,113},{18,22},{19,115},{4,0},... | collective-permute-start | bytes 1572872 | tf_op jit(solution)/shard_map/ppermute | solution.py:42
  63.4 12.1 %collective-permute-start.17 = (f32[136,1024]{1,0:T(8,128)S(1)}, f32[136,1024]{1,0:T(8,128)S(1)}, u32[]{:S(2)}, u32[]{:S(2)}) collective-permute-start(f32[136,1024]{1,0:T(8,128)S(1)} %slice.52), channel_id=1, source_target_pairs={{0,12},{1,33},{2,14},{3,35},{16,28},{17,49},{18,30},{19,51},{4,8},... | collective-permute-start | bytes 1671176 | tf_op jit(solution)/shard_map/ppermute | solution.py:42
  65.1 11.7 %collective-permute-start.18 = (f32[136,1024]{1,0:T(8,128)S(1)}, f32[136,1024]{1,0:T(8,128)S(1)}, u32[]{:S(2)}, u32[]{:S(2)}) collective-permute-start(f32[136,1024]{1,0:T(8,128)S(1)} %slice.54), channel_id=1, source_target_pairs={{0,4},{1,97},{2,6},{3,99},{16,20},{17,113},{18,22},{19,115},{4,0},... | collective-permute-start | bytes 1671176 | tf_op jit(solution)/shard_map/ppermute | solution.py:42
  70.9 10.5 %collective-permute-start.20 = (f32[128,1024]{1,0:T(8,128)S(1)}, f32[128,1024]{1,0:T(8,128)S(1)}, u32[]{:S(2)}, u32[]{:S(2)}) collective-permute-start(f32[128,1024]{1,0:T(8,128)S(1)} %slice_add_fusion.2), channel_id=1, source_target_pairs={{0,12},{1,33},{2,14},{3,35},{16,28},{17,49},{18,30},{19,51},{4,8},... | collective-permute-start | bytes 1572872 | tf_op jit(solution)/shard_map/ppermute | solution.py:42
  72.2 10.2 %collective-permute-start.19 = (f32[128,1024]{1,0:T(8,128)S(1)}, f32[128,1024]{1,0:T(8,128)S(1)}, u32[]{:S(2)}, u32[]{:S(2)}) collective-permute-start(f32[128,1024]{1,0:T(8,128)S(1)} %slice_add_fusion.3), channel_id=1, source_target_pairs={{0,4},{1,97},{2,6},{3,99},{16,20},{17,113},{18,22},{19,115},{4,0},... | collective-permute-start | bytes 1572872 | tf_op jit(solution)/shard_map/ppermute | solution.py:42
  82.6 8.0 %collective-permute-start.22 = (f32[64,1024]{1,0:T(8,128)S(1)}, f32[64,1024]{1,0:T(8,128)S(1)}, u32[]{:S(2)}, u32[]{:S(2)}) collective-permute-start(f32[64,1024]{1,0:T(8,128)S(1)} %get-tuple-element.116), channel_id=1, source_target_pairs={{0,64},{1,9},{2,66},{3,11},{16,80},{17,25},{18,82},{19,27},{4,68},... | collective-permute-start | bytes 786440 | tf_op jit(solution)/shard_map/ppermute | solution.py:42
  85.7 7.6 %collective-permute-start.23 = (f32[64,1024]{1,0:T(8,128)S(1)}, f32[64,1024]{1,0:T(8,128)S(1)}, u32[]{:S(2)}, u32[]{:S(2)}) collective-permute-start(f32[64,1024]{1,0:T(8,128)S(1)} %get-tuple-element.115), channel_id=1, source_target_pairs={{0,96},{1,5},{2,98},{3,7},{16,112},{17,21},{18,114},{19,23},{4,100... | collective-permute-start | bytes 786440 | tf_op jit(solution)/shard_map/ppermute | solution.py:42
  86.9 6.6 %collective-permute-start.21 = (f32[64,1024]{1,0:T(8,128)S(1)}, f32[64,1024]{1,0:T(8,128)S(1)}, u32[]{:S(2)}, u32[]{:S(2)}) collective-permute-start(f32[64,1024]{1,0:T(8,128)S(1)} %slice.71), channel_id=1, source_target_pairs={{0,32},{1,13},{2,34},{3,15},{16,48},{17,29},{18,50},{19,31},{4,36}... | collective-permute-start | bytes 786440 | tf_op jit(solution)/shard_map/ppermute | solution.py:42

commit v6 on v5

--- a/solution.py
+++ b/solution.py
@@ -187,6 +187,7 @@
     n = generated.shape[0]
     scale = total_real // total_gen
 
+    first = generated
     generated = resident(generated)
     real = real_bank.at[subset_rows].get(mode="promise_in_bounds", wrap_negative_indices=False)
     own = jnp.concatenate([generated, real], axis=0)
@@ -197,7 +198,7 @@
     x_far = move(own, "zz", "far")
     x_both = move(x_near, "zz", "far")
 
-    line = [generated] + [move(generated, "xy", step) for step in ("near", "far", "both")]
+    line = [generated] + [move(first, "xy", step) for step in ("near", "far", "both")]
     line = jnp.concatenate(line, axis=0)
     half = 2 * n
     line_near, line_far = move(line, "yx", "near"), move(line, "yx", "far")

time: 94.4 us -> 96 us (1.017)
  starting transfers between devices: 31.8 us -> 37.1 us
  waiting for transfers between devices: 34 us -> 30.3 us
    ppermute x19, starting transfers between devices: 31.2 us -> 36.5 us  [move(): return lax.ppermute(v, AXES, STEPS[axes, step])]
    ppermute x19, waiting for transfers between devices: 33.5 us -> 29.7 us  [move(): return lax.ppermute(v, AXES, STEPS[axes, step])]
  transfers between devices with their start and end apart: 24 -> 24, of which waited for: 14 -> 10; matrix products, arithmetic and copies ran while one was open for 4% -> 4% of each run, Pallas kernels for 22% -> 23%
where the time goes in v6:
time: 96 us; the launch traced here: 95.7 us
  starting transfers between devices  37.1 us (39%)
  waiting for transfers between devices  30.3 us (32%)
  Pallas kernels  23.2 us (24%)
  other arithmetic  3.2 us (3%)
  local copies, waits for them, and re-layouts  1.63 us (2%)
    ppermute x19, starting transfers between devices, move(): return lax.ppermute(v, AXES, STEPS[axes, step])  36.5 us
    ppermute x19, waiting for transfers between devices, move(): return lax.ppermute(v, AXES, STEPS[axes, step])  29.7 us
    pallas_call x8, Pallas kernels, pairs(): pl.pallas_call(functools.partial(pair_kernel, [len(batch) for batch in ro...  21.5 us
  transfers between devices with their start and end apart: 24, of which 10 were waited for; matrix products, arithmetic and copies ran while one was open for 4% of the time, Pallas kernels for 23%

profile of v6, /device:TPU:0, one launch (start us, length us, event | category | flops | bytes accessed | tf_op | source)
XLA Modules:
  0.0 95.7 jit_solution(14749783543828667254)
XLA Ops:
  0.0 1.6 %collective-permute-start = (f32[64,1024]{1,0:T(8,128)}, f32[64,1024]{1,0:T(8,128)}, u32[]{:S(2)}, u32[]{:S(2)}) collective-permute-start(f32[64,1024]{1,0:T(8,128)} %v_ref.1), channel_id=1, source_target_pairs={{0,32},{1,13},{2,34},{3,15},{16,48},{17,29},{18,50},{19,31},{4,36}... | collective-permute-start | bytes 786440 | tf_op jit(solution)/shard_map/ppermute | solution.py:42
  1.6 2.1 %collective-permute-start.1 = (f32[64,1024]{1,0:T(8,128)}, f32[64,1024]{1,0:T(8,128)}, u32[]{:S(2)}, u32[]{:S(2)}) collective-permute-start(f32[64,1024]{1,0:T(8,128)} %v_ref.1), channel_id=1, source_target_pairs={{0,96},{1,5},{2,98},{3,7},{16,112},{17,21},{18,114},{19,23},{4,100... | collective-permute-start | bytes 786440 | tf_op jit(solution)/shard_map/ppermute | solution.py:42
  3.7 0.6 collective-permute-start.2
  4.3 1.7 %shard_map.37 = f32[64,1024]{1,0:T(8,128)} custom-call(f32[64,1024]{1,0:T(8,128)} %v_ref.1), custom_call_target="tpu_custom_call" | custom-call | tf_op jit(solution)/shard_map/pallas_call | solution.py:176
  6.0 0.7 pad_clamp_fusion
  6.7 1.1 %gather_fusion = f32[256,1024]{1,0:T(8,128)S(1)} fusion(f32[512,1024]{1,0:T(8,128)S(1)} %copy-done, s32[1024]{0:T(1024)S(1)} %pad_clamp_fusion), kind=kCustom, calls=%fused_computation | custom fusion | bytes 2098176 | tf_op jit(solution)/shard_map/gather | solution.py:192
  7.8 0.1 pad_maximum_fusion.refs_3_.refs_2_
  7.9 2.0 %collective-permute-start.5 = (f32[320,1024]{1,0:T(8,128)S(1)}, f32[320,1024]{1,0:T(8,128)S(1)}, u32[]{:S(2)}, u32[]{:S(2)}) collective-permute-start(f32[320,1024]{1,0:T(8,128)S(1)} %pad_maximum_fusion.refs_3_.refs_2_), channel_id=1, source_target_pairs={{0,2},{1,19},{2,0},{3,17},{16,18},{17,3},{18,16},{19,1},{4,6},{5,2... | collective-permute-start | bytes 3932168 | tf_op jit(solution)/shard_map/ppermute | solution.py:42
  9.9 0.0 collective-permute-done
  9.9 2.4 %collective-permute-done.1 = f32[64,1024]{1,0:T(8,128)} collective-permute-done((f32[64,1024]{1,0:T(8,128)}, f32[64,1024]{1,0:T(8,128)}, u32[]{:S(2)}, u32[]{:S(2)}) %collective-permute-start.1) | collective-permute-done | bytes 262176 | tf_op jit(solution)/shard_map/ppermute | solution.py:42
  12.3 0.0 collective-permute-done.2
  12.3 1.2 %pad_maximum_fusion.1.refs_0_ = f32[256,1024]{1,0:T(8,128)S(1)} fusion(f32[64,1024]{1,0:T(8,128)} %collective-permute-done.2, f32[64,1024]{1,0:T(8,128)} %collective-permute-done.1, f32[64,1024]{1,0:T(8,128)} %collective-permute-done, f32[64,1024]{1,0:T(8,128)S(1)} %copy-done.1), kind=kLoop, calls=%fused_computation.2 | loop fusion | flops 786432 | bytes 2097152 | tf_op jit(solution)/shard_map/concatenate | solution.py:202
  13.5 1.7 %collective-permute-start.3 = (f32[256,1024]{1,0:T(8,128)S(1)}, f32[256,1024]{1,0:T(8,128)S(1)}, u32[]{:S(2)}, u32[]{:S(2)}) collective-permute-start(f32[256,1024]{1,0:T(8,128)S(1)} %pad_maximum_fusion.1.refs_0_), channel_id=1, source_target_pairs={{0,4},{1,97},{2,6},{3,99},{16,20},{17,113},{18,22},{19,115},{4,0},... | collective-permute-start | bytes 3145736 | tf_op jit(solution)/shard_map/ppermute | solution.py:42
  15.2 2.2 %collective-permute-start.4 = (f32[256,1024]{1,0:T(8,128)S(1)}, f32[256,1024]{1,0:T(8,128)S(1)}, u32[]{:S(2)}, u32[]{:S(2)}) collective-permute-start(f32[256,1024]{1,0:T(8,128)S(1)} %pad_maximum_fusion.1.refs_0_), channel_id=1, source_target_pairs={{0,12},{1,33},{2,14},{3,35},{16,28},{17,49},{18,30},{19,51},{4,8},... | collective-permute-start | bytes 3145736 | tf_op jit(solution)/shard_map/ppermute | solution.py:42
  17.3 0.0 collective-permute-start.8
  17.3 4.0 %collective-permute-start.6 = (f32[320,1024]{1,0:T(8,128)S(1)}, f32[320,1024]{1,0:T(8,128)S(1)}, u32[]{:S(2)}, u32[]{:S(2)}) collective-permute-start(f32[320,1024]{1,0:T(8,128)S(1)} %pad_maximum_fusion.refs_3_.refs_2_), channel_id=1, source_target_pairs={{0,18},{1,3},{2,16},{3,1},{16,2},{17,19},{18,0},{19,17},{4,22},{5,... | collective-permute-start | bytes 3932168 | tf_op jit(solution)/shard_map/ppermute | solution.py:42
  21.4 7.0 %collective-permute-done.3.refs_1_.refs_0_ = f32[256,1024]{1,0:T(8,128)S(1)} collective-permute-done((f32[256,1024]{1,0:T(8,128)S(1)}, f32[256,1024]{1,0:T(8,128)S(1)}, u32[]{:S(2)}, u32[]{:S(2)}) %collective-permute-start.3) | collective-permute-done | bytes 1048608 | tf_op jit(solution)/shard_map/ppermute | solution.py:42
  28.4 2.8 %collective-permute-done.4.refs_2_.refs_1_ = f32[256,1024]{1,0:T(8,128)S(1)} collective-permute-done((f32[256,1024]{1,0:T(8,128)S(1)}, f32[256,1024]{1,0:T(8,128)S(1)}, u32[]{:S(2)}, u32[]{:S(2)}) %collective-permute-start.4) | collective-permute-done | bytes 1048608 | tf_op jit(solution)/shard_map/ppermute | solution.py:42
  31.2 0.0 collective-permute-done.5.refs_3_.refs_4_
  31.2 0.0 collective-permute-start.7
  31.2 1.8 %collective-permute-start.10 = (f32[128,1024]{1,0:T(8,128)S(1)}, f32[128,1024]{1,0:T(8,128)S(1)}, u32[]{:S(2)}, u32[]{:S(2)}) collective-permute-start(f32[128,1024]{1,0:T(8,128)S(1)} %slice.67), channel_id=1, source_target_pairs={{0,4},{1,97},{2,6},{3,99},{16,20},{17,113},{18,22},{19,115},{4,0},... | collective-permute-start | bytes 1572872 | tf_op jit(solution)/shard_map/ppermute | solution.py:42
  33.1 3.8 %collective-permute-start.9 = (f32[128,1024]{1,0:T(8,128)S(1)}, f32[128,1024]{1,0:T(8,128)S(1)}, u32[]{:S(2)}, u32[]{:S(2)}) collective-permute-start(f32[128,1024]{1,0:T(8,128)S(1)} %slice.66), channel_id=1, source_target_pairs={{0,12},{1,33},{2,14},{3,35},{16,28},{17,49},{18,30},{19,51},{4,8},... | collective-permute-start | bytes 1572872 | tf_op jit(solution)/shard_map/ppermute | solution.py:42
  36.9 0.0 collective-permute-done.8.refs_4_.refs_3_
  37.0 4.2 %collective-permute-start.11 = (f32[320,1024]{1,0:T(8,128)S(1)}, f32[320,1024]{1,0:T(8,128)S(1)}, u32[]{:S(2)}, u32[]{:S(2)}) collective-permute-start(f32[320,1024]{1,0:T(8,128)S(1)} %collective-permute-done.5.refs_3_.refs_4_), channel_id=1, source_target_pairs={{0,18},{1,3},{2,16},{3,1},{16,2},{17,19},{18,0},{19,17},{4,22},{5,... | collective-permute-start | bytes 3932168 | tf_op jit(solution)/shard_map/ppermute | solution.py:42
  41.2 3.5 %shard_map.38 = (f32[256,1024]{1,0:T(8,128)S(1)}, f32[256,128]{1,0:T(8,128)S(1)}, f32[256,1024]{1,0:T(8,128)S(1)}, f32[256,128]{1,0:T(8,128)S(1)}, f32[256,1024]{1,0:T(8,128)S(1)}, /*index=5*/f32[256,128]{1,0:T(8,128)S(1)}) custom-call(f32[256,1024]{1,0:T(8,128)S(1)} %pad_maximum_fusion.1.refs_0_, f32[256,1024]{1,0:T(8,128)S(1)} %collective-permute-done.3.refs_1_.refs_0_, ...), custom_call_target="tpu_custom_call" | custom-call | flops 2415919104 | bytes 5767168 | tf_op jit(solution)/shard_map/pallas_call | solution.py:143
  44.7 0.0 collective-permute-done.7.refs_4_.refs_5_
  44.7 0.1 fusion.1
  44.9 0.1 collective-permute-start.12
  45.0 0.5 collective-permute-start.13
  45.5 4.1 %shard_map.39 = (f32[256,1024]{1,0:T(8,128)S(1)}, f32[256,128]{1,0:T(8,128)S(1)}, f32[256,1024]{1,0:T(8,128)S(1)}, f32[256,128]{1,0:T(8,128)S(1)}, f32[256,1024]{1,0:T(8,128)S(1)}, /*index=5*/f32[256,128]{1,0:T(8,128)S(1)}) custom-call(f32[256,1024]{1,0:T(8,128)S(1)} %pad_maximum_fusion.1.re, ...), custom_call_target="tpu_custom_call", output_to_operand_aliasing={{0}: (5, {}), {1}: (6, {}), {2}: (7, {}), {3}: (8, {}), {4}... | custom-call | flops 2415919104 | bytes 5767168 | tf_op jit(solution)/shard_map/pallas_call | solution.py:143
  49.5 0.0 collective-permute-done.10.refs_1_.refs_3_
  49.6 2.2 %shard_map.40 = (f32[256,1024]{1,0:T(8,128)S(1)}, f32[256,128]{1,0:T(8,128)S(1)}) custom-call(f32[128,1024]{1,0:T(8,128)S(1)} %collective-permute-done.9.refs_0_.refs_2_, f32[128,1024]{1,0:T(8,128)S(1)} %collective-permute-done.10.refs_1_.refs_3_, f32[320,1024]{1,0:T(8,128)S(1)} %pad_maximum_fusion.refs_3_.refs_2_, ...), custom_call_target="tpu_custom_call" | custom-call | flops 1610612736 | bytes 8388608 | tf_op jit(solution)/shard_map/pallas_call | solution.py:143
  51.7 0.0 collective-permute-done.12
  51.8 0.1 constant_dynamic-update-slice_fusion.1
  51.8 0.1 constant_dynamic-update-slice_fusion.refs_5_.refs_2_
  51.9 4.1 %shard_map.41 = (f32[256,1024]{1,0:T(8,128)S(1)}, f32[256,128]{1,0:T(8,128)S(1)}, f32[256,1024]{1,0:T(8,128)S(1)}, f32[256,128]{1,0:T(8,128)S(1)}, f32[256,1024]{1,0:T(8,128)S(1)}, /*index=5*/f32[256,128]{1,0:T(8,128)S(1)}) custom-call(f32[256,1024]{1,0:T(8,128)S(1)} %collective-permute-done, ...), custom_call_target="tpu_custom_call", output_to_operand_aliasing={{0}: (6, {}), {1}: (7, {}), {2}: (8, {}), {3}: (9, {}), {4}... | custom-call | flops 2415919104 | bytes 5767168 | tf_op jit(solution)/shard_map/pallas_call | solution.py:143
  56.0 0.8 collective-permute-done.11.refs_4_.refs_3_
  56.7 0.0 collective-permute-start.14
  56.7 2.5 %shard_map.42 = (f32[256,1024]{1,0:T(8,128)S(1)}, f32[256,128]{1,0:T(8,128)S(1)}, f32[256,1024]{1,0:T(8,128)S(1)}, f32[256,128]{1,0:T(8,128)S(1)}, f32[256,1024]{1,0:T(8,128)S(1)}, /*index=5*/f32[256,128]{1,0:T(8,128)S(1)}) custom-call(f32[256,1024]{1,0:T(8,128)S(1)} %collective-permute-done, ...), custom_call_target="tpu_custom_call", output_to_operand_aliasing={{0}: (5, {}), {1}: (6, {}), {2}: (7, {}), {3}: (8, {}), {4}... | custom-call | flops 1207959552 | bytes 4456448 | tf_op jit(solution)/shard_map/pallas_call | solution.py:143
  59.3 0.5 collective-permute-done.14.refs_2_.refs_4_
  59.8 0.9 shard_map.43
  60.7 0.8 collective-permute-start.15
  61.5 0.0 collective-permute-start.16
  61.5 1.7 %shard_map.45 = (f32[256,1024]{1,0:T(8,128)S(1)}, f32[256,1024]{1,0:T(8,128)S(1)}) custom-call(f32[256,1024]{1,0:T(8,128)S(1)} %collective-permute-done.3.refs_1_.refs_0_, f32[256,1024]{1,0:T(8,128)S(1)} %collective-permute-done.4.refs_2_.refs_1_, f32[320,1024]{1,0:T(8,128)S(1)} %collective-permute-done.14.refs_2_.refs_4_, ...), custom_call_target="tpu_custom_call" | custom-call | flops 805306368 | bytes 4456448 | tf_op jit(solution)/shard_map/pallas_call | solution.py:143
  63.3 2.6 %collective-permute-start.17 = (f32[136,1024]{1,0:T(8,128)S(1)}, f32[136,1024]{1,0:T(8,128)S(1)}, u32[]{:S(2)}, u32[]{:S(2)}) collective-permute-start(f32[136,1024]{1,0:T(8,128)S(1)} %slice.52), channel_id=1, source_target_pairs={{0,12},{1,33},{2,14},{3,35},{16,28},{17,49},{18,30},{19,51},{4,8},... | collective-permute-start | bytes 1671176 | tf_op jit(solution)/shard_map/ppermute | solution.py:42
  66.0 1.5 %collective-permute-start.18 = (f32[136,1024]{1,0:T(8,128)S(1)}, f32[136,1024]{1,0:T(8,128)S(1)}, u32[]{:S(2)}, u32[]{:S(2)}) collective-permute-start(f32[136,1024]{1,0:T(8,128)S(1)} %slice.54), channel_id=1, source_target_pairs={{0,4},{1,97},{2,6},{3,99},{16,20},{17,113},{18,22},{19,115},{4,0},... | collective-permute-start | bytes 1671176 | tf_op jit(solution)/shard_map/ppermute | solution.py:42
  67.5 2.5 %shard_map.44 = f32[256,1024]{1,0:T(8,128)S(1)} custom-call(f32[256,1024]{1,0:T(8,128)S(1)} %pad_maximum_fusion.1.refs_0_, f32[320,1024]{1,0:T(8,128)S(1)} %collective-permute-done.6.refs_4_.refs_1_, f32[320,1024]{1,0:T(8,128)S(1)} %constant_dynamic-update-slice_fusion.refs_5_.refs_2_, f32[320,1024]{1,0:T(8,128)S(1)} %collective-permute-done.11.refs_4_.refs_3_, ...), custom_call_target="tpu_custom_call" | custom-call | flops 1610612736 | bytes 8388608 | tf_op jit(solution)/shard_map/pallas_call | solution.py:143
  69.9 1.3 %collective-permute-done.15 = f32[128,1024]{1,0:T(8,128)S(1)} collective-permute-done((f32[128,1024]{1,0:T(8,128)S(1)}, f32[128,1024]{1,0:T(8,128)S(1)}, u32[]{:S(2)}, u32[]{:S(2)}) %collective-permute-start.15) | collective-permute-done | bytes 524320 | tf_op jit(solution)/shard_map/ppermute | solution.py:42
  71.2 0.0 collective-permute-done.16
  71.2 0.1 slice_add_fusion.2
  71.3 2.1 %collective-permute-start.20 = (f32[128,1024]{1,0:T(8,128)S(1)}, f32[128,1024]{1,0:T(8,128)S(1)}, u32[]{:S(2)}, u32[]{:S(2)}) collective-permute-start(f32[128,1024]{1,0:T(8,128)S(1)} %slice_add_fusion.2), channel_id=1, source_target_pairs={{0,12},{1,33},{2,14},{3,35},{16,28},{17,49},{18,30},{19,51},{4,8},... | collective-permute-start | bytes 1572872 | tf_op jit(solution)/shard_map/ppermute | solution.py:42
  73.4 0.1 slice_add_fusion.3
  73.4 0.1 collective-permute-start.19
  73.5 3.6 %collective-permute-done.17 = f32[136,1024]{1,0:T(8,128)S(1)} collective-permute-done((f32[136,1024]{1,0:T(8,128)S(1)}, f32[136,1024]{1,0:T(8,128)S(1)}, u32[]{:S(2)}, u32[]{:S(2)}) %collective-permute-start.17) | collective-permute-done | bytes 557088 | tf_op jit(solution)/shard_map/ppermute | solution.py:42
  77.3 0.2 maximum_add_fusion
  77.4 5.3 %collective-permute-done.20 = f32[128,1024]{1,0:T(8,128)S(1)} collective-permute-done((f32[128,1024]{1,0:T(8,128)S(1)}, f32[128,1024]{1,0:T(8,128)S(1)}, u32[]{:S(2)}, u32[]{:S(2)}) %collective-permute-start.20) | collective-permute-done | bytes 524320 | tf_op jit(solution)/shard_map/ppermute | solution.py:42
  82.8 0.2 slice_add_fusion
  83.0 4.3 %collective-permute-start.22 = (f32[64,1024]{1,0:T(8,128)S(1)}, f32[64,1024]{1,0:T(8,128)S(1)}, u32[]{:S(2)}, u32[]{:S(2)}) collective-permute-start(f32[64,1024]{1,0:T(8,128)S(1)} %get-tuple-element.116), channel_id=1, source_target_pairs={{0,64},{1,9},{2,66},{3,11},{16,80},{17,25},{18,82},{19,27},{4,68},... | collective-permute-start | bytes 786440 | tf_op jit(solution)/shard_map/ppermute | solution.py:42
  87.3 1.0 collective-permute-start.23
  88.3 0.1 collective-permute-start.21
  88.4 3.3 %collective-permute-done.22 = f32[64,1024]{1,0:T(8,128)S(1)} collective-permute-done((f32[64,1024]{1,0:T(8,128)S(1)}, f32[64,1024]{1,0:T(8,128)S(1)}, u32[]{:S(2)}, u32[]{:S(2)}) %collective-permute-start.22) | collective-permute-done | bytes 262176 | tf_op jit(solution)/shard_map/ppermute | solution.py:42
  91.7 3.2 %collective-permute-done.23 = f32[64,1024]{1,0:T(8,128)S(1)} collective-permute-done((f32[64,1024]{1,0:T(8,128)S(1)}, f32[64,1024]{1,0:T(8,128)S(1)}, u32[]{:S(2)}, u32[]{:S(2)}) %collective-permute-start.23) | collective-permute-done | bytes 262176 | tf_op jit(solution)/shard_map/ppermute | solution.py:42
  94.9 0.0 collective-permute-done.21
  94.9 0.8 fusion
  (17 shorter events, 0.3 us)
Async XLA Ops:
  0.0 6.7 %copy-start = (f32[512,1024]{1,0:T(8,128)S(1)}, f32[512,1024]{1,0:T(8,128)}, u32[]{:S(2)}) copy-start(f32[512,1024]{1,0:T(8,128)} %param.4) | copy-start | bytes 6291460
  0.0 9.9 %collective-permute-start = (f32[64,1024]{1,0:T(8,128)}, f32[64,1024]{1,0:T(8,128)}, u32[]{:S(2)}, u32[]{:S(2)}) collective-permute-start(f32[64,1024]{1,0:T(8,128)} %v_ref.1), channel_id=1, source_target_pairs={{0,32},{1,13},{2,34},{3,15},{16,48},{17,29},{18,50},{19,31},{4,36}... | collective-permute-start | bytes 786440 | tf_op jit(solution)/shard_map/ppermute | solution.py:42
  1.6 10.7 %collective-permute-start.1 = (f32[64,1024]{1,0:T(8,128)}, f32[64,1024]{1,0:T(8,128)}, u32[]{:S(2)}, u32[]{:S(2)}) collective-permute-start(f32[64,1024]{1,0:T(8,128)} %v_ref.1), channel_id=1, source_target_pairs={{0,96},{1,5},{2,98},{3,7},{16,112},{17,21},{18,114},{19,23},{4,100... | collective-permute-start | bytes 786440 | tf_op jit(solution)/shard_map/ppermute | solution.py:42
  3.7 8.6 %collective-permute-start.2 = (f32[64,1024]{1,0:T(8,128)}, f32[64,1024]{1,0:T(8,128)}, u32[]{:S(2)}, u32[]{:S(2)}) collective-permute-start(f32[64,1024]{1,0:T(8,128)} %v_ref.1), channel_id=1, source_target_pairs={{0,64},{1,9},{2,66},{3,11},{16,80},{17,25},{18,82},{19,27},{4,68},... | collective-permute-start | bytes 786440 | tf_op jit(solution)/shard_map/ppermute | solution.py:42
  6.7 1.1 %copy-start.1 = (f32[64,1024]{1,0:T(8,128)S(1)}, f32[64,1024]{1,0:T(8,128)}, u32[]{:S(2)}) copy-start(f32[64,1024]{1,0:T(8,128)} %shard_map.37) | copy-start | bytes 786436
  7.9 23.3 %collective-permute-start.5 = (f32[320,1024]{1,0:T(8,128)S(1)}, f32[320,1024]{1,0:T(8,128)S(1)}, u32[]{:S(2)}, u32[]{:S(2)}) collective-permute-start(f32[320,1024]{1,0:T(8,128)S(1)} %pad_maximum_fusion.refs_3_.refs_2_), channel_id=1, source_target_pairs={{0,2},{1,19},{2,0},{3,17},{16,18},{17,3},{18,16},{19,1},{4,6},{5,2... | collective-permute-start | bytes 3932168 | tf_op jit(solution)/shard_map/ppermute | solution.py:42
  13.5 14.9 %collective-permute-start.3 = (f32[256,1024]{1,0:T(8,128)S(1)}, f32[256,1024]{1,0:T(8,128)S(1)}, u32[]{:S(2)}, u32[]{:S(2)}) collective-permute-start(f32[256,1024]{1,0:T(8,128)S(1)} %pad_maximum_fusion.1.refs_0_), channel_id=1, source_target_pairs={{0,4},{1,97},{2,6},{3,99},{16,20},{17,113},{18,22},{19,115},{4,0},... | collective-permute-start | bytes 3145736 | tf_op jit(solution)/shard_map/ppermute | solution.py:42
  15.2 16.0 %collective-permute-start.4 = (f32[256,1024]{1,0:T(8,128)S(1)}, f32[256,1024]{1,0:T(8,128)S(1)}, u32[]{:S(2)}, u32[]{:S(2)}) collective-permute-start(f32[256,1024]{1,0:T(8,128)S(1)} %pad_maximum_fusion.1.refs_0_), channel_id=1, source_target_pairs={{0,12},{1,33},{2,14},{3,35},{16,28},{17,49},{18,30},{19,51},{4,8},... | collective-permute-start | bytes 3145736 | tf_op jit(solution)/shard_map/ppermute | solution.py:42
  17.3 19.6 %collective-permute-start.8 = (f32[320,1024]{1,0:T(8,128)S(1)}, f32[320,1024]{1,0:T(8,128)S(1)}, u32[]{:S(2)}, u32[]{:S(2)}) collective-permute-start(f32[320,1024]{1,0:T(8,128)S(1)} %pad_maximum_fusion.refs_3_.refs_2_), channel_id=1, source_target_pairs={{0,1},{1,0},{2,3},{3,2},{4,5},{5,4},{6,7},{7,6},{8,9},{9,8},{10,11... | collective-permute-start | bytes 3932168 | tf_op jit(solution)/shard_map/ppermute | solution.py:46
  17.3 27.4 %collective-permute-start.6 = (f32[320,1024]{1,0:T(8,128)S(1)}, f32[320,1024]{1,0:T(8,128)S(1)}, u32[]{:S(2)}, u32[]{:S(2)}) collective-permute-start(f32[320,1024]{1,0:T(8,128)S(1)} %pad_maximum_fusion.refs_3_.refs_2_), channel_id=1, source_target_pairs={{0,18},{1,3},{2,16},{3,1},{16,2},{17,19},{18,0},{19,17},{4,22},{5,... | collective-permute-start | bytes 3932168 | tf_op jit(solution)/shard_map/ppermute | solution.py:42
  31.2 13.6 %collective-permute-start.7 = (f32[320,1024]{1,0:T(8,128)S(1)}, f32[320,1024]{1,0:T(8,128)S(1)}, u32[]{:S(2)}, u32[]{:S(2)}) collective-permute-start(f32[320,1024]{1,0:T(8,128)S(1)} %collective-permute-done.5.refs_3_.refs_4_), channel_id=1, source_target_pairs={{0,1},{1,0},{2,3},{3,2},{4,5},{5,4},{6,7},{7,6},{8,9},{9,8},{10,11... | collective-permute-start | bytes 3932168 | tf_op jit(solution)/shard_map/ppermute | solution.py:46
  31.2 18.3 %collective-permute-start.10 = (f32[128,1024]{1,0:T(8,128)S(1)}, f32[128,1024]{1,0:T(8,128)S(1)}, u32[]{:S(2)}, u32[]{:S(2)}) collective-permute-start(f32[128,1024]{1,0:T(8,128)S(1)} %slice.67), channel_id=1, source_target_pairs={{0,4},{1,97},{2,6},{3,99},{16,20},{17,113},{18,22},{19,115},{4,0},... | collective-permute-start | bytes 1572872 | tf_op jit(solution)/shard_map/ppermute | solution.py:42
  33.1 16.4 %collective-permute-start.9 = (f32[128,1024]{1,0:T(8,128)S(1)}, f32[128,1024]{1,0:T(8,128)S(1)}, u32[]{:S(2)}, u32[]{:S(2)}) collective-permute-start(f32[128,1024]{1,0:T(8,128)S(1)} %slice.66), channel_id=1, source_target_pairs={{0,12},{1,33},{2,14},{3,35},{16,28},{17,49},{18,30},{19,51},{4,8},... | collective-permute-start | bytes 1572872 | tf_op jit(solution)/shard_map/ppermute | solution.py:42
  37.0 19.8 %collective-permute-start.11 = (f32[320,1024]{1,0:T(8,128)S(1)}, f32[320,1024]{1,0:T(8,128)S(1)}, u32[]{:S(2)}, u32[]{:S(2)}) collective-permute-start(f32[320,1024]{1,0:T(8,128)S(1)} %collective-permute-done.5.refs_3_.refs_4_), channel_id=1, source_target_pairs={{0,18},{1,3},{2,16},{3,1},{16,2},{17,19},{18,0},{19,17},{4,22},{5,... | collective-permute-start | bytes 3932168 | tf_op jit(solution)/shard_map/ppermute | solution.py:42
  44.9 6.9 %collective-permute-start.12 = (f32[160,1024]{1,0:T(8,128)S(1)}, f32[160,1024]{1,0:T(8,128)S(1)}, u32[]{:S(2)}, u32[]{:S(2)}) collective-permute-start(f32[160,1024]{1,0:T(8,128)S(1)} %get-tuple-element.112), channel_id=1, source_target_pairs={{0,1},{1,0},{2,3},{3,2},{4,5},{5,4},{6,7},{7,6},{8,9},{9,8},{10,11... | collective-permute-start | bytes 1966088 | tf_op jit(solution)/shard_map/ppermute | solution.py:46
  45.0 6.8 %collective-permute-start.13 = (f32[160,1024]{1,0:T(8,128)S(1)}, f32[160,1024]{1,0:T(8,128)S(1)}, u32[]{:S(2)}, u32[]{:S(2)}) collective-permute-start(f32[160,1024]{1,0:T(8,128)S(1)} %get-tuple-element.111), channel_id=1, source_target_pairs={{0,1},{1,0},{2,3},{3,2},{4,5},{5,4},{6,7},{7,6},{8,9},{9,8},{10,11... | collective-permute-start | bytes 1966088 | tf_op jit(solution)/shard_map/ppermute | solution.py:46
  56.7 3.0 %collective-permute-start.14 = (f32[320,1024]{1,0:T(8,128)S(1)}, f32[320,1024]{1,0:T(8,128)S(1)}, u32[]{:S(2)}, u32[]{:S(2)}) collective-permute-start(f32[320,1024]{1,0:T(8,128)S(1)} %collective-permute-done.11.refs_4_.refs_3_), channel_id=1, source_target_pairs={{0,1},{1,0},{2,3},{3,2},{4,5},{5,4},{6,7},{7,6},{8,9},{9,8},{10,11... | collective-permute-start | bytes 3932168 | tf_op jit(solution)/shard_map/ppermute | solution.py:46
  60.7 10.5 %collective-permute-start.15 = (f32[128,1024]{1,0:T(8,128)S(1)}, f32[128,1024]{1,0:T(8,128)S(1)}, u32[]{:S(2)}, u32[]{:S(2)}) collective-permute-start(f32[128,1024]{1,0:T(8,128)S(1)} %get-tuple-element.95), channel_id=1, source_target_pairs={{0,12},{1,33},{2,14},{3,35},{16,28},{17,49},{18,30},{19,51},{4,8},... | collective-permute-start | bytes 1572872 | tf_op jit(solution)/shard_map/ppermute | solution.py:42
  61.5 9.7 %collective-permute-start.16 = (f32[128,1024]{1,0:T(8,128)S(1)}, f32[128,1024]{1,0:T(8,128)S(1)}, u32[]{:S(2)}, u32[]{:S(2)}) collective-permute-start(f32[128,1024]{1,0:T(8,128)S(1)} %get-tuple-element.96), channel_id=1, source_target_pairs={{0,4},{1,97},{2,6},{3,99},{16,20},{17,113},{18,22},{19,115},{4,0},... | collective-permute-start | bytes 1572872 | tf_op jit(solution)/shard_map/ppermute | solution.py:42
  63.3 13.8 %collective-permute-start.17 = (f32[136,1024]{1,0:T(8,128)S(1)}, f32[136,1024]{1,0:T(8,128)S(1)}, u32[]{:S(2)}, u32[]{:S(2)}) collective-permute-start(f32[136,1024]{1,0:T(8,128)S(1)} %slice.52), channel_id=1, source_target_pairs={{0,12},{1,33},{2,14},{3,35},{16,28},{17,49},{18,30},{19,51},{4,8},... | collective-permute-start | bytes 1671176 | tf_op jit(solution)/shard_map/ppermute | solution.py:42
  66.0 11.2 %collective-permute-start.18 = (f32[136,1024]{1,0:T(8,128)S(1)}, f32[136,1024]{1,0:T(8,128)S(1)}, u32[]{:S(2)}, u32[]{:S(2)}) collective-permute-start(f32[136,1024]{1,0:T(8,128)S(1)} %slice.54), channel_id=1, source_target_pairs={{0,4},{1,97},{2,6},{3,99},{16,20},{17,113},{18,22},{19,115},{4,0},... | collective-permute-start | bytes 1671176 | tf_op jit(solution)/shard_map/ppermute | solution.py:42
  71.3 11.5 %collective-permute-start.20 = (f32[128,1024]{1,0:T(8,128)S(1)}, f32[128,1024]{1,0:T(8,128)S(1)}, u32[]{:S(2)}, u32[]{:S(2)}) collective-permute-start(f32[128,1024]{1,0:T(8,128)S(1)} %slice_add_fusion.2), channel_id=1, source_target_pairs={{0,12},{1,33},{2,14},{3,35},{16,28},{17,49},{18,30},{19,51},{4,8},... | collective-permute-start | bytes 1572872 | tf_op jit(solution)/shard_map/ppermute | solution.py:42
  73.4 9.4 %collective-permute-start.19 = (f32[128,1024]{1,0:T(8,128)S(1)}, f32[128,1024]{1,0:T(8,128)S(1)}, u32[]{:S(2)}, u32[]{:S(2)}) collective-permute-start(f32[128,1024]{1,0:T(8,128)S(1)} %slice_add_fusion.3), channel_id=1, source_target_pairs={{0,4},{1,97},{2,6},{3,99},{16,20},{17,113},{18,22},{19,115},{4,0},... | collective-permute-start | bytes 1572872 | tf_op jit(solution)/shard_map/ppermute | solution.py:42
  83.0 8.7 %collective-permute-start.22 = (f32[64,1024]{1,0:T(8,128)S(1)}, f32[64,1024]{1,0:T(8,128)S(1)}, u32[]{:S(2)}, u32[]{:S(2)}) collective-permute-start(f32[64,1024]{1,0:T(8,128)S(1)} %get-tuple-element.116), channel_id=1, source_target_pairs={{0,64},{1,9},{2,66},{3,11},{16,80},{17,25},{18,82},{19,27},{4,68},... | collective-permute-start | bytes 786440 | tf_op jit(solution)/shard_map/ppermute | solution.py:42
  87.3 7.6 %collective-permute-start.23 = (f32[64,1024]{1,0:T(8,128)S(1)}, f32[64,1024]{1,0:T(8,128)S(1)}, u32[]{:S(2)}, u32[]{:S(2)}) collective-permute-start(f32[64,1024]{1,0:T(8,128)S(1)} %get-tuple-element.115), channel_id=1, source_target_pairs={{0,96},{1,5},{2,98},{3,7},{16,112},{17,21},{18,114},{19,23},{4,100... | collective-permute-start | bytes 786440 | tf_op jit(solution)/shard_map/ppermute | solution.py:42
  88.3 6.6 %collective-permute-start.21 = (f32[64,1024]{1,0:T(8,128)S(1)}, f32[64,1024]{1,0:T(8,128)S(1)}, u32[]{:S(2)}, u32[]{:S(2)}) collective-permute-start(f32[64,1024]{1,0:T(8,128)S(1)} %slice.71), channel_id=1, source_target_pairs={{0,32},{1,13},{2,34},{3,15},{16,48},{17,29},{18,50},{19,31},{4,36}... | collective-permute-start | bytes 786440 | tf_op jit(solution)/shard_map/ppermute | solution.py:42
